TPU v7x, 512 devices: a whole 4x4x16 slice. The times are simulated.
512 devices in a mesh: dp: 16 (over z), feat: 32 (over y, x, core).
Axes of the slice: x: 4, y: 4, z: 16, core: 2. Of those that a mesh axis runs over, the one named last changes fastest.
Arguments:
- features: bfloat16 [128, 65536], P('feat', 'dp'), may hold values from -6 to 6
- neighbours_one: int32 [65536, 15], P('dp'), may hold values from 0 to 4095
- counts_one: int32 [65536], P('dp'), may hold values from 1 to 15
- neighbours_two: int32 [65536, 10], P(('dp', 'feat')), may hold values from 0 to 4095, as said below
- counts_two: int32 [65536], P(('dp', 'feat')), may hold values from 1 to 10
- self_one: bfloat16 [128, 256], P('feat'), may hold values from -0.5 to 0.5
- neigh_one: bfloat16 [128, 256], P('feat'), may hold values from -1 to 1
- bias_one: float32 [256], replicated, may hold values from -3 to 3
- self_two: bfloat16 [256, 256], replicated, may hold values from -0.375 to 0.375
- neigh_two: bfloat16 [256, 256], replicated, may hold values from -0.5 to 0.5
- bias_two: float32 [256], replicated, may hold values from -3 to 3
- cotangent: bfloat16 [65536, 256], P(('dp', 'feat')), may hold values from -40 to 40
Outputs:
- hidden_two: bfloat16 [65536, 256], P(('dp', 'feat'))
- grad_self: float32 [256, 256], replicated
- grad_neigh: float32 [256, 256], replicated
- grad_bias: float32 [256], replicated
Inputs may be any that keep to these rules, and one draw needn't show every extreme that they name: `neighbours_two`: the neighbours of node number k of a mini-batch lie in its own block of 128 nodes (k // 128) or in the block just before or just after it.
All inputs are finite; a program needn't handle non-finite values.
Results may differ from a plain program's by a relative error of at most 0.0053.
Values may be sent and summed in bfloat16 or wider, within the bound.
No kernel may reach another device: no remote copies, remote signals or barrier semaphores. Data moves between devices by JAX's collectives and lax.ppermute only.
A program may use at most 64 MiB of HBM per device.

v0:
```python
import jax
import jax.numpy as jnp
from jax import lax
from jax.sharding import PartitionSpec as P


def with_halo(block, sides, width):
    for axis, dim in sides:
        count = lax.axis_size(axis)
        forward = [(i, i + 1) for i in range(count - 1)]
        backward = [(target, source) for source, target in forward]
        low = lax.ppermute(
            lax.slice_in_dim(block, block.shape[dim] - width, None, axis=dim), axis, forward
        )
        high = lax.ppermute(lax.slice_in_dim(block, 0, width, axis=dim), axis, backward)
        block = jnp.concatenate([low, block, high], axis=dim)
    return block


def local(
    features,
    neighbours_one,
    counts_one,
    neighbours_two,
    counts_two,
    self_one,
    neigh_one,
    bias_one,
    self_two,
    neigh_two,
    bias_two,
    cotangent,
):
    width = features.shape[0]
    batch_nodes = features.shape[1]
    groups = lax.axis_size("feat")
    node_rows = batch_nodes // groups
    first_fan = neighbours_one.shape[1]
    second_fan = neighbours_two.shape[1]
    picked = jnp.take(features, neighbours_one.reshape(-1), axis=1).reshape(
        width, batch_nodes, first_fan
    )
    live_one = (jnp.arange(first_fan, dtype=jnp.int32)[None, :] < counts_one[:, None]).astype(
        jnp.float32
    )
    summed = jnp.sum(picked.astype(jnp.float32) * live_one[None, :, :], axis=2)
    agg_one = (summed / counts_one[None, :].astype(jnp.float32)).astype(jnp.bfloat16)
    contract = (((0,), (0,)), ((), ()))
    term = lax.dot_general(features, self_one, contract, preferred_element_type=jnp.float32)
    pre_one = lax.psum_scatter(
        term + lax.dot_general(agg_one, neigh_one, contract, preferred_element_type=jnp.float32),
        "feat",
        scatter_dimension=0,
        tiled=True,
    )
    hidden_one = jax.nn.gelu(pre_one + bias_one, approximate=True).astype(jnp.bfloat16)
    padded = with_halo(hidden_one, (("feat", 0),), node_rows)
    first_node = lax.axis_index("feat") * node_rows
    local_ids = neighbours_two - first_node + node_rows
    rows_two = padded[local_ids.reshape(-1)].reshape(node_rows, second_fan, hidden_one.shape[1])
    live_two = (jnp.arange(second_fan, dtype=jnp.int32)[None, :] < counts_two[:, None]).astype(
        jnp.float32
    )
    summed_two = jnp.sum(rows_two.astype(jnp.float32) * live_two[:, :, None], axis=1)
    agg_two = (summed_two / counts_two[:, None].astype(jnp.float32)).astype(jnp.bfloat16)
    pre_two = jnp.dot(hidden_one, self_two, preferred_element_type=jnp.float32)
    pre_two = pre_two + jnp.dot(agg_two, neigh_two, preferred_element_type=jnp.float32) + bias_two
    hidden_two = jax.nn.gelu(pre_two, approximate=True).astype(jnp.bfloat16)
    slope_fn = jax.vjp(lambda value: jax.nn.gelu(value, approximate=True), pre_two)[1]
    delta = slope_fn(cotangent.astype(jnp.float32))[0].astype(jnp.bfloat16)
    local_self = jnp.dot(hidden_one.T, delta, preferred_element_type=jnp.float32)
    local_neigh = jnp.dot(agg_two.T, delta, preferred_element_type=jnp.float32)
    local_bias = jnp.sum(delta.astype(jnp.float32), axis=0)
    total_self, total_neigh, total_bias = lax.psum(
        (local_self, local_neigh, local_bias), ("dp", "feat")
    )
    scale = 1.0 / (node_rows * groups * lax.axis_size("dp"))
    return (hidden_two, total_self * scale, total_neigh * scale, total_bias * scale)


def solution(mesh):
    return jax.shard_map(
        local,
        mesh=mesh,
        in_specs=(
            P("feat", "dp"),
            P("dp", None),
            P("dp"),
            P(("dp", "feat"), None),
            P(("dp", "feat")),
            P("feat", None),
            P("feat", None),
            P(),
            P(),
            P(),
            P(),
            P(("dp", "feat"), None),
        ),
        out_specs=(P(("dp", "feat"), None), P(), P(), P()),
        check_vma=False,
    )
```

profile of v0, /device:TPU:1, one launch (start us, length us, event | category | flops | bytes accessed | tf_op | source)
XLA Modules:
  0.0 860.7 jit_solution(16249477336347824559)
XLA Ops:
  7.2 1.6 copy.19
  8.8 1.0 compare_and_fusion
  9.9 3.5 fusion
  13.4 1.8 reshape.132
  16.0 214.7 %gather_fusion = bf16[61440,4]{1,0:T(8,128)(2,1)} fusion(bf16[4,4096]{0,1:T(8,128)(2,1)S(1)} %copy.20, s32[61440]{0:T(1024)S(1)} %broadcast_clamp_fusion), kind=kCustom, calls=%fused_computation | custom fusion | bytes 1228800 | tf_op jit(solution)/shard_map/jit(_take)/gather | solution.py:40
  230.7 11.9 %copy.21 = bf16[4,61440]{1,0:T(4,128)(2,1)S(1)} copy(bf16[4,61440]{0,1:T(8,128)(2,1)} %bitcast.11) | data formatting | bytes 983040 | tf_op jit(solution)/shard_map/jit(_take)/gather | solution.py:40
  242.6 12.0 %gather.10 = bf16[4,4096,15]{2,1,0:T(8,128)(2,1)} reshape(bf16[4,61440]{1,0:T(4,128)(2,1)S(1)} %copy.21) | data formatting | bytes 983040 | tf_op jit(solution)/shard_map/jit(_take)/gather | solution.py:40
  254.6 0.8 copy.18
  255.5 0.8 fusion.25
  256.2 1.4 copy-done.1
  257.7 2.5 multiply_reduce_fusion
  260.2 2.7 convolution_add_fusion
  264.0 107.7 %reduce-scatter.2.cloned.1.call-done = f32[128,256]{1,0:T(8,128)} async-done(((f32[4096,256]{1,0:T(8,128)}), f32[128,256]{1,0:T(8,128)}) %reduce-scatter.2.cloned.1.call-update) | async-done | bytes 131088 | tf_op jit(solution)/shard_map/reduce_scatter | solution.py:50
  371.8 1.0 fusion.19
  372.7 5.0 collective-permute-start
  377.7 1.9 collective-permute-start.1
  379.8 3.5 collective-permute-done.1
  383.3 4.3 gather_fusion.1
  388.4 1.0 convert_reduce_fusion
  389.3 1.0 fusion.23
  390.3 0.9 fusion.27
  391.3 107.1 %psum.23 = f32[256]{0:T(256)S(1)} all-reduce(f32[256]{0:T(256)S(1)} %get-tuple-element.6), channel_id=1, replica_groups=mesh['dp'=16,'feat'=32] {'dp','feat'}, use_global_device_ids=true, to_apply=%region_6.7 | all-reduce | flops 256 | bytes 2048 | tf_op jit(solution)/shard_map/psum | solution.py:74
  498.9 353.1 %all-reduce.3.cloned.1.call-done = (f32[256,256]{1,0:T(8,128)}, f32[256,256]{1,0:T(8,128)}) async-done(((f32[256,256]{1,0:T(8,128)}, f32[256,256]{1,0:T(8,128)}), (f32[256,256]{1,0:T(8,128)}, f32[256,256]{1,0:T(8,128)})) %all-reduce.3.cloned.1.call-update) | async-done | bytes 524304 | tf_op jit(solution)/shard_map/psum | solution.py:74
  852.0 1.9 broadcast_multiply_fusion
  (46 shorter events, 3.4 us)
Async XLA Ops:
  7.2 381.2 %copy-start = (bf16[256,256]{1,0:T(8,128)(2,1)S(1)}, bf16[256,256]{1,0:T(8,128)(2,1)}, u32[]{:S(2)}) copy-start(bf16[256,256]{1,0:T(8,128)(2,1)} %param.21) | copy-start | bytes 393220
  7.2 6.2 copy-start.5
  7.2 8.3 copy-start.3
  7.2 364.5 %reduce-scatter.2.cloned.1.call-start = ((), (), s32[]{:S(2)}) async-start(), calls=%async_computation.1 | async-start | bytes 4325376 | tf_op jit(solution)/shard_map/reduce_scatter | solution.py:50
  242.6 12.8 %copy-start.7 = (bf16[4,256]{1,0:T(4,128)(2,1)S(1)}, bf16[4,256]{1,0:T(4,128)(2,1)}, u32[]{:S(2)}) copy-start(bf16[4,256]{1,0:T(4,128)(2,1)} %param.17) | copy-start | bytes 6148
  242.6 13.6 %copy-start.2 = (f32[4096,15]{1,0:T(8,128)S(1)}, f32[4096,15]{1,0:T(8,128)}, u32[]{:S(2)}) copy-start(f32[4096,15]{1,0:T(8,128)} %fusion) | copy-start | bytes 737284
  255.5 2.2 copy-start.1
  257.7 2.5 copy-start.8
  262.9 0.7 copy-start.6
  262.9 1.0 copy-start.10
  262.9 108.8 %copy-start.9 = (f32[256]{0:T(256)S(1)}, f32[256]{0:T(256)}, u32[]{:S(2)}) copy-start(f32[256]{0:T(256)} %param.19) | copy-start | bytes 3076
  262.9 116.7 %copy-start.4 = (bf16[256,256]{1,0:T(8,128)(2,1)S(1)}, bf16[256,256]{1,0:T(8,128)(2,1)}, u32[]{:S(2)}) copy-start(bf16[256,256]{1,0:T(8,128)(2,1)} %param.20) | copy-start | bytes 393220
  262.9 589.1 %all-reduce.3.cloned.1.call-start = ((), (), s32[]{:S(2)}) async-start(), calls=%async_computation.2 | async-start | bytes 1048576 | tf_op jit(solution)/shard_map/psum | solution.py:74
  372.7 7.1 collective-permute-start
  377.7 5.6 collective-permute-start.1
  383.3 5.1 copy-start.11
  383.3 5.1 copy-start.12
Sparse Core Ops, SparseCore 0:
  263.1 108.6 reduce-scatter.1
  391.4 460.5 all-reduce.2
where the time goes:
time: 862 us; the launch traced here: 861 us
  waiting for transfers between devices  464 us (54%)
  local copies, waits for them, and re-layouts  250 us (29%)
  blocking collectives  107 us (12%)
  between operations  14.3 us (2%)
  other arithmetic  11.4 us (1%)
    psum x1, waiting for transfers between devices, local(): lax.psum((local_self, local_neigh, local_bias), ('dp', 'feat'))  353 us
    gather x3, local copies, waits for them, and re-layouts, local(): jnp.take(features, neighbours_one.reshape(-1), axis=1)  239 us
    reduce_scatter x1, waiting for transfers between devices, local(): lax.psum_scatter(term + lax.dot_general(agg_one, neigh_one, contract, pre...  108 us
    psum x1, blocking collectives, local(): lax.psum((local_self, local_neigh, local_bias), ('dp', 'feat'))  107 us
  transfers between devices with their start and end apart: 4, of which 3 were waited for; matrix products, arithmetic and copies ran while one was open for 0% of the time, Pallas kernels for 0%

commit v1 on v0

v1 whole, which is shorter than its diff:
```python
import functools
import math

import jax
import jax.numpy as jnp
from jax import lax
from jax.experimental import pallas as pl
from jax.experimental.pallas import tpu as pltpu
from jax.sharding import Mesh
from jax.sharding import PartitionSpec as P

LANES = 128
INNER = math.sqrt(2.0 / math.pi)
CUBIC = 0.044715
VMEM_BYTES = 48 * 1024 * 1024


def pick_kernel(feats_ref, ids_ref, counts_ref, self_ref, neigh_ref, out_ref, table, sums):
    rows, nodes = feats_ref.shape
    fan = ids_ref.shape[0]
    blocks = nodes // LANES
    wide = feats_ref[...].astype(jnp.float32)
    table[0:rows, :] = wide
    table[rows : 2 * rows, :] = wide
    upper = lax.broadcasted_iota(jnp.int32, (2 * rows, LANES), 0) < rows

    def two_blocks(pair, carry):
        start = pl.multiple_of(pair * 2 * LANES, 2 * LANES)
        first, second = pl.ds(start, LANES), pl.ds(start + LANES, LANES)

        def both(ref, k):
            return jnp.where(
                upper,
                jnp.broadcast_to(ref[k : k + 1, first], upper.shape),
                jnp.broadcast_to(ref[k : k + 1, second], upper.shape),
            )

        counts = both(counts_ref, 0)
        total = jnp.zeros(upper.shape, jnp.float32)
        for k in range(fan):
            ids = both(ids_ref, k)
            lane = jnp.bitwise_and(ids, LANES - 1)
            block = lax.shift_right_logical(ids, 7)
            level = [
                jnp.take_along_axis(
                    table[:, j * LANES : (j + 1) * LANES], lane, axis=1, mode="promise_in_bounds"
                )
                for j in range(blocks)
            ]
            bit = 1
            while len(level) > 1:
                odd = jnp.bitwise_and(block, bit) != 0
                level = [
                    jnp.where(odd, level[i + 1], level[i]) for i in range(0, len(level), 2)
                ]
                bit *= 2
            total = total + jnp.where(counts > k, level[0], 0.0)
        mean = total / counts.astype(jnp.float32)
        at_first = pl.multiple_of(start + LANES, LANES)
        at_second = pl.multiple_of(start + 2 * LANES, LANES)
        sums[:, pl.ds(at_first, LANES)] = jnp.where(
            upper, table[:, first], pltpu.roll(mean, rows, axis=0)
        )
        sums[:, pl.ds(at_second, LANES)] = jnp.where(upper, table[:, second], mean)
        return carry

    lax.fori_loop(0, blocks // 2, two_blocks, 0)
    sums[:, 0:LANES] = sums[:, blocks * LANES : (blocks + 1) * LANES]
    sums[:, (blocks + 1) * LANES :] = sums[:, LANES : 2 * LANES]
    weights = jnp.concatenate(
        [self_ref[...].astype(jnp.float32), neigh_ref[...].astype(jnp.float32)], axis=0
    ).astype(jnp.bfloat16)
    for block in range(blocks):
        out_ref[block, :, 0 : 3 * LANES] = sums[
            :, block * LANES : (block + 3) * LANES
        ].astype(jnp.bfloat16)
        out_ref[block, :, 3 * LANES :] = weights


def gelu_parts(value):
    square = value * value
    bent = jnp.tanh(INNER * (value + CUBIC * (value * square)))
    half = 0.5 * (1.0 + bent)
    slope = half + 0.5 * value * (1.0 - bent * bent) * (INNER * (1.0 + 3.0 * CUBIC * square))
    return value * half, slope


def layers_kernel(
    got_ref, ids_ref, counts_ref, bias_one_ref, self_ref, neigh_ref, bias_two_ref, cot_ref,
    hidden_ref, grads_ref, bias_ref,
):
    node_rows = cot_ref.shape[0]
    hid = cot_ref.shape[1]
    span = 3 * node_rows
    fan = ids_ref.shape[1]
    over_rows = (((0,), (0,)), ((), ()))
    got = got_ref[...]
    pre_one = lax.dot_general(
        got[:, :span], got[:, span:], over_rows, preferred_element_type=jnp.float32
    )
    hidden = gelu_parts(pre_one + bias_one_ref[...])[0].astype(jnp.bfloat16)
    own = hidden[node_rows : 2 * node_rows]
    ids, counts = ids_ref[...], counts_ref[...]
    column = lax.broadcasted_iota(jnp.int32, (node_rows, span), 1)
    often = jnp.zeros((node_rows, span), jnp.float32)
    for k in range(fan):
        hit = jnp.where(counts > k, ids[:, k : k + 1], -1) == column
        often = often + jnp.where(hit, 1.0, 0.0)
    summed = jnp.dot(often.astype(jnp.bfloat16), hidden, preferred_element_type=jnp.float32)
    agg = (summed / counts.astype(jnp.float32)).astype(jnp.bfloat16)
    pre_two = jnp.dot(own, self_ref[...], preferred_element_type=jnp.float32)
    pre_two = pre_two + jnp.dot(agg, neigh_ref[...], preferred_element_type=jnp.float32)
    value, slope = gelu_parts(pre_two + bias_two_ref[...])
    hidden_ref[...] = value.astype(jnp.bfloat16)
    delta = (cot_ref[...].astype(jnp.float32) * slope).astype(jnp.bfloat16)
    grads_ref[0:hid, :] = lax.dot_general(
        own, delta, over_rows, preferred_element_type=jnp.float32
    )
    grads_ref[hid:, :] = lax.dot_general(
        agg, delta, over_rows, preferred_element_type=jnp.float32
    )
    bias_ref[...] = jnp.sum(delta.astype(jnp.float32), axis=0, keepdims=True)


def local(
    features,
    neighbours_one,
    counts_one,
    neighbours_two,
    counts_two,
    self_one,
    neigh_one,
    bias_one,
    self_two,
    neigh_two,
    bias_two,
    cotangent,
):
    rows, batch_nodes = features.shape
    groups = lax.axis_size("feat")
    node_rows = batch_nodes // groups
    hid = self_one.shape[1]
    span = 3 * node_rows
    params = pltpu.CompilerParams(vmem_limit_bytes=VMEM_BYTES)
    chunks = pl.pallas_call(
        pick_kernel,
        out_shape=jax.ShapeDtypeStruct((groups, 2 * rows, span + hid), jnp.bfloat16),
        scratch_shapes=[
            pltpu.VMEM((2 * rows, batch_nodes), jnp.float32),
            pltpu.VMEM((2 * rows, batch_nodes + 2 * node_rows), jnp.float32),
        ],
        compiler_params=params,
        name="pick",
    )(features, neighbours_one.T, counts_one[None, :], self_one, neigh_one)
    got = lax.all_to_all(chunks, "feat", 0, 0, tiled=True)
    first_node = lax.axis_index("feat") * node_rows
    hidden_two, grads, bias = pl.pallas_call(
        layers_kernel,
        out_shape=(
            jax.ShapeDtypeStruct((node_rows, hid), jnp.bfloat16),
            jax.ShapeDtypeStruct((2 * hid, hid), jnp.float32),
            jax.ShapeDtypeStruct((1, hid), jnp.float32),
        ),
        compiler_params=params,
        name="layers",
    )(
        got.reshape(groups * 2 * rows, span + hid),
        neighbours_two - first_node + node_rows,
        counts_two[:, None],
        bias_one[None, :],
        self_two,
        neigh_two,
        bias_two[None, :],
        cotangent,
    )
    group = lax.axis_size("pair") * groups
    others = lax.axis_size("apart")
    parts = jnp.concatenate(
        [grads.reshape(group, -1, 2, LANES), bias.reshape(1, 1, 2, LANES) * jnp.ones((group, 1, 1, 1), jnp.float32)], axis=1
    )
    inner = lax.all_to_all(parts, ("pair", "feat"), 0, 0, tiled=True).sum(axis=0)
    spread = jnp.broadcast_to(inner[None], (others,) + inner.shape)
    total = lax.all_to_all(spread, "apart", 0, 0, tiled=True).sum(axis=0)
    scale = 1.0 / (batch_nodes * lax.axis_size("pair") * others)
    total = total * scale
    total_bias = total[-1].reshape(hid)
    narrow = total[:-1].astype(jnp.bfloat16)
    spread = jnp.broadcast_to(narrow[None], (group,) + narrow.shape)
    whole = lax.all_to_all(spread, ("pair", "feat"), 0, 0, tiled=True)
    whole = whole.reshape(2 * hid, hid).astype(jnp.float32)
    return hidden_two, whole[:hid], whole[hid:], total_bias


def solution(mesh):
    replicas, groups = mesh.devices.shape
    split = Mesh(mesh.devices.reshape(replicas // 2, 2, groups), ("apart", "pair", "feat"))
    dp = ("apart", "pair")
    every = ("apart", "pair", "feat")
    return jax.shard_map(
        local,
        mesh=split,
        in_specs=(
            P("feat", dp),
            P(dp, None),
            P(dp),
            P(every, None),
            P(every),
            P("feat", None),
            P("feat", None),
            P(),
            P(),
            P(),
            P(),
            P(every, None),
        ),
        out_specs=(P(every, None), P(), P(), P()),
        check_vma=False,
    )
```

time: 862 us -> 99.6 us (0.12)
  waiting for transfers between devices: 464 us -> 18 us
  local copies, waits for them, and re-layouts: 250 us -> 7.63 us
  blocking collectives: 107 us -> 41.9 us
  between operations: 14.3 us -> 0.78 us
  Pallas kernels: 0 us -> 12.5 us
  other arithmetic: 11.4 us -> 0.55 us
  starting transfers between devices: 6.99 us -> 17.6 us
    psum x1 -> x0, waiting for transfers between devices: 353 us -> none  [local(): lax.psum((local_self, local_neigh, local_bias), ('dp', 'feat'))]
    gather x4 -> x0, local copies, waits for them, and re-layouts: 243 us -> none  [the longest x3 239 us: local(): jnp.take(features, neighbours_one.reshape(-1), axis=1)]
    reduce_scatter x1 -> x0, waiting for transfers between devices: 108 us -> none  [local(): lax.psum_scatter(term + lax.dot_general(agg_one, neigh_one, contract, pre...]
    psum x1 -> x0, blocking collectives: 107 us -> none  [local(): lax.psum((local_self, local_neigh, local_bias), ('dp', 'feat'))]
    all_to_all x0 -> x2, blocking collectives: none -> 41.9 us  [the longest x1 25.2 us: local(): total = lax.all_to_all(spread, 'apart', 0, 0, tiled=True).sum(axis=0)]
    all_to_all x0 -> x2, waiting for transfers between devices: none -> 18 us  [the longest x1 9.17 us: local(): whole = lax.all_to_all(spread, ('pair', 'feat'), 0, 0, tiled=True)]
    all_to_all x0 -> x2, starting transfers between devices: none -> 17.6 us  [the longest x1 10.5 us: local(): got = lax.all_to_all(chunks, 'feat', 0, 0, tiled=True)]
    pallas_call x0 -> x2, Pallas kernels: none -> 12.5 us  [the longest x1 10.9 us: local(): pl.pallas_call(pick_kernel, out_shape=jax.ShapeDtypeStruct((groups, 2 * r...]
  transfers between devices with their start and end apart: 4 -> 2, of which waited for: 3 -> 2; matrix products, arithmetic and copies ran while one was open for 0% -> 1% of each run, Pallas kernels for 0% -> 0%
where the time goes in v1:
time: 99.6 us; the launch traced here: 99 us
  blocking collectives  41.9 us (42%)
  waiting for transfers between devices  18 us (18%)
  starting transfers between devices  17.6 us (18%)
  Pallas kernels  12.5 us (13%)
  local copies, waits for them, and re-layouts  7.63 us (8%)
    all_to_all x1, blocking collectives, local(): total = lax.all_to_all(spread, 'apart', 0, 0, tiled=True).sum(axis=0)  25.2 us
    all_to_all x1, blocking collectives, local(): lax.all_to_all(parts, ('pair', 'feat'), 0, 0, tiled=True).sum(axis=0)  16.7 us
    pallas_call x1, Pallas kernels, local(): pl.pallas_call(pick_kernel, out_shape=jax.ShapeDtypeStruct((groups, 2 * r...  10.9 us
    all_to_all x1, starting transfers between devices, local(): got = lax.all_to_all(chunks, 'feat', 0, 0, tiled=True)  10.5 us
    all_to_all x1, waiting for transfers between devices, local(): whole = lax.all_to_all(spread, ('pair', 'feat'), 0, 0, tiled=True)  9.17 us
    all_to_all x1, waiting for transfers between devices, local(): got = lax.all_to_all(chunks, 'feat', 0, 0, tiled=True)  8.84 us
    all_to_all x1, starting transfers between devices, local(): whole = lax.all_to_all(spread, ('pair', 'feat'), 0, 0, tiled=True)  7.11 us
    unnamed x24, local copies, waits for them, and re-layouts  4.96 us
  transfers between devices with their start and end apart: 2, of which 2 were waited for; matrix products, arithmetic and copies ran while one was open for 1% of the time, Pallas kernels for 0%

profile of v1, /device:TPU:1, one launch (start us, length us, event | category | flops | bytes accessed | tf_op | source)
XLA Modules:
  0.0 99.0 jit_solution(11292779436046811651)
XLA Ops:
  0.6 0.7 copy-done.6
  1.3 0.9 copy-done
  2.3 0.8 copy-done.4
  3.0 0.7 copy-done.5
  3.7 0.7 copy-done.7
  4.4 10.9 %pick.1 = bf16[32,8,640]{2,1,0:T(8,128)(2,1)} custom-call(bf16[4,4096]{1,0:T(4,128)(2,1)S(1)} %copy-done.4, s32[15,4096]{1,0:T(8,128)S(1)} %bitcast.16, s32[1,4096]{1,0:T(1,128)S(1)} %bitcast.17, bf16[4,256]{1,0:T(4,128)(2,1)S(1)} %copy-done.6, bf16[4,256]{1,0:T(4,128)(2,1)S(1)} %copy-done.7), custom_call_target="tpu_custom_call" | custom-call | tf_op jit(solution)/shard_map/pick/pallas_call | solution.py:145
  15.3 10.5 %all-to-all-start = ((bf16[32,8,640]{2,1,0:T(8,128)(2,1)}), bf16[32,8,640]{2,1,0:T(8,128)(2,1)S(1)}, u32[]{:S(2)}, u32[]{:S(2)}) async-start(bf16[32,8,640]{2,1,0:T(8,128)(2,1)} %pick.1), calls=%async_computation | async-start | bytes 655360 | tf_op jit(solution)/shard_map/all_to_all | solution.py:155
  25.9 0.0 copy-start.2
  25.9 0.1 copy.40
  26.1 0.5 copy-done.11
  26.6 0.1 copy.42.counts_ref
  26.7 8.8 %all-to-all-done = bf16[32,8,640]{2,1,0:T(8,128)(2,1)S(1)} async-done(((bf16[32,8,640]{2,1,0:T(8,128)(2,1)}), bf16[32,8,640]{2,1,0:T(8,128)(2,1)S(1)}, u32[]{:S(2)}, u32[]{:S(2)}) %all-to-all-start) | async-done | bytes 327712 | tf_op jit(solution)/shard_map/all_to_all | solution.py:155
  35.5 0.7 copy-done.8
  36.2 1.6 %layers.1 = (bf16[128,256]{1,0:T(8,128)(2,1)}, f32[512,256]{1,0:T(8,128)S(1)}, f32[1,256]{1,0:T(1,128)S(1)}) custom-call(bf16[256,640]{1,0:T(8,128)(2,1)S(1)} %bitcast.14, s32[128,10]{1,0:T(8,128)S(1)} %broadcast_add_fusion.ids_ref, s32[128,1]{1,0:T(8,128)S(1)} %copy.42.counts_ref, f32[1,256]{1,0:T(1,128)S(1)} %bitcast.18, bf16[256,256]{1,0:T(8,128)(2,1)S(1)} %copy-done.1, ...), custom_call_target="tpu_custom_call" | custom-call | tf_op jit(solution)/shard_map/layers/pallas_call | solution.py:157
  37.8 0.3 copy.43
  38.1 0.3 pad_maximum_fusion
  38.4 16.7 %all_to_all.20 = f32[64,9,2,128]{3,2,1,0:T(2,128)S(1)} all-to-all(f32[64,9,2,128]{3,2,1,0:T(2,128)S(1)} %pad_maximum_fusion), channel_id=1, replica_groups=mesh['apart'=8,'pair'=2,'feat'=32] {'pair','feat'}, dimensions={0} | all-to-all | bytes 1179648 | tf_op jit(solution)/shard_map/all_to_all | solution.py:181
  55.1 0.2 reduce_sum.18
  55.3 25.2 %all_to_all.21 = f32[8,9,2,128]{3,2,1,0:T(2,128)S(1)} all-to-all(f32[8,9,2,128]{3,2,1,0:T(2,128)S(1)} %broadcast_in_dim.28), channel_id=1, replica_groups=mesh['apart'=8,'pair'=2,'feat'=32] {'apart'}, dimensions={0} | all-to-all | bytes 147456 | tf_op jit(solution)/shard_map/all_to_all | solution.py:183
  80.6 0.7 broadcast_in_dim.29
  81.3 7.1 %all-to-all-start.3 = ((bf16[64,8,2,128]{3,1,2,0:T(8,128)(2,1)}), bf16[64,8,2,128]{3,1,2,0:T(8,128)(2,1)S(1)}, u32[]{:S(2)}, u32[]{:S(2)}) async-start(bf16[64,8,2,128]{3,1,2,0:T(8,128)(2,1)} %broadcast_in_dim.29), calls=%async_computation.3 | async-start | bytes 524288 | tf_op jit(solution)/shard_map/all_to_all | solution.py:189
  88.4 0.6 slice_bitcast_fusion.2
  89.0 9.2 %all-to-all-done.3 = bf16[64,8,2,128]{3,1,2,0:T(8,128)(2,1)S(1)} async-done(((bf16[64,8,2,128]{3,1,2,0:T(8,128)(2,1)}), bf16[64,8,2,128]{3,1,2,0:T(8,128)(2,1)S(1)}, u32[]{:S(2)}, u32[]{:S(2)}) %all-to-all-start.3) | async-done | bytes 262176 | tf_op jit(solution)/shard_map/all_to_all | solution.py:189
  98.2 0.8 slice_bitcast_fusion
  (25 shorter events, 0.2 us)
Async XLA Ops:
  0.6 0.7 copy-start.6
  1.3 0.9 copy-start
  2.3 0.8 copy-start.4
  3.0 0.7 copy-start.5
  3.7 0.7 copy-start.7
  15.3 10.6 %copy-start.10 = (s32[128,10]{0,1:T(8,128)S(1)}, s32[128,10]{0,1:T(8,128)}, u32[]{:S(2)}) copy-start(s32[128,10]{0,1:T(8,128)} %param.15) | copy-start | bytes 15364
  15.3 20.2 %copy-start.3 = (bf16[128,256]{1,0:T(8,128)(2,1)S(1)}, bf16[128,256]{1,0:T(8,128)(2,1)}, u32[]{:S(2)}) copy-start(bf16[128,256]{1,0:T(8,128)(2,1)} %cot_ref.1) | copy-start | bytes 196612
  15.3 20.2 %all-to-all-start = ((bf16[32,8,640]{2,1,0:T(8,128)(2,1)}), bf16[32,8,640]{2,1,0:T(8,128)(2,1)S(1)}, u32[]{:S(2)}, u32[]{:S(2)}) async-start(bf16[32,8,640]{2,1,0:T(8,128)(2,1)} %pick.1), calls=%async_computation | async-start | bytes 655360 | tf_op jit(solution)/shard_map/all_to_all | solution.py:155
  25.9 0.7 copy-start.11
  25.9 9.6 %copy-start.1 = (bf16[256,256]{1,0:T(8,128)(2,1)S(1)}, bf16[256,256]{1,0:T(8,128)(2,1)}, u32[]{:S(2)}) copy-start(bf16[256,256]{1,0:T(8,128)(2,1)} %self_ref.3) | copy-start | bytes 393220
  25.9 9.6 %copy-start.2 = (bf16[256,256]{1,0:T(8,128)(2,1)S(1)}, bf16[256,256]{1,0:T(8,128)(2,1)}, u32[]{:S(2)}) copy-start(bf16[256,256]{1,0:T(8,128)(2,1)} %neigh_ref.3) | copy-start | bytes 393220
  26.7 8.9 %copy-start.9 = (f32[256]{0:T(256)S(1)}, f32[256]{0:T(256)}, u32[]{:S(2)}) copy-start(f32[256]{0:T(256)} %param.22) | copy-start | bytes 3076
  35.5 0.7 copy-start.8
  81.3 16.8 %all-to-all-start.3 = ((bf16[64,8,2,128]{3,1,2,0:T(8,128)(2,1)}), bf16[64,8,2,128]{3,1,2,0:T(8,128)(2,1)S(1)}, u32[]{:S(2)}, u32[]{:S(2)}) async-start(bf16[64,8,2,128]{3,1,2,0:T(8,128)(2,1)} %broadcast_in_dim.29), calls=%async_computation.3 | async-start | bytes 524288 | tf_op jit(solution)/shard_map/all_to_all | solution.py:189

commit v2 on v1

--- a/solution.py
+++ b/solution.py
@@ -13,58 +13,98 @@
 INNER = math.sqrt(2.0 / math.pi)
 CUBIC = 0.044715
 VMEM_BYTES = 48 * 1024 * 1024
-
-
-def pick_kernel(feats_ref, ids_ref, counts_ref, self_ref, neigh_ref, out_ref, table, sums):
+PICK_VMEM_BYTES = 57_000_000
+
+
+WITHIN = lax.GatherDimensionNumbers(
+    offset_dims=(),
+    collapsed_slice_dims=(1,),
+    start_index_map=(1,),
+    operand_batching_dims=(0,),
+    start_indices_batching_dims=(0,),
+)
+
+
+def lane_gather(table, lane):
+    return lax.gather(
+        table, lane[..., None], WITHIN, (1, 1), mode=lax.GatherScatterMode.PROMISE_IN_BOUNDS
+    )
+
+
+def pick_kernel(
+    feats_hbm, ids_hbm, counts_hbm, self_hbm, neigh_hbm, out_ref,
+    feats_ref, ids_ref, counts_ref, self_ref, neigh_ref, wide, table, sums, arrived,
+):
+    copies = [
+        pltpu.make_async_copy(source, target, arrived.at[i])
+        for i, (source, target) in enumerate(
+            (
+                (feats_hbm, feats_ref),
+                (ids_hbm, ids_ref),
+                (counts_hbm, counts_ref),
+                (self_hbm, self_ref),
+                (neigh_hbm, neigh_ref),
+            )
+        )
+    ]
+    for copy in copies:
+        copy.start()
     rows, nodes = feats_ref.shape
     fan = ids_ref.shape[0]
     blocks = nodes // LANES
-    wide = feats_ref[...].astype(jnp.float32)
-    table[0:rows, :] = wide
-    table[rows : 2 * rows, :] = wide
+    copies[0].wait()
+    values = feats_ref[...].astype(jnp.float32)
+    wide[0:rows, :] = values
+    wide[rows : 2 * rows, :] = values
+    table[...] = jnp.concatenate([wide[...]] * 2, axis=0).astype(jnp.bfloat16)
+    for copy in copies[1:]:
+        copy.wait()
+    row = lax.broadcasted_iota(jnp.int32, (4 * rows, LANES), 0)
     upper = lax.broadcasted_iota(jnp.int32, (2 * rows, LANES), 0) < rows
 
-    def two_blocks(pair, carry):
-        start = pl.multiple_of(pair * 2 * LANES, 2 * LANES)
-        first, second = pl.ds(start, LANES), pl.ds(start + LANES, LANES)
-
-        def both(ref, k):
+    def four_blocks(quad, carry):
+        start = pl.multiple_of(quad * 4 * LANES, 4 * LANES)
+
+        def spread(ref, k):
+            parts = [
+                jnp.broadcast_to(ref[k : k + 1, pl.ds(start + i * LANES, LANES)], row.shape)
+                for i in range(4)
+            ]
             return jnp.where(
-                upper,
-                jnp.broadcast_to(ref[k : k + 1, first], upper.shape),
-                jnp.broadcast_to(ref[k : k + 1, second], upper.shape),
+                row < 2 * rows,
+                jnp.where(row < rows, parts[0], parts[1]),
+                jnp.where(row < 3 * rows, parts[2], parts[3]),
             )
 
-        counts = both(counts_ref, 0)
-        total = jnp.zeros(upper.shape, jnp.float32)
+        counts = spread(counts_ref, 0)
+        total = jnp.zeros(row.shape, jnp.float32)
         for k in range(fan):
-            ids = both(ids_ref, k)
-            lane = jnp.bitwise_and(ids, LANES - 1)
-            block = lax.shift_right_logical(ids, 7)
+            ids = spread(ids_ref, k)
+            lane = jnp.bitwise_and(ids, LANES - 1).astype(jnp.int16)
+            block = lax.shift_right_logical(ids, 7).astype(jnp.int16)
             level = [
-                jnp.take_along_axis(
-                    table[:, j * LANES : (j + 1) * LANES], lane, axis=1, mode="promise_in_bounds"
-                )
-                for j in range(blocks)
+                lane_gather(table[:, j * LANES : (j + 1) * LANES], lane) for j in range(blocks)
             ]
             bit = 1
             while len(level) > 1:
-                odd = jnp.bitwise_and(block, bit) != 0
+                odd = jnp.bitwise_and(block, jnp.int16(bit)) != 0
                 level = [
                     jnp.where(odd, level[i + 1], level[i]) for i in range(0, len(level), 2)
                 ]
                 bit *= 2
-            total = total + jnp.where(counts > k, level[0], 0.0)
+            total = total + jnp.where(counts > k, level[0].astype(jnp.float32), 0.0)
         mean = total / counts.astype(jnp.float32)
-        at_first = pl.multiple_of(start + LANES, LANES)
-        at_second = pl.multiple_of(start + 2 * LANES, LANES)
-        sums[:, pl.ds(at_first, LANES)] = jnp.where(
-            upper, table[:, first], pltpu.roll(mean, rows, axis=0)
-        )
-        sums[:, pl.ds(at_second, LANES)] = jnp.where(upper, table[:, second], mean)
+        for i in range(4):
+            half = mean[(i // 2) * 2 * rows : (i // 2 + 1) * 2 * rows]
+            if i % 2 == 0:
+                half = pltpu.roll(half, rows, axis=0)
+            to = pl.multiple_of(start + (i + 1) * LANES, LANES)
+            sums[:, pl.ds(to, LANES)] = jnp.where(
+                upper, wide[:, pl.ds(start + i * LANES, LANES)], half
+            )
         return carry
 
-    lax.fori_loop(0, blocks // 2, two_blocks, 0)
+    lax.fori_loop(0, blocks // 4, four_blocks, 0)
     sums[:, 0:LANES] = sums[:, blocks * LANES : (blocks + 1) * LANES]
     sums[:, (blocks + 1) * LANES :] = sums[:, LANES : 2 * LANES]
     weights = jnp.concatenate(
@@ -145,11 +185,19 @@
     chunks = pl.pallas_call(
         pick_kernel,
         out_shape=jax.ShapeDtypeStruct((groups, 2 * rows, span + hid), jnp.bfloat16),
+        in_specs=[pl.BlockSpec(memory_space=pltpu.HBM)] * 5,
         scratch_shapes=[
+            pltpu.VMEM(features.shape, features.dtype),
+            pltpu.VMEM(neighbours_one.shape[::-1], jnp.int32),
+            pltpu.VMEM((1, batch_nodes), jnp.int32),
+            pltpu.VMEM(self_one.shape, self_one.dtype),
+            pltpu.VMEM(neigh_one.shape, neigh_one.dtype),
             pltpu.VMEM((2 * rows, batch_nodes), jnp.float32),
+            pltpu.VMEM((4 * rows, batch_nodes), jnp.bfloat16),
             pltpu.VMEM((2 * rows, batch_nodes + 2 * node_rows), jnp.float32),
+            pltpu.SemaphoreType.DMA((5,)),
         ],
-        compiler_params=params,
+        compiler_params=pltpu.CompilerParams(vmem_limit_bytes=PICK_VMEM_BYTES),
         name="pick",
     )(features, neighbours_one.T, counts_one[None, :], self_one, neigh_one)
     got = lax.all_to_all(chunks, "feat", 0, 0, tiled=True)

time: 99.6 us -> 91.6 us (0.920)
  Pallas kernels: 12.5 us -> 8.46 us
  local copies, waits for them, and re-layouts: 7.63 us -> 3.86 us
    pallas_call x1, Pallas kernels: 10.9 us -> 6.88 us  [local(): pl.pallas_call(pick_kernel, out_shape=jax.ShapeDtypeStruct((groups, 2 * r...]
    unnamed x24 -> x14, local copies, waits for them, and re-layouts: 4.96 us -> 1.19 us
where the time goes in v2:
time: 91.6 us; the launch traced here: 91.2 us
  blocking collectives  41.9 us (46%)
  waiting for transfers between devices  18 us (20%)
  starting transfers between devices  17.7 us (19%)
  Pallas kernels  8.46 us (9%)
  local copies, waits for them, and re-layouts  3.86 us (4%)
    all_to_all x1, blocking collectives, local(): total = lax.all_to_all(spread, 'apart', 0, 0, tiled=True).sum(axis=0)  25.2 us
    all_to_all x1, blocking collectives, local(): lax.all_to_all(parts, ('pair', 'feat'), 0, 0, tiled=True).sum(axis=0)  16.7 us
    all_to_all x1, starting transfers between devices, local(): got = lax.all_to_all(chunks, 'feat', 0, 0, tiled=True)  10.5 us
    all_to_all x1, waiting for transfers between devices, local(): whole = lax.all_to_all(spread, ('pair', 'feat'), 0, 0, tiled=True)  9.17 us
    all_to_all x1, waiting for transfers between devices, local(): got = lax.all_to_all(chunks, 'feat', 0, 0, tiled=True)  8.84 us
    all_to_all x1, starting transfers between devices, local(): whole = lax.all_to_all(spread, ('pair', 'feat'), 0, 0, tiled=True)  7.11 us
    pallas_call x1, Pallas kernels, local(): pl.pallas_call(pick_kernel, out_shape=jax.ShapeDtypeStruct((groups, 2 * r...  6.88 us
  transfers between devices with their start and end apart: 2, of which 2 were waited for; matrix products, arithmetic and copies ran while one was open for 1% of the time, Pallas kernels for 0%

profile of v2, /device:TPU:1, one launch (start us, length us, event | category | flops | bytes accessed | tf_op | source)
XLA Modules:
  0.0 91.2 jit_solution(8174544357983476989)
XLA Ops:
  0.6 6.9 %pick.1 = bf16[32,8,640]{2,1,0:T(8,128)(2,1)} custom-call(bf16[4,4096]{1,0:T(4,128)(2,1)} %feats_hbm.1, s32[15,4096]{1,0:T(8,128)} %bitcast.19, s32[1,4096]{1,0:T(1,128)} %bitcast.20, bf16[4,256]{1,0:T(4,128)(2,1)} %self_hbm.1, bf16[4,256]{1,0:T(4,128)(2,1)} %neigh_hbm.1), custom_call_target="tpu_custom_call" | custom-call | tf_op jit(solution)/shard_map/pick/pallas_call | solution.py:185
  7.5 0.0 copy-start.5
  7.5 0.0 copy-start.2
  7.5 10.5 %all-to-all-start = ((bf16[32,8,640]{2,1,0:T(8,128)(2,1)}), bf16[32,8,640]{2,1,0:T(8,128)(2,1)S(1)}, u32[]{:S(2)}, u32[]{:S(2)}) async-start(bf16[32,8,640]{2,1,0:T(8,128)(2,1)} %pick.1), calls=%async_computation | async-start | bytes 655360 | tf_op jit(solution)/shard_map/all_to_all | solution.py:203
  18.1 0.0 copy-start.6
  18.1 0.0 copy-start
  18.1 0.0 copy-start.1
  18.2 0.1 copy.40
  18.3 0.5 copy-done.6
  18.8 0.1 copy.42.counts_ref
  18.9 8.8 %all-to-all-done = bf16[32,8,640]{2,1,0:T(8,128)(2,1)S(1)} async-done(((bf16[32,8,640]{2,1,0:T(8,128)(2,1)}), bf16[32,8,640]{2,1,0:T(8,128)(2,1)S(1)}, u32[]{:S(2)}, u32[]{:S(2)}) %all-to-all-start) | async-done | bytes 327712 | tf_op jit(solution)/shard_map/all_to_all | solution.py:203
  27.8 0.0 copy-done
  27.8 0.7 copy-done.3
  28.4 1.6 %layers.1 = (bf16[128,256]{1,0:T(8,128)(2,1)}, f32[512,256]{1,0:T(8,128)S(1)}, f32[1,256]{1,0:T(1,128)S(1)}) custom-call(bf16[256,640]{1,0:T(8,128)(2,1)S(1)} %bitcast.14, s32[128,10]{1,0:T(8,128)S(1)} %broadcast_add_fusion.ids_ref, s32[128,1]{1,0:T(8,128)S(1)} %copy.42.counts_ref, f32[1,256]{1,0:T(1,128)S(1)} %bitcast.16, bf16[256,256]{1,0:T(8,128)(2,1)S(1)} %copy-done, ...), custom_call_target="tpu_custom_call" | custom-call | tf_op jit(solution)/shard_map/layers/pallas_call | solution.py:205
  30.0 0.3 copy.43
  30.3 0.3 pad_maximum_fusion
  30.6 16.7 %all_to_all.20 = f32[64,9,2,128]{3,2,1,0:T(2,128)S(1)} all-to-all(f32[64,9,2,128]{3,2,1,0:T(2,128)S(1)} %pad_maximum_fusion), channel_id=1, replica_groups=mesh['apart'=8,'pair'=2,'feat'=32] {'pair','feat'}, dimensions={0} | all-to-all | bytes 1179648 | tf_op jit(solution)/shard_map/all_to_all | solution.py:229
  47.3 0.2 reduce_sum.18
  47.5 25.2 %all_to_all.21 = f32[8,9,2,128]{3,2,1,0:T(2,128)S(1)} all-to-all(f32[8,9,2,128]{3,2,1,0:T(2,128)S(1)} %broadcast_in_dim.28), channel_id=1, replica_groups=mesh['apart'=8,'pair'=2,'feat'=32] {'apart'}, dimensions={0} | all-to-all | bytes 147456 | tf_op jit(solution)/shard_map/all_to_all | solution.py:231
  72.8 0.7 broadcast_in_dim.29
  73.5 7.1 %all-to-all-start.3 = ((bf16[64,8,2,128]{3,1,2,0:T(8,128)(2,1)}), bf16[64,8,2,128]{3,1,2,0:T(8,128)(2,1)S(1)}, u32[]{:S(2)}, u32[]{:S(2)}) async-start(bf16[64,8,2,128]{3,1,2,0:T(8,128)(2,1)} %broadcast_in_dim.29), calls=%async_computation.3 | async-start | bytes 524288 | tf_op jit(solution)/shard_map/all_to_all | solution.py:237
  80.6 0.6 slice_bitcast_fusion.2
  81.2 9.2 %all-to-all-done.3 = bf16[64,8,2,128]{3,1,2,0:T(8,128)(2,1)S(1)} async-done(((bf16[64,8,2,128]{3,1,2,0:T(8,128)(2,1)}), bf16[64,8,2,128]{3,1,2,0:T(8,128)(2,1)S(1)}, u32[]{:S(2)}, u32[]{:S(2)}) %all-to-all-start.3) | async-done | bytes 262176 | tf_op jit(solution)/shard_map/all_to_all | solution.py:237
  90.4 0.8 slice_bitcast_fusion
  (15 shorter events, 0.1 us)
Async XLA Ops:
  7.5 10.6 %copy-start.5 = (s32[128,10]{0,1:T(8,128)S(1)}, s32[128,10]{0,1:T(8,128)}, u32[]{:S(2)}) copy-start(s32[128,10]{0,1:T(8,128)} %param.15) | copy-start | bytes 15364
  7.5 20.2 %copy-start.2 = (bf16[128,256]{1,0:T(8,128)(2,1)S(1)}, bf16[128,256]{1,0:T(8,128)(2,1)}, u32[]{:S(2)}) copy-start(bf16[128,256]{1,0:T(8,128)(2,1)} %cot_ref.1) | copy-start | bytes 196612
  7.5 20.2 %all-to-all-start = ((bf16[32,8,640]{2,1,0:T(8,128)(2,1)}), bf16[32,8,640]{2,1,0:T(8,128)(2,1)S(1)}, u32[]{:S(2)}, u32[]{:S(2)}) async-start(bf16[32,8,640]{2,1,0:T(8,128)(2,1)} %pick.1), calls=%async_computation | async-start | bytes 655360 | tf_op jit(solution)/shard_map/all_to_all | solution.py:203
  18.1 0.7 copy-start.6
  18.1 9.6 %copy-start = (bf16[256,256]{1,0:T(8,128)(2,1)S(1)}, bf16[256,256]{1,0:T(8,128)(2,1)}, u32[]{:S(2)}) copy-start(bf16[256,256]{1,0:T(8,128)(2,1)} %self_ref.1) | copy-start | bytes 393220
  18.1 9.6 %copy-start.1 = (bf16[256,256]{1,0:T(8,128)(2,1)S(1)}, bf16[256,256]{1,0:T(8,128)(2,1)}, u32[]{:S(2)}) copy-start(bf16[256,256]{1,0:T(8,128)(2,1)} %neigh_ref.1) | copy-start | bytes 393220
  18.9 8.9 %copy-start.4 = (f32[256]{0:T(256)S(1)}, f32[256]{0:T(256)}, u32[]{:S(2)}) copy-start(f32[256]{0:T(256)} %param.22) | copy-start | bytes 3076
  27.7 0.7 copy-start.3
  73.5 16.8 %all-to-all-start.3 = ((bf16[64,8,2,128]{3,1,2,0:T(8,128)(2,1)}), bf16[64,8,2,128]{3,1,2,0:T(8,128)(2,1)S(1)}, u32[]{:S(2)}, u32[]{:S(2)}) async-start(bf16[64,8,2,128]{3,1,2,0:T(8,128)(2,1)} %broadcast_in_dim.29), calls=%async_computation.3 | async-start | bytes 524288 | tf_op jit(solution)/shard_map/all_to_all | solution.py:237

commit v3 on v2

--- a/solution.py
+++ b/solution.py
@@ -1,4 +1,3 @@
-import functools
 import math
 
 import jax
@@ -110,11 +109,11 @@
     weights = jnp.concatenate(
         [self_ref[...].astype(jnp.float32), neigh_ref[...].astype(jnp.float32)], axis=0
     ).astype(jnp.bfloat16)
-    for block in range(blocks):
-        out_ref[block, :, 0 : 3 * LANES] = sums[
-            :, block * LANES : (block + 3) * LANES
-        ].astype(jnp.bfloat16)
-        out_ref[block, :, 3 * LANES :] = weights
+    for first in range(0, blocks, 2):
+        span = sums[:, first * LANES : (first + 4) * LANES].astype(jnp.bfloat16)
+        for block in (first, first + 1):
+            out_ref[block, :, 0 : 4 * LANES] = span
+            out_ref[block, :, 4 * LANES :] = weights
 
 
 def gelu_parts(value):
@@ -126,40 +125,65 @@
 
 
 def layers_kernel(
-    got_ref, ids_ref, counts_ref, bias_one_ref, self_ref, neigh_ref, bias_two_ref, cot_ref,
-    hidden_ref, grads_ref, bias_ref,
+    core_ref, got_ref, own_meta_ref, other_meta_ref, counts_ref, bias_ref, self_ref, neigh_ref,
+    own_cot_ref, other_cot_ref, hidden_ref, grads_ref, bias_grad_ref,
 ):
-    node_rows = cot_ref.shape[0]
-    hid = cot_ref.shape[1]
-    span = 3 * node_rows
-    fan = ids_ref.shape[1]
+    node_rows, hid = own_cot_ref.shape
+    span = 4 * node_rows
+    fan = own_meta_ref.shape[0]
     over_rows = (((0,), (0,)), ((), ()))
+    is_first = core_ref[0] == 0
     got = got_ref[...]
     pre_one = lax.dot_general(
         got[:, :span], got[:, span:], over_rows, preferred_element_type=jnp.float32
     )
-    hidden = gelu_parts(pre_one + bias_one_ref[...])[0].astype(jnp.bfloat16)
-    own = hidden[node_rows : 2 * node_rows]
-    ids, counts = ids_ref[...], counts_ref[...]
-    column = lax.broadcasted_iota(jnp.int32, (node_rows, span), 1)
-    often = jnp.zeros((node_rows, span), jnp.float32)
-    for k in range(fan):
-        hit = jnp.where(counts > k, ids[:, k : k + 1], -1) == column
-        often = often + jnp.where(hit, 1.0, 0.0)
-    summed = jnp.dot(often.astype(jnp.bfloat16), hidden, preferred_element_type=jnp.float32)
-    agg = (summed / counts.astype(jnp.float32)).astype(jnp.bfloat16)
+    hidden = gelu_parts(pre_one + bias_ref[0:1, :])[0].astype(jnp.bfloat16)
+    own = hidden[node_rows : 3 * node_rows]
+    own_meta, other_meta = own_meta_ref[...], other_meta_ref[...]
+    number = lax.broadcasted_iota(jnp.int32, (span, node_rows), 0).astype(jnp.int16)
+    one, zero = jnp.ones((), jnp.bfloat16), jnp.zeros((), jnp.bfloat16)
+    often = []
+    for meta in (
+        jnp.where(is_first, own_meta, other_meta),
+        jnp.where(is_first, other_meta, own_meta),
+    ):
+        total = jnp.zeros((span, node_rows), jnp.bfloat16)
+        for k in range(fan):
+            ids = jnp.broadcast_to(meta[k : k + 1, :], (span, node_rows)).astype(jnp.int16)
+            total = total + jnp.where(ids == number, one, zero)
+        often.append(total)
+    summed = lax.dot_general(
+        jnp.concatenate(often, axis=1), hidden, over_rows, preferred_element_type=jnp.float32
+    )
+    agg = (summed / counts_ref[...].astype(jnp.float32)).astype(jnp.bfloat16)
     pre_two = jnp.dot(own, self_ref[...], preferred_element_type=jnp.float32)
     pre_two = pre_two + jnp.dot(agg, neigh_ref[...], preferred_element_type=jnp.float32)
-    value, slope = gelu_parts(pre_two + bias_two_ref[...])
-    hidden_ref[...] = value.astype(jnp.bfloat16)
-    delta = (cot_ref[...].astype(jnp.float32) * slope).astype(jnp.bfloat16)
-    grads_ref[0:hid, :] = lax.dot_general(
-        own, delta, over_rows, preferred_element_type=jnp.float32
-    )
-    grads_ref[hid:, :] = lax.dot_general(
-        agg, delta, over_rows, preferred_element_type=jnp.float32
-    )
-    bias_ref[...] = jnp.sum(delta.astype(jnp.float32), axis=0, keepdims=True)
+    value, slope = gelu_parts(pre_two + bias_ref[1:2, :])
+    hidden_ref[...] = jnp.where(is_first, value[:node_rows], value[node_rows:]).astype(jnp.bfloat16)
+    own_cot = own_cot_ref[...].astype(jnp.float32)
+    other_cot = other_cot_ref[...].astype(jnp.float32)
+    cot = jnp.concatenate(
+        [jnp.where(is_first, own_cot, other_cot), jnp.where(is_first, other_cot, own_cot)], axis=0
+    )
+    delta = (cot * slope).astype(jnp.bfloat16)
+    rows = jnp.where(is_first, own, agg)
+    grads_ref[...] = lax.dot_general(rows, delta, over_rows, preferred_element_type=jnp.float32)
+    bias_grad_ref[...] = jnp.sum(delta.astype(jnp.float32), axis=0, keepdims=True)
+
+
+def repeat_kernel(part_ref, out_ref):
+    part = part_ref[...].astype(jnp.bfloat16)
+    for to in range(out_ref.shape[0]):
+        out_ref[to] = part
+
+
+def widen_kernel(got_ref, self_ref, neigh_ref):
+    pairs, chips, _, rows, _ = got_ref.shape
+    for pair in range(pairs):
+        for chip in range(chips):
+            at = (pair * chips + chip) * rows
+            self_ref[at : at + rows, :] = got_ref[pair, chip, 0].astype(jnp.float32)
+            neigh_ref[at : at + rows, :] = got_ref[pair, chip, 1].astype(jnp.float32)
 
 
 def local(
@@ -177,10 +201,12 @@
     cotangent,
 ):
     rows, batch_nodes = features.shape
-    groups = lax.axis_size("feat")
+    pairs, chips, cores = lax.axis_size("pair"), lax.axis_size("chip"), lax.axis_size("core")
+    others = lax.axis_size("apart")
+    groups = chips * cores
     node_rows = batch_nodes // groups
     hid = self_one.shape[1]
-    span = 3 * node_rows
+    span = 4 * node_rows
     params = pltpu.CompilerParams(vmem_limit_bytes=VMEM_BYTES)
     chunks = pl.pallas_call(
         pick_kernel,
@@ -200,61 +226,96 @@
         compiler_params=pltpu.CompilerParams(vmem_limit_bytes=PICK_VMEM_BYTES),
         name="pick",
     )(features, neighbours_one.T, counts_one[None, :], self_one, neigh_one)
-    got = lax.all_to_all(chunks, "feat", 0, 0, tiled=True)
-    first_node = lax.axis_index("feat") * node_rows
+    got = lax.all_to_all(chunks, ("chip", "core"), 0, 0, tiled=True)
+
+    swap = [(0, 1), (1, 0)]
+    core = lax.axis_index("core")
+    first_node = (lax.axis_index("chip") * cores - 1) * node_rows
+    meta = jnp.concatenate([neighbours_two.T, counts_two[None, :]], axis=0)
+    other_meta = lax.ppermute(meta, "core", swap)
+    other_cot = lax.ppermute(cotangent, "core", swap)
+
+    def numbers(kept):
+        live = jnp.arange(kept.shape[0] - 1, dtype=jnp.int32)[:, None] < kept[-1:]
+        return jnp.where(live, kept[:-1] - first_node, -1)
+
+    counts = jnp.where(
+        core == 0,
+        jnp.concatenate([counts_two, other_meta[-1]]),
+        jnp.concatenate([other_meta[-1], counts_two]),
+    )
     hidden_two, grads, bias = pl.pallas_call(
         layers_kernel,
         out_shape=(
             jax.ShapeDtypeStruct((node_rows, hid), jnp.bfloat16),
-            jax.ShapeDtypeStruct((2 * hid, hid), jnp.float32),
+            jax.ShapeDtypeStruct((hid, hid), jnp.float32),
             jax.ShapeDtypeStruct((1, hid), jnp.float32),
         ),
+        in_specs=[pl.BlockSpec(memory_space=pltpu.SMEM)]
+        + [pl.BlockSpec(memory_space=pltpu.VMEM)] * 9,
         compiler_params=params,
         name="layers",
     )(
+        core[None],
         got.reshape(groups * 2 * rows, span + hid),
-        neighbours_two - first_node + node_rows,
-        counts_two[:, None],
-        bias_one[None, :],
+        numbers(meta),
+        numbers(other_meta),
+        counts[:, None],
+        jnp.stack([bias_one, bias_two]),
         self_two,
         neigh_two,
-        bias_two[None, :],
         cotangent,
-    )
-    group = lax.axis_size("pair") * groups
-    others = lax.axis_size("apart")
+        other_cot,
+    )
+    group = pairs * chips
     parts = jnp.concatenate(
-        [grads.reshape(group, -1, 2, LANES), bias.reshape(1, 1, 2, LANES) * jnp.ones((group, 1, 1, 1), jnp.float32)], axis=1
-    )
-    inner = lax.all_to_all(parts, ("pair", "feat"), 0, 0, tiled=True).sum(axis=0)
+        [
+            grads.reshape(group, -1, 2, LANES),
+            jnp.broadcast_to(bias.reshape(1, 1, 2, LANES), (group, 1, 2, LANES)),
+        ],
+        axis=1,
+    )
+    inner = lax.all_to_all(parts, ("pair", "chip"), 0, 0, tiled=True).sum(axis=0)
     spread = jnp.broadcast_to(inner[None], (others,) + inner.shape)
     total = lax.all_to_all(spread, "apart", 0, 0, tiled=True).sum(axis=0)
-    scale = 1.0 / (batch_nodes * lax.axis_size("pair") * others)
-    total = total * scale
-    total_bias = total[-1].reshape(hid)
-    narrow = total[:-1].astype(jnp.bfloat16)
-    spread = jnp.broadcast_to(narrow[None], (group,) + narrow.shape)
-    whole = lax.all_to_all(spread, ("pair", "feat"), 0, 0, tiled=True)
-    whole = whole.reshape(2 * hid, hid).astype(jnp.float32)
-    return hidden_two, whole[:hid], whole[hid:], total_bias
+    total = total * (1.0 / (batch_nodes * pairs * others))
+    part = total[:-1].reshape(hid // group, hid)
+    everyone = group * cores
+    spread = pl.pallas_call(
+        repeat_kernel,
+        out_shape=jax.ShapeDtypeStruct((everyone,) + part.shape, jnp.bfloat16),
+        compiler_params=params,
+        name="repeat",
+    )(part)
+    whole = lax.all_to_all(spread, ("pair", "chip", "core"), 0, 0, tiled=True)
+    grad_self, grad_neigh = pl.pallas_call(
+        widen_kernel,
+        out_shape=(jax.ShapeDtypeStruct((hid, hid), jnp.float32),) * 2,
+        compiler_params=params,
+        name="widen",
+    )(whole.reshape((pairs, chips, cores) + part.shape))
+    return hidden_two, grad_self, grad_neigh, total[-1].reshape(hid)
 
 
 def solution(mesh):
     replicas, groups = mesh.devices.shape
-    split = Mesh(mesh.devices.reshape(replicas // 2, 2, groups), ("apart", "pair", "feat"))
+    split = Mesh(
+        mesh.devices.reshape(replicas // 2, 2, groups // 2, 2), ("apart", "pair", "chip", "core")
+    )
     dp = ("apart", "pair")
-    every = ("apart", "pair", "feat")
+    feat = ("chip", "core")
+    every = dp + feat
     return jax.shard_map(
         local,
         mesh=split,
         in_specs=(
-            P("feat", dp),
+            P(feat, dp),
             P(dp, None),
             P(dp),
             P(every, None),
             P(every),
-            P("feat", None),
-            P("feat", None),
+            P(feat, None),
+            P(feat, None),
             P(),
             P(),
             P(),

time: 91.6 us -> 87.7 us (0.957)
  starting transfers between devices: 17.7 us -> 22.6 us
  waiting for transfers between devices: 18 us -> 13.3 us
  blocking collectives: 41.9 us -> 37.6 us
  Pallas kernels: 8.46 us -> 10.2 us
  local copies, waits for them, and re-layouts: 3.86 us -> 2.36 us
    all_to_all x1, blocking collectives: 16.7 us -> 11.8 us  [local(): lax.all_to_all(parts, ('pair', 'chip'), 0, 0, tiled=True).sum(axis=0)]
    all_to_all x2, waiting for transfers between devices: 18 us -> 13.3 us  [the longest x1 9.17 us: local(): whole = lax.all_to_all(spread, ('pair', 'chip', 'core'), 0, 0, tiled=True)]
    ppermute x0 -> x2, starting transfers between devices: none -> 4.31 us  [the longest x1 2.24 us: local(): other_meta = lax.ppermute(meta, 'core', swap)]
    pallas_call x0 -> x2, Pallas kernels: none -> 1.55 us  [the longest x1 0.82 us: local(): pl.pallas_call(widen_kernel, out_shape=(jax.ShapeDtypeStruct((hid, hid),...]
  transfers between devices with their start and end apart: 2 -> 4, of which waited for: 2 -> 2; matrix products, arithmetic and copies ran while one was open for 1% -> 1% of each run, Pallas kernels for 0% -> 0%
where the time goes in v3:
time: 87.7 us; the launch traced here: 87.2 us
  blocking collectives  37.6 us (43%)
  starting transfers between devices  22.6 us (26%)
  waiting for transfers between devices  13.3 us (15%)
  Pallas kernels  10.2 us (12%)
  local copies, waits for them, and re-layouts  2.36 us (3%)
    all_to_all x1, blocking collectives, local(): total = lax.all_to_all(spread, 'apart', 0, 0, tiled=True).sum(axis=0)  25.7 us
    all_to_all x1, blocking collectives, local(): lax.all_to_all(parts, ('pair', 'chip'), 0, 0, tiled=True).sum(axis=0)  11.8 us
    all_to_all x1, starting transfers between devices, local(): got = lax.all_to_all(chunks, ('chip', 'core'), 0, 0, tiled=True)  10.6 us
    all_to_all x1, waiting for transfers between devices, local(): whole = lax.all_to_all(spread, ('pair', 'chip', 'core'), 0, 0, tiled=True)  9.17 us
    all_to_all x1, starting transfers between devices, local(): whole = lax.all_to_all(spread, ('pair', 'chip', 'core'), 0, 0, tiled=True)  7.71 us
    pallas_call x1, Pallas kernels, local(): pl.pallas_call(pick_kernel, out_shape=jax.ShapeDtypeStruct((groups, 2 * r...  6.9 us
    all_to_all x1, waiting for transfers between devices, local(): got = lax.all_to_all(chunks, ('chip', 'core'), 0, 0, tiled=True)  4.15 us
    ppermute x1, starting transfers between devices, local(): other_meta = lax.ppermute(meta, 'core', swap)  2.24 us
  transfers between devices with their start and end apart: 4, of which 2 were waited for; matrix products, arithmetic and copies ran while one was open for 1% of the time, Pallas kernels for 0%

profile of v3, /device:TPU:1, one launch (start us, length us, event | category | flops | bytes accessed | tf_op | source)
XLA Modules:
  0.0 87.2 jit_solution(5937610145785660216)
XLA Ops:
  0.6 6.9 %pick.1 = bf16[32,8,768]{2,1,0:T(8,128)(2,1)} custom-call(bf16[4,4096]{1,0:T(4,128)(2,1)} %feats_hbm.1, s32[15,4096]{1,0:T(8,128)} %bitcast.29, s32[1,4096]{1,0:T(1,128)} %bitcast.31, bf16[4,256]{1,0:T(4,128)(2,1)} %self_hbm.1, bf16[4,256]{1,0:T(4,128)(2,1)} %neigh_hbm.1), custom_call_target="tpu_custom_call" | custom-call | tf_op jit(solution)/shard_map/pick/pallas_call | solution.py:211
  7.5 0.0 copy-start.3
  7.5 0.0 copy-start.2
  7.6 10.6 %all-to-all-start = ((bf16[32,8,768]{2,1,0:T(8,128)(2,1)}), bf16[32,8,768]{2,1,0:T(8,128)(2,1)S(1)}, u32[]{:S(2)}, u32[]{:S(2)}) async-start(bf16[32,8,768]{2,1,0:T(8,128)(2,1)} %pick.1), calls=%async_computation | async-start | bytes 786432 | tf_op jit(solution)/shard_map/all_to_all | solution.py:229
  18.1 0.0 copy-start.4
  18.1 0.6 copy-done.4
  18.8 2.2 %collective-permute-start = (s32[11,128]{1,0:T(8,128)S(1)}, s32[11,128]{1,0:T(8,128)S(1)}, u32[]{:S(2)}, u32[]{:S(2)}) collective-permute-start(s32[11,128]{1,0:T(8,128)S(1)} %pad_add_fusion), channel_id=1, source_target_pairs={{0,1},{1,0},{2,3},{3,2},{4,5},{5,4},{6,7},{7,6},{8,9},{9,8},{10,11... | collective-permute-start | bytes 16904 | tf_op jit(solution)/shard_map/ppermute | solution.py:235
  21.1 2.1 %collective-permute-start.1 = (bf16[128,256]{1,0:T(8,128)(2,1)S(1)}, bf16[128,256]{1,0:T(8,128)(2,1)S(1)}, u32[]{:S(2)}, u32[]{:S(2)}) collective-permute-start(bf16[128,256]{1,0:T(8,128)(2,1)S(1)} %copy-done.2), channel_id=1, source_target_pairs={{0,1},{1,0},{2,3},{3,2},{4,5},{5,4},{6,7},{7,6},{8,9},{9,8},{10,11... | collective-permute-start | bytes 196616 | tf_op jit(solution)/shard_map/ppermute | solution.py:236
  23.2 0.6 copy-done.6
  23.8 0.0 copy-done.5
  23.9 0.1 copy.30
  24.0 0.1 copy.31
  24.3 4.2 %all-to-all-done = bf16[32,8,768]{2,1,0:T(8,128)(2,1)S(1)} async-done(((bf16[32,8,768]{2,1,0:T(8,128)(2,1)}), bf16[32,8,768]{2,1,0:T(8,128)(2,1)S(1)}, u32[]{:S(2)}, u32[]{:S(2)}) %all-to-all-start) | async-done | bytes 393248 | tf_op jit(solution)/shard_map/all_to_all | solution.py:229
  28.4 1.8 %layers.1 = (bf16[128,256]{1,0:T(8,128)(2,1)}, f32[256,256]{1,0:T(8,128)S(1)}, f32[1,256]{1,0:T(1,128)S(1)}) custom-call(s32[1]{0:T(128)} %bitcast.core_ref, bf16[256,768]{1,0:T(8,128)(2,1)S(1)} %bitcast.24, s32[10,128]{1,0:T(8,128)S(1)} %subtract_select_fusion.own_meta_ref, s32[10,128]{1,0:T(8,128)S(1)} %fusion.other_meta_ref, ...), custom_call_target="tpu_custom_call" | custom-call | tf_op jit(solution)/shard_map/layers/pallas_call | solution.py:247
  30.2 0.1 copy.32
  30.3 0.1 pad_maximum_fusion
  30.5 11.8 %all_to_all.20 = f32[32,9,2,128]{3,2,1,0:T(2,128)S(1)} all-to-all(f32[32,9,2,128]{3,2,1,0:T(2,128)S(1)} %pad_maximum_fusion), channel_id=1, replica_groups=mesh['apart'=8,'pair'=2,'chip'=16,'core'=2] {'pair','chip'}, dimensions={0} | all-to-all | bytes 589824 | tf_op jit(solution)/shard_map/all_to_all | solution.py:278
  42.3 0.1 reduce_sum.18
  42.5 25.7 %all_to_all.21 = f32[8,9,2,128]{3,2,1,0:T(2,128)S(1)} all-to-all(f32[8,9,2,128]{3,2,1,0:T(2,128)S(1)} %broadcast_in_dim.36), channel_id=1, replica_groups=mesh['apart'=8,'pair'=2,'chip'=16,'core'=2] {'apart'}, dimensions={0} | all-to-all | bytes 147456 | tf_op jit(solution)/shard_map/all_to_all | solution.py:280
  68.2 0.7 repeat.1
  69.0 7.7 %all-to-all-start.3 = ((bf16[64,8,256]{2,1,0:T(8,128)(2,1)}), bf16[64,8,256]{2,1,0:T(8,128)(2,1)S(1)}, u32[]{:S(2)}, u32[]{:S(2)}) async-start(bf16[64,8,256]{2,1,0:T(8,128)(2,1)} %repeat.1), calls=%async_computation.3 | async-start | bytes 524288 | tf_op jit(solution)/shard_map/all_to_all | solution.py:290
  76.7 0.6 slice_bitcast_fusion.1
  77.2 9.2 %all-to-all-done.3 = bf16[64,8,256]{2,1,0:T(8,128)(2,1)S(1)} async-done(((bf16[64,8,256]{2,1,0:T(8,128)(2,1)}), bf16[64,8,256]{2,1,0:T(8,128)(2,1)S(1)}, u32[]{:S(2)}, u32[]{:S(2)}) %all-to-all-start.3) | async-done | bytes 262176 | tf_op jit(solution)/shard_map/all_to_all | solution.py:290
  86.4 0.8 widen.1
  (23 shorter events, 0.2 us)
Async XLA Ops:
  7.5 10.6 %copy-start.3 = (s32[128,10]{0,1:T(8,128)S(1)}, s32[128,10]{0,1:T(8,128)}, u32[]{:S(2)}) copy-start(s32[128,10]{0,1:T(8,128)} %param.15) | copy-start | bytes 15364
  7.5 13.5 %copy-start.2 = (bf16[128,256]{1,0:T(8,128)(2,1)S(1)}, bf16[128,256]{1,0:T(8,128)(2,1)}, u32[]{:S(2)}) copy-start(bf16[128,256]{1,0:T(8,128)(2,1)} %own_cot_ref.1) | copy-start | bytes 196612
  7.6 20.8 %all-to-all-start = ((bf16[32,8,768]{2,1,0:T(8,128)(2,1)}), bf16[32,8,768]{2,1,0:T(8,128)(2,1)S(1)}, u32[]{:S(2)}, u32[]{:S(2)}) async-start(bf16[32,8,768]{2,1,0:T(8,128)(2,1)} %pick.1), calls=%async_computation | async-start | bytes 786432 | tf_op jit(solution)/shard_map/all_to_all | solution.py:229
  18.1 0.7 copy-start.4
  18.8 5.1 %collective-permute-start = (s32[11,128]{1,0:T(8,128)S(1)}, s32[11,128]{1,0:T(8,128)S(1)}, u32[]{:S(2)}, u32[]{:S(2)}) collective-permute-start(s32[11,128]{1,0:T(8,128)S(1)} %pad_add_fusion), channel_id=1, source_target_pairs={{0,1},{1,0},{2,3},{3,2},{4,5},{5,4},{6,7},{7,6},{8,9},{9,8},{10,11... | collective-permute-start | bytes 16904 | tf_op jit(solution)/shard_map/ppermute | solution.py:235
  21.1 3.2 %collective-permute-start.1 = (bf16[128,256]{1,0:T(8,128)(2,1)S(1)}, bf16[128,256]{1,0:T(8,128)(2,1)S(1)}, u32[]{:S(2)}, u32[]{:S(2)}) collective-permute-start(bf16[128,256]{1,0:T(8,128)(2,1)S(1)} %copy-done.2), channel_id=1, source_target_pairs={{0,1},{1,0},{2,3},{3,2},{4,5},{5,4},{6,7},{7,6},{8,9},{9,8},{10,11... | collective-permute-start | bytes 196616 | tf_op jit(solution)/shard_map/ppermute | solution.py:236
  23.1 0.7 copy-start.6
  23.2 0.7 copy-start.5
  24.2 4.2 %copy-start = (bf16[256,256]{1,0:T(8,128)(2,1)S(1)}, bf16[256,256]{1,0:T(8,128)(2,1)}, u32[]{:S(2)}) copy-start(bf16[256,256]{1,0:T(8,128)(2,1)} %self_ref.1) | copy-start | bytes 393220
  24.2 4.2 %copy-start.1 = (bf16[256,256]{1,0:T(8,128)(2,1)S(1)}, bf16[256,256]{1,0:T(8,128)(2,1)}, u32[]{:S(2)}) copy-start(bf16[256,256]{1,0:T(8,128)(2,1)} %neigh_ref.1) | copy-start | bytes 393220
  69.0 17.4 %all-to-all-start.3 = ((bf16[64,8,256]{2,1,0:T(8,128)(2,1)}), bf16[64,8,256]{2,1,0:T(8,128)(2,1)S(1)}, u32[]{:S(2)}, u32[]{:S(2)}) async-start(bf16[64,8,256]{2,1,0:T(8,128)(2,1)} %repeat.1), calls=%async_computation.3 | async-start | bytes 524288 | tf_op jit(solution)/shard_map/all_to_all | solution.py:290

commit v4 on v3

--- a/solution.py
+++ b/solution.py
@@ -1,3 +1,4 @@
+import functools
 import math
 
 import jax
@@ -31,7 +32,7 @@
 
 
 def pick_kernel(
-    feats_hbm, ids_hbm, counts_hbm, self_hbm, neigh_hbm, out_ref,
+    order, feats_hbm, ids_hbm, counts_hbm, self_hbm, neigh_hbm, out_ref,
     feats_ref, ids_ref, counts_ref, self_ref, neigh_ref, wide, table, sums, arrived,
 ):
     copies = [
@@ -103,7 +104,7 @@
             )
         return carry
 
-    lax.fori_loop(0, blocks // 4, four_blocks, 0)
+    lax.fori_loop(0, blocks // 4, four_blocks, 0, unroll=True)
     sums[:, 0:LANES] = sums[:, blocks * LANES : (blocks + 1) * LANES]
     sums[:, (blocks + 1) * LANES :] = sums[:, LANES : 2 * LANES]
     weights = jnp.concatenate(
@@ -112,8 +113,9 @@
     for first in range(0, blocks, 2):
         span = sums[:, first * LANES : (first + 4) * LANES].astype(jnp.bfloat16)
         for block in (first, first + 1):
-            out_ref[block, :, 0 : 4 * LANES] = span
-            out_ref[block, :, 4 * LANES :] = weights
+            to = order.index(block)
+            out_ref[to, :, 0 : 4 * LANES] = span
+            out_ref[to, :, 4 * LANES :] = weights
 
 
 def gelu_parts(value):
@@ -126,7 +128,7 @@
 
 def layers_kernel(
     core_ref, got_ref, own_meta_ref, other_meta_ref, counts_ref, bias_ref, self_ref, neigh_ref,
-    own_cot_ref, other_cot_ref, hidden_ref, grads_ref, bias_grad_ref,
+    own_cot_ref, other_cot_ref, hidden_ref, parts_ref,
 ):
     node_rows, hid = own_cot_ref.shape
     span = 4 * node_rows
@@ -167,23 +169,35 @@
     )
     delta = (cot * slope).astype(jnp.bfloat16)
     rows = jnp.where(is_first, own, agg)
-    grads_ref[...] = lax.dot_general(rows, delta, over_rows, preferred_element_type=jnp.float32)
-    bias_grad_ref[...] = jnp.sum(delta.astype(jnp.float32), axis=0, keepdims=True)
+    grads = lax.dot_general(rows, delta, over_rows, preferred_element_type=jnp.float32)
+    bias = jnp.sum(delta.astype(jnp.float32), axis=0, keepdims=True)
+    row = lax.broadcasted_iota(jnp.int32, (8, LANES), 0)
+    halves = jnp.where(
+        row == 0,
+        jnp.broadcast_to(bias[:, :LANES], row.shape),
+        jnp.where(row == 1, jnp.broadcast_to(bias[:, LANES:], row.shape), 0.0),
+    )
+    for part in range(parts_ref.shape[0]):
+        parts_ref[part, 0:8, :] = grads[part * 8 : part * 8 + 8, :LANES]
+        parts_ref[part, 8:16, :] = grads[part * 8 : part * 8 + 8, LANES:]
+        parts_ref[part, 16:24, :] = halves
 
 
 def repeat_kernel(part_ref, out_ref):
-    part = part_ref[...].astype(jnp.bfloat16)
+    part = jnp.concatenate([part_ref[0:8, :], part_ref[8:16, :]], axis=1).astype(jnp.bfloat16)
     for to in range(out_ref.shape[0]):
         out_ref[to] = part
 
 
 def widen_kernel(got_ref, self_ref, neigh_ref):
-    pairs, chips, _, rows, _ = got_ref.shape
-    for pair in range(pairs):
-        for chip in range(chips):
-            at = (pair * chips + chip) * rows
-            self_ref[at : at + rows, :] = got_ref[pair, chip, 0].astype(jnp.float32)
-            neigh_ref[at : at + rows, :] = got_ref[pair, chip, 1].astype(jnp.float32)
+    parts, _, rows, _ = got_ref.shape
+    for part in range(parts):
+        self_ref[part * rows : (part + 1) * rows, :] = got_ref[part, 0].astype(jnp.float32)
+        neigh_ref[part * rows : (part + 1) * rows, :] = got_ref[part, 1].astype(jnp.float32)
+
+
+def from_member(first, size):
+    return [(first + i) % size for i in range(size)]
 
 
 def local(
@@ -208,8 +222,16 @@
     hid = self_one.shape[1]
     span = 4 * node_rows
     params = pltpu.CompilerParams(vmem_limit_bytes=VMEM_BYTES)
+    group = pairs * chips
+    everyone = group * cores
+    first_chip = chips // 2 + chips // 8
+    first_part = group - chips + first_chip
+    feat_order = from_member(first_chip * cores, groups)
+    part_order = from_member(first_part, group)
+    every_order = from_member(first_part * cores, everyone)
+    apart_order = from_member(others // 2, others)
     chunks = pl.pallas_call(
-        pick_kernel,
+        functools.partial(pick_kernel, feat_order),
         out_shape=jax.ShapeDtypeStruct((groups, 2 * rows, span + hid), jnp.bfloat16),
         in_specs=[pl.BlockSpec(memory_space=pltpu.HBM)] * 5,
         scratch_shapes=[
@@ -226,7 +248,9 @@
         compiler_params=pltpu.CompilerParams(vmem_limit_bytes=PICK_VMEM_BYTES),
         name="pick",
     )(features, neighbours_one.T, counts_one[None, :], self_one, neigh_one)
-    got = lax.all_to_all(chunks, ("chip", "core"), 0, 0, tiled=True)
+    got = lax.all_to_all(
+        chunks, ("chip", "core"), 0, 0, tiled=True, axis_index_groups=[feat_order]
+    )
 
     swap = [(0, 1), (1, 0)]
     core = lax.axis_index("core")
@@ -244,12 +268,11 @@
         jnp.concatenate([counts_two, other_meta[-1]]),
         jnp.concatenate([other_meta[-1], counts_two]),
     )
-    hidden_two, grads, bias = pl.pallas_call(
+    hidden_two, parts = pl.pallas_call(
         layers_kernel,
         out_shape=(
             jax.ShapeDtypeStruct((node_rows, hid), jnp.bfloat16),
-            jax.ShapeDtypeStruct((hid, hid), jnp.float32),
-            jax.ShapeDtypeStruct((1, hid), jnp.float32),
+            jax.ShapeDtypeStruct((group, 24, LANES), jnp.float32),
         ),
         in_specs=[pl.BlockSpec(memory_space=pltpu.SMEM)]
         + [pl.BlockSpec(memory_space=pltpu.VMEM)] * 9,
@@ -267,34 +290,31 @@
         cotangent,
         other_cot,
     )
-    group = pairs * chips
-    parts = jnp.concatenate(
-        [
-            grads.reshape(group, -1, 2, LANES),
-            jnp.broadcast_to(bias.reshape(1, 1, 2, LANES), (group, 1, 2, LANES)),
-        ],
-        axis=1,
-    )
-    inner = lax.all_to_all(parts, ("pair", "chip"), 0, 0, tiled=True).sum(axis=0)
+    inner = lax.all_to_all(
+        parts, ("pair", "chip"), 0, 0, tiled=True, axis_index_groups=[part_order]
+    ).sum(axis=0)
+    inner = inner[:18].reshape(9, 2, LANES)
     spread = jnp.broadcast_to(inner[None], (others,) + inner.shape)
-    total = lax.all_to_all(spread, "apart", 0, 0, tiled=True).sum(axis=0)
-    total = total * (1.0 / (batch_nodes * pairs * others))
-    part = total[:-1].reshape(hid // group, hid)
-    everyone = group * cores
+    total = lax.all_to_all(
+        spread, "apart", 0, 0, tiled=True, axis_index_groups=[apart_order]
+    ).sum(axis=0)
+    total = total.reshape(18, LANES) * (1.0 / (batch_nodes * pairs * others))
     spread = pl.pallas_call(
         repeat_kernel,
-        out_shape=jax.ShapeDtypeStruct((everyone,) + part.shape, jnp.bfloat16),
+        out_shape=jax.ShapeDtypeStruct((everyone, hid // group, hid), jnp.bfloat16),
         compiler_params=params,
         name="repeat",
-    )(part)
-    whole = lax.all_to_all(spread, ("pair", "chip", "core"), 0, 0, tiled=True)
+    )(total)
+    whole = lax.all_to_all(
+        spread, ("pair", "chip", "core"), 0, 0, tiled=True, axis_index_groups=[every_order]
+    )
     grad_self, grad_neigh = pl.pallas_call(
         widen_kernel,
         out_shape=(jax.ShapeDtypeStruct((hid, hid), jnp.float32),) * 2,
         compiler_params=params,
         name="widen",
-    )(whole.reshape((pairs, chips, cores) + part.shape))
-    return hidden_two, grad_self, grad_neigh, total[-1].reshape(hid)
+    )(whole.reshape(group, cores, hid // group, hid))
+    return hidden_two, grad_self, grad_neigh, total[16:].reshape(hid)
 
 
 def solution(mesh):

time: 87.7 us -> 83.1 us (0.948)
  starting transfers between devices: 22.6 us -> 30.5 us
  blocking collectives: 37.6 us -> 30.6 us
  waiting for transfers between devices: 13.3 us -> 7.25 us
    all_to_all x2, blocking collectives: 37.6 us -> 30.6 us  [the longest x1 17.2 us: local(): lax.all_to_all(spread, 'apart', 0, 0, tiled=True, axis_index_groups=[apar...]
    ppermute x1, starting transfers between devices: 2.24 us -> 8.77 us  [local(): other_meta = lax.ppermute(meta, 'core', swap)]
    all_to_all x2, waiting for transfers between devices: 13.3 us -> 7.25 us  [the longest x1 3.75 us: local(): lax.all_to_all(chunks, ('chip', 'core'), 0, 0, tiled=True, axis_index_gro...]
    all_to_all x2, starting transfers between devices: 18.3 us -> 19.8 us  [the longest x1 12.3 us: local(): lax.all_to_all(spread, ('pair', 'chip', 'core'), 0, 0, tiled=True, axis_i...]
    unnamed x16 -> x14, local copies, waits for them, and re-layouts: 1.35 us -> 2.04 us
  transfers between devices with their start and end apart: 4 -> 4, of which waited for: 2 -> 2; matrix products, arithmetic and copies ran while one was open for 1% -> 1% of each run, Pallas kernels for 0% -> 8%
where the time goes in v4:
time: 83.1 us; the launch traced here: 82.6 us
  blocking collectives  30.6 us (37%)
  starting transfers between devices  30.5 us (37%)
  Pallas kernels  9.67 us (12%)
  waiting for transfers between devices  7.25 us (9%)
  local copies, waits for them, and re-layouts  2.92 us (4%)
    all_to_all x1, blocking collectives, local(): lax.all_to_all(spread, 'apart', 0, 0, tiled=True, axis_index_groups=[apar...  17.2 us
    all_to_all x1, blocking collectives, local(): lax.all_to_all(parts, ('pair', 'chip'), 0, 0, tiled=True, axis_index_grou...  13.4 us
    all_to_all x1, starting transfers between devices, local(): lax.all_to_all(spread, ('pair', 'chip', 'core'), 0, 0, tiled=True, axis_i...  12.3 us
    ppermute x1, starting transfers between devices, local(): other_meta = lax.ppermute(meta, 'core', swap)  8.77 us
    all_to_all x1, starting transfers between devices, local(): lax.all_to_all(chunks, ('chip', 'core'), 0, 0, tiled=True, axis_index_gro...  7.52 us
    pallas_call x1, Pallas kernels, local(): pl.pallas_call(functools.partial(pick_kernel, feat_order), out_shape=jax....  6.36 us
    all_to_all x1, waiting for transfers between devices, local(): lax.all_to_all(chunks, ('chip', 'core'), 0, 0, tiled=True, axis_index_gro...  3.75 us
    all_to_all x1, waiting for transfers between devices, local(): lax.all_to_all(spread, ('pair', 'chip', 'core'), 0, 0, tiled=True, axis_i...  3.5 us
  transfers between devices with their start and end apart: 4, of which 2 were waited for; matrix products, arithmetic and copies ran while one was open for 1% of the time, Pallas kernels for 8%

profile of v4, /device:TPU:1, one launch (start us, length us, event | category | flops | bytes accessed | tf_op | source)
XLA Modules:
  0.0 82.6 jit_solution(10517174724164039803)
XLA Ops:
  0.6 0.6 copy-done.4
  1.3 0.7 pad_add_fusion
  2.0 8.8 %collective-permute-start = (s32[11,128]{1,0:T(8,128)S(1)}, s32[11,128]{1,0:T(8,128)S(1)}, u32[]{:S(2)}, u32[]{:S(2)}) collective-permute-start(s32[11,128]{1,0:T(8,128)S(1)} %pad_add_fusion), channel_id=1, source_target_pairs={{0,1},{1,0},{2,3},{3,2},{4,5},{5,4},{6,7},{7,6},{8,9},{9,8},{10,11... | collective-permute-start | bytes 16904 | tf_op jit(solution)/shard_map/ppermute | solution.py:259
  10.8 1.9 %collective-permute-start.1 = (bf16[128,256]{1,0:T(8,128)(2,1)}, bf16[128,256]{1,0:T(8,128)(2,1)S(1)}, u32[]{:S(2)}, u32[]{:S(2)}) collective-permute-start(bf16[128,256]{1,0:T(8,128)(2,1)} %own_cot_ref.1), channel_id=1, source_target_pairs={{0,1},{1,0},{2,3},{3,2},{4,5},{5,4},{6,7},{7,6},{8,9},{9,8},{10,11... | collective-permute-start | bytes 196616 | tf_op jit(solution)/shard_map/ppermute | solution.py:260
  12.7 6.4 %pick.1 = bf16[32,8,768]{2,1,0:T(8,128)(2,1)} custom-call(bf16[4,4096]{1,0:T(4,128)(2,1)} %feats_hbm.1, s32[15,4096]{1,0:T(8,128)} %bitcast.20, s32[1,4096]{1,0:T(1,128)} %bitcast.23, bf16[4,256]{1,0:T(4,128)(2,1)} %self_hbm.1, bf16[4,256]{1,0:T(4,128)(2,1)} %neigh_hbm.1), custom_call_target="tpu_custom_call" | custom-call | tf_op jit(solution)/shard_map/pick/pallas_call | solution.py:233
  19.1 7.5 %all-to-all-start = ((bf16[32,8,768]{2,1,0:T(8,128)(2,1)}), bf16[32,8,768]{2,1,0:T(8,128)(2,1)S(1)}, u32[]{:S(2)}, u32[]{:S(2)}) async-start(bf16[32,8,768]{2,1,0:T(8,128)(2,1)} %pick.1), calls=%async_computation | async-start | bytes 786432 | tf_op jit(solution)/shard_map/all_to_all | solution.py:251
  26.6 0.0 copy-start.3
  26.6 0.7 copy-done.3
  27.3 0.7 copy-done.6
  28.0 0.0 copy-done.5
  28.0 0.1 copy.25
  28.2 0.1 copy.24
  28.3 0.0 copy-start
  28.3 0.0 copy-start.1
  28.3 0.0 copy-start.2
  28.4 3.7 %all-to-all-done = bf16[32,8,768]{2,1,0:T(8,128)(2,1)S(1)} async-done(((bf16[32,8,768]{2,1,0:T(8,128)(2,1)}), bf16[32,8,768]{2,1,0:T(8,128)(2,1)S(1)}, u32[]{:S(2)}, u32[]{:S(2)}) %all-to-all-start) | async-done | bytes 393248 | tf_op jit(solution)/shard_map/all_to_all | solution.py:251
  32.2 1.8 %layers.1 = (bf16[128,256]{1,0:T(8,128)(2,1)}, f32[32,24,128]{2,1,0:T(8,128)S(1)}) custom-call(s32[1]{0:T(128)} %bitcast.core_ref, bf16[256,768]{1,0:T(8,128)(2,1)S(1)} %bitcast.18, s32[10,128]{1,0:T(8,128)S(1)} %subtract_select_fusion.own_meta_ref, s32[10,128]{1,0:T(8,128)S(1)} %fusion.other_meta_ref, s32[256,1]{1,0:T(8,128)S(1)} %broadcast_select_fusion.counts_ref, ...), custom_call_target="tpu_custom_call" | custom-call | tf_op jit(solution)/shard_map/layers/pallas_call | solution.py:271
  33.9 13.4 %all_to_all.20 = f32[32,24,128]{2,1,0:T(8,128)S(1)} all-to-all(f32[32,24,128]{2,1,0:T(8,128)S(1)} %get-tuple-element.9), channel_id=1, replica_groups={{52,54,56,58,60,62,0,2,4,6,8,10,12,14,16,18,20,22,24,26,28,30,32,34,36,..., dimensions={0} | all-to-all | bytes 786432 | tf_op jit(solution)/shard_map/all_to_all | solution.py:293
  47.4 17.2 %all_to_all.21 = f32[8,9,2,128]{3,2,1,0:T(2,128)S(1)} all-to-all(f32[8,9,2,128]{3,2,1,0:T(2,128)S(1)} %broadcast_in_dim.29), channel_id=1, replica_groups={{256,320,384,448,0,64,128,192},{257,321,385,449,1,65,129,193},{258,322,..., dimensions={0} | all-to-all | bytes 147456 | tf_op jit(solution)/shard_map/all_to_all | solution.py:298
  64.7 0.7 repeat.1
  65.4 12.3 %all-to-all-start.3 = ((bf16[64,8,256]{2,1,0:T(8,128)(2,1)}), bf16[64,8,256]{2,1,0:T(8,128)(2,1)S(1)}, u32[]{:S(2)}, u32[]{:S(2)}) async-start(bf16[64,8,256]{2,1,0:T(8,128)(2,1)} %repeat.1), calls=%async_computation.3 | async-start | bytes 524288 | tf_op jit(solution)/shard_map/all_to_all | solution.py:308
  77.7 0.6 slice_bitcast_fusion
  78.2 3.5 %all-to-all-done.3 = bf16[64,8,256]{2,1,0:T(8,128)(2,1)S(1)} async-done(((bf16[64,8,256]{2,1,0:T(8,128)(2,1)}), bf16[64,8,256]{2,1,0:T(8,128)(2,1)S(1)}, u32[]{:S(2)}, u32[]{:S(2)}) %all-to-all-start.3) | async-done | bytes 262176 | tf_op jit(solution)/shard_map/all_to_all | solution.py:308
  81.7 0.8 widen.1
  (20 shorter events, 0.2 us)
Async XLA Ops:
  0.6 0.7 copy-start.4
  2.0 26.0 %collective-permute-start = (s32[11,128]{1,0:T(8,128)S(1)}, s32[11,128]{1,0:T(8,128)S(1)}, u32[]{:S(2)}, u32[]{:S(2)}) collective-permute-start(s32[11,128]{1,0:T(8,128)S(1)} %pad_add_fusion), channel_id=1, source_target_pairs={{0,1},{1,0},{2,3},{3,2},{4,5},{5,4},{6,7},{7,6},{8,9},{9,8},{10,11... | collective-permute-start | bytes 16904 | tf_op jit(solution)/shard_map/ppermute | solution.py:259
  10.8 17.6 %collective-permute-start.1 = (bf16[128,256]{1,0:T(8,128)(2,1)}, bf16[128,256]{1,0:T(8,128)(2,1)S(1)}, u32[]{:S(2)}, u32[]{:S(2)}) collective-permute-start(bf16[128,256]{1,0:T(8,128)(2,1)} %own_cot_ref.1), channel_id=1, source_target_pairs={{0,1},{1,0},{2,3},{3,2},{4,5},{5,4},{6,7},{7,6},{8,9},{9,8},{10,11... | collective-permute-start | bytes 196616 | tf_op jit(solution)/shard_map/ppermute | solution.py:260
  19.1 13.1 %all-to-all-start = ((bf16[32,8,768]{2,1,0:T(8,128)(2,1)}), bf16[32,8,768]{2,1,0:T(8,128)(2,1)S(1)}, u32[]{:S(2)}, u32[]{:S(2)}) async-start(bf16[32,8,768]{2,1,0:T(8,128)(2,1)} %pick.1), calls=%async_computation | async-start | bytes 786432 | tf_op jit(solution)/shard_map/all_to_all | solution.py:251
  26.6 0.7 copy-start.3
  27.3 0.7 copy-start.6
  27.3 0.7 copy-start.5
  28.3 3.8 %copy-start = (bf16[256,256]{1,0:T(8,128)(2,1)S(1)}, bf16[256,256]{1,0:T(8,128)(2,1)}, u32[]{:S(2)}) copy-start(bf16[256,256]{1,0:T(8,128)(2,1)} %self_ref.1) | copy-start | bytes 393220
  28.3 3.8 %copy-start.1 = (bf16[256,256]{1,0:T(8,128)(2,1)S(1)}, bf16[256,256]{1,0:T(8,128)(2,1)}, u32[]{:S(2)}) copy-start(bf16[256,256]{1,0:T(8,128)(2,1)} %neigh_ref.1) | copy-start | bytes 393220
  28.3 3.8 %copy-start.2 = (bf16[128,256]{1,0:T(8,128)(2,1)S(1)}, bf16[128,256]{1,0:T(8,128)(2,1)}, u32[]{:S(2)}) copy-start(bf16[128,256]{1,0:T(8,128)(2,1)} %own_cot_ref.1) | copy-start | bytes 196612
  65.4 16.3 %all-to-all-start.3 = ((bf16[64,8,256]{2,1,0:T(8,128)(2,1)}), bf16[64,8,256]{2,1,0:T(8,128)(2,1)S(1)}, u32[]{:S(2)}, u32[]{:S(2)}) async-start(bf16[64,8,256]{2,1,0:T(8,128)(2,1)} %repeat.1), calls=%async_computation.3 | async-start | bytes 524288 | tf_op jit(solution)/shard_map/all_to_all | solution.py:308

commit v5 on v4

--- a/solution.py
+++ b/solution.py
@@ -32,7 +32,7 @@
 
 
 def pick_kernel(
-    order, feats_hbm, ids_hbm, counts_hbm, self_hbm, neigh_hbm, out_ref,
+    order, feats_hbm, ids_hbm, counts_hbm, self_hbm, neigh_hbm, out_ref, zeros_ref,
     feats_ref, ids_ref, counts_ref, self_ref, neigh_ref, wide, table, sums, arrived,
 ):
     copies = [
@@ -49,6 +49,7 @@
     ]
     for copy in copies:
         copy.start()
+    zeros_ref[...] = jnp.zeros_like(zeros_ref)
     rows, nodes = feats_ref.shape
     fan = ids_ref.shape[0]
     blocks = nodes // LANES
@@ -171,16 +172,13 @@
     rows = jnp.where(is_first, own, agg)
     grads = lax.dot_general(rows, delta, over_rows, preferred_element_type=jnp.float32)
     bias = jnp.sum(delta.astype(jnp.float32), axis=0, keepdims=True)
-    row = lax.broadcasted_iota(jnp.int32, (8, LANES), 0)
-    halves = jnp.where(
-        row == 0,
-        jnp.broadcast_to(bias[:, :LANES], row.shape),
-        jnp.where(row == 1, jnp.broadcast_to(bias[:, LANES:], row.shape), 0.0),
-    )
-    for part in range(parts_ref.shape[0]):
-        parts_ref[part, 0:8, :] = grads[part * 8 : part * 8 + 8, :LANES]
-        parts_ref[part, 8:16, :] = grads[part * 8 : part * 8 + 8, LANES:]
-        parts_ref[part, 16:24, :] = halves
+    for half in range(2):
+        columns = slice(half * LANES, (half + 1) * LANES)
+        for part in range(parts_ref.shape[0]):
+            parts_ref[part, 4 * half : 4 * half + 4] = grads[
+                part * 8 : part * 8 + 8, columns
+            ].reshape(4, 2, LANES)
+            parts_ref[part, 8, half : half + 1, :] = bias[:, columns]
 
 
 def repeat_kernel(part_ref, out_ref):
@@ -230,9 +228,12 @@
     part_order = from_member(first_part, group)
     every_order = from_member(first_part * cores, everyone)
     apart_order = from_member(others // 2, others)
-    chunks = pl.pallas_call(
+    chunks, zeros = pl.pallas_call(
         functools.partial(pick_kernel, feat_order),
-        out_shape=jax.ShapeDtypeStruct((groups, 2 * rows, span + hid), jnp.bfloat16),
+        out_shape=(
+            jax.ShapeDtypeStruct((groups, 2 * rows, span + hid), jnp.bfloat16),
+            jax.ShapeDtypeStruct((1, hid), jnp.int32),
+        ),
         in_specs=[pl.BlockSpec(memory_space=pltpu.HBM)] * 5,
         scratch_shapes=[
             pltpu.VMEM(features.shape, features.dtype),
@@ -256,8 +257,9 @@
     core = lax.axis_index("core")
     first_node = (lax.axis_index("chip") * cores - 1) * node_rows
     meta = jnp.concatenate([neighbours_two.T, counts_two[None, :]], axis=0)
+    meta = meta + zeros[:, : meta.shape[1]]
     other_meta = lax.ppermute(meta, "core", swap)
-    other_cot = lax.ppermute(cotangent, "core", swap)
+    other_cot = lax.ppermute(jnp.where(zeros == 0, cotangent, 0), "core", swap)
 
     def numbers(kept):
         live = jnp.arange(kept.shape[0] - 1, dtype=jnp.int32)[:, None] < kept[-1:]
@@ -272,7 +274,7 @@
         layers_kernel,
         out_shape=(
             jax.ShapeDtypeStruct((node_rows, hid), jnp.bfloat16),
-            jax.ShapeDtypeStruct((group, 24, LANES), jnp.float32),
+            jax.ShapeDtypeStruct((group, 9, 2, LANES), jnp.float32),
         ),
         in_specs=[pl.BlockSpec(memory_space=pltpu.SMEM)]
         + [pl.BlockSpec(memory_space=pltpu.VMEM)] * 9,
@@ -293,7 +295,6 @@
     inner = lax.all_to_all(
         parts, ("pair", "chip"), 0, 0, tiled=True, axis_index_groups=[part_order]
     ).sum(axis=0)
-    inner = inner[:18].reshape(9, 2, LANES)
     spread = jnp.broadcast_to(inner[None], (others,) + inner.shape)
     total = lax.all_to_all(
         spread, "apart", 0, 0, tiled=True, axis_index_groups=[apart_order]

time: 83.1 us -> 77.9 us (0.937)
  waiting for transfers between devices: 7.25 us -> 3.51 us
  blocking collectives: 30.6 us -> 28.4 us
  local copies, waits for them, and re-layouts: 2.92 us -> 3.79 us
    all_to_all x1, starting transfers between devices: 7.52 us -> 14 us  [local(): lax.all_to_all(chunks, ('chip', 'core'), 0, 0, tiled=True, axis_index_gro...]
    ppermute x1, starting transfers between devices: 8.77 us -> 2.26 us  [local(): other_meta = lax.ppermute(meta, 'core', swap)]
    all_to_all x1, waiting for transfers between devices: 3.75 us -> 0.01 us  [local(): lax.all_to_all(chunks, ('chip', 'core'), 0, 0, tiled=True, axis_index_gro...]
    all_to_all x1, blocking collectives: 13.4 us -> 11.2 us  [local(): lax.all_to_all(parts, ('pair', 'chip'), 0, 0, tiled=True, axis_index_grou...]
    unnamed x14 -> x16, local copies, waits for them, and re-layouts: 2.04 us -> 2.91 us
  transfers between devices with their start and end apart: 4 -> 4, of which waited for: 2 -> 1; matrix products, arithmetic and copies ran while one was open for 1% -> 1% of each run, Pallas kernels for 8% -> 0%
where the time goes in v5:
time: 77.9 us; the launch traced here: 77.4 us
  starting transfers between devices  30.9 us (40%)
  blocking collectives  28.4 us (36%)
  Pallas kernels  9.67 us (12%)
  local copies, waits for them, and re-layouts  3.79 us (5%)
  waiting for transfers between devices  3.51 us (5%)
  between operations  0.85 us (1%)
    all_to_all x1, blocking collectives, local(): lax.all_to_all(spread, 'apart', 0, 0, tiled=True, axis_index_groups=[apar...  17.2 us
    all_to_all x1, starting transfers between devices, local(): lax.all_to_all(chunks, ('chip', 'core'), 0, 0, tiled=True, axis_index_gro...  14 us
    all_to_all x1, starting transfers between devices, local(): lax.all_to_all(spread, ('pair', 'chip', 'core'), 0, 0, tiled=True, axis_i...  12.6 us
    all_to_all x1, blocking collectives, local(): lax.all_to_all(parts, ('pair', 'chip'), 0, 0, tiled=True, axis_index_grou...  11.2 us
    pallas_call x1, Pallas kernels, local(): pl.pallas_call(functools.partial(pick_kernel, feat_order), out_shape=(jax...  6.37 us
    all_to_all x1, waiting for transfers between devices, local(): lax.all_to_all(spread, ('pair', 'chip', 'core'), 0, 0, tiled=True, axis_i...  3.5 us
    unnamed x16, local copies, waits for them, and re-layouts  2.91 us
    ppermute x1, starting transfers between devices, local(): other_meta = lax.ppermute(meta, 'core', swap)  2.26 us
  transfers between devices with their start and end apart: 4, of which 1 were waited for; matrix products, arithmetic and copies ran while one was open for 1% of the time, Pallas kernels for 0%

profile of v5, /device:TPU:1, one launch (start us, length us, event | category | flops | bytes accessed | tf_op | source)
XLA Modules:
  0.0 77.4 jit_solution(1433521842076567553)
XLA Ops:
  0.6 6.4 %pick.1 = (bf16[32,8,768]{2,1,0:T(8,128)(2,1)}, s32[1,256]{1,0:T(1,128)}) custom-call(bf16[4,4096]{1,0:T(4,128)(2,1)} %feats_hbm.1, s32[15,4096]{1,0:T(8,128)} %bitcast.22, s32[1,4096]{1,0:T(1,128)} %bitcast.23, bf16[4,256]{1,0:T(4,128)(2,1)} %self_hbm.1, bf16[4,256]{1,0:T(4,128)(2,1)} %neigh_hbm.1), custom_call_target="tpu_custom_call" | custom-call | tf_op jit(solution)/shard_map/pick/pallas_call | solution.py:231
  7.0 0.0 copy-start.3
  7.0 0.0 copy-start
  7.0 14.0 %all-to-all-start = ((bf16[32,8,768]{2,1,0:T(8,128)(2,1)}), bf16[32,8,768]{2,1,0:T(8,128)(2,1)S(1)}, u32[]{:S(2)}, u32[]{:S(2)}) async-start(bf16[32,8,768]{2,1,0:T(8,128)(2,1)} %get-tuple-element.10), calls=%async_computation | async-start | bytes 786432 | tf_op jit(solution)/shard_map/all_to_all | solution.py:252
  21.1 0.0 copy-start.7
  21.1 0.7 copy-done.7
  21.8 0.7 copy-done.4
  22.4 2.3 %collective-permute-start = (s32[11,128]{1,0:T(8,128)S(1)}, s32[11,128]{1,0:T(8,128)S(1)}, u32[]{:S(2)}, u32[]{:S(2)}) collective-permute-start(s32[11,128]{1,0:T(8,128)S(1)} %add_add_fusion), channel_id=1, source_target_pairs={{0,1},{1,0},{2,3},{3,2},{4,5},{5,4},{6,7},{7,6},{8,9},{9,8},{10,11... | collective-permute-start | bytes 16904 | tf_op jit(solution)/shard_map/ppermute | solution.py:261
  24.7 2.1 %collective-permute-start.1 = (bf16[128,256]{1,0:T(8,128)(2,1)S(1)}, bf16[128,256]{1,0:T(8,128)(2,1)S(1)}, u32[]{:S(2)}, u32[]{:S(2)}) collective-permute-start(bf16[128,256]{1,0:T(8,128)(2,1)S(1)} %broadcast_select_fusion), channel_id=1, source_target_pairs={{0,1},{1,0},{2,3},{3,2},{4,5},{5,4},{6,7},{7,6},{8,9},{9,8},{10,11... | collective-permute-start | bytes 196616 | tf_op jit(solution)/shard_map/ppermute | solution.py:262
  26.9 0.6 copy-done.6
  27.5 0.0 copy-done.5
  27.6 0.1 copy.25
  27.7 0.1 copy.24
  28.0 0.8 %copy-done.1 = bf16[256,256]{1,0:T(8,128)(2,1)S(1)} copy-done((bf16[256,256]{1,0:T(8,128)(2,1)S(1)}, bf16[256,256]{1,0:T(8,128)(2,1)}, u32[]{:S(2)}) %copy-start.1) | copy-done | bytes 131096
  28.8 0.1 copy-done.2
  28.8 1.7 %layers.1 = (bf16[128,256]{1,0:T(8,128)(2,1)}, f32[32,9,2,128]{3,2,1,0:T(2,128)S(1)}) custom-call(s32[1]{0:T(128)} %bitcast.core_ref, bf16[256,768]{1,0:T(8,128)(2,1)S(1)} %bitcast.20, s32[10,128]{1,0:T(8,128)S(1)} %fusion.1.own_meta_ref, s32[10,128]{1,0:T(8,128)S(1)} %fusion.other_meta_ref, s32[256,1]{1,0:T(8,128)S(1)} %broadcast_select_fusion.1.counts_ref, ...), custom_call_target="tpu_custom_call" | custom-call | tf_op jit(solution)/shard_map/layers/pallas_call | solution.py:273
  30.6 11.2 %all_to_all.20 = f32[32,9,2,128]{3,2,1,0:T(2,128)S(1)} all-to-all(f32[32,9,2,128]{3,2,1,0:T(2,128)S(1)} %get-tuple-element.13), channel_id=1, replica_groups={{52,54,56,58,60,62,0,2,4,6,8,10,12,14,16,18,20,22,24,26,28,30,32,34,36,..., dimensions={0} | all-to-all | bytes 589824 | tf_op jit(solution)/shard_map/all_to_all | solution.py:295
  41.8 0.1 reduce_sum.18
  41.9 17.2 %all_to_all.21 = f32[8,9,2,128]{3,2,1,0:T(2,128)S(1)} all-to-all(f32[8,9,2,128]{3,2,1,0:T(2,128)S(1)} %broadcast_in_dim.44), channel_id=1, replica_groups={{256,320,384,448,0,64,128,192},{257,321,385,449,1,65,129,193},{258,322,..., dimensions={0} | all-to-all | bytes 147456 | tf_op jit(solution)/shard_map/all_to_all | solution.py:299
  59.2 0.7 repeat.1
  59.9 12.6 %all-to-all-start.3 = ((bf16[64,8,256]{2,1,0:T(8,128)(2,1)}), bf16[64,8,256]{2,1,0:T(8,128)(2,1)S(1)}, u32[]{:S(2)}, u32[]{:S(2)}) async-start(bf16[64,8,256]{2,1,0:T(8,128)(2,1)} %repeat.1), calls=%async_computation.3 | async-start | bytes 524288 | tf_op jit(solution)/shard_map/all_to_all | solution.py:309
  72.5 0.6 slice_bitcast_fusion
  73.1 3.5 %all-to-all-done.3 = bf16[64,8,256]{2,1,0:T(8,128)(2,1)S(1)} async-done(((bf16[64,8,256]{2,1,0:T(8,128)(2,1)}), bf16[64,8,256]{2,1,0:T(8,128)(2,1)S(1)}, u32[]{:S(2)}, u32[]{:S(2)}) %all-to-all-start.3) | async-done | bytes 262176 | tf_op jit(solution)/shard_map/all_to_all | solution.py:309
  76.6 0.8 %widen.1 = (f32[256,256]{1,0:T(8,128)}, f32[256,256]{1,0:T(8,128)}) custom-call(bf16[32,2,8,256]{3,2,1,0:T(8,128)(2,1)S(1)} %bitcast.21), custom_call_target="tpu_custom_call" | custom-call | tf_op jit(solution)/shard_map/widen/pallas_call | solution.py:312
  (25 shorter events, 0.2 us)
Async XLA Ops:
  7.0 14.8 %copy-start.3 = (s32[128,10]{0,1:T(8,128)S(1)}, s32[128,10]{0,1:T(8,128)}, u32[]{:S(2)}) copy-start(s32[128,10]{0,1:T(8,128)} %param.15) | copy-start | bytes 15364
  7.0 17.7 %copy-start = (bf16[128,256]{1,0:T(8,128)(2,1)S(1)}, bf16[128,256]{1,0:T(8,128)(2,1)}, u32[]{:S(2)}) copy-start(bf16[128,256]{1,0:T(8,128)(2,1)} %own_cot_ref.1) | copy-start | bytes 196612
  7.0 20.9 %all-to-all-start = ((bf16[32,8,768]{2,1,0:T(8,128)(2,1)}), bf16[32,8,768]{2,1,0:T(8,128)(2,1)S(1)}, u32[]{:S(2)}, u32[]{:S(2)}) async-start(bf16[32,8,768]{2,1,0:T(8,128)(2,1)} %get-tuple-element.10), calls=%async_computation | async-start | bytes 786432 | tf_op jit(solution)/shard_map/all_to_all | solution.py:252
  21.1 0.7 copy-start.7
  21.8 0.7 copy-start.4
  22.4 5.1 %collective-permute-start = (s32[11,128]{1,0:T(8,128)S(1)}, s32[11,128]{1,0:T(8,128)S(1)}, u32[]{:S(2)}, u32[]{:S(2)}) collective-permute-start(s32[11,128]{1,0:T(8,128)S(1)} %add_add_fusion), channel_id=1, source_target_pairs={{0,1},{1,0},{2,3},{3,2},{4,5},{5,4},{6,7},{7,6},{8,9},{9,8},{10,11... | collective-permute-start | bytes 16904 | tf_op jit(solution)/shard_map/ppermute | solution.py:261
  24.7 3.2 %collective-permute-start.1 = (bf16[128,256]{1,0:T(8,128)(2,1)S(1)}, bf16[128,256]{1,0:T(8,128)(2,1)S(1)}, u32[]{:S(2)}, u32[]{:S(2)}) collective-permute-start(bf16[128,256]{1,0:T(8,128)(2,1)S(1)} %broadcast_select_fusion), channel_id=1, source_target_pairs={{0,1},{1,0},{2,3},{3,2},{4,5},{5,4},{6,7},{7,6},{8,9},{9,8},{10,11... | collective-permute-start | bytes 196616 | tf_op jit(solution)/shard_map/ppermute | solution.py:262
  26.8 0.7 copy-start.6
  26.9 0.7 copy-start.5
  27.9 0.9 %copy-start.1 = (bf16[256,256]{1,0:T(8,128)(2,1)S(1)}, bf16[256,256]{1,0:T(8,128)(2,1)}, u32[]{:S(2)}) copy-start(bf16[256,256]{1,0:T(8,128)(2,1)} %self_ref.1) | copy-start | bytes 393220
  27.9 1.0 %copy-start.2 = (bf16[256,256]{1,0:T(8,128)(2,1)S(1)}, bf16[256,256]{1,0:T(8,128)(2,1)}, u32[]{:S(2)}) copy-start(bf16[256,256]{1,0:T(8,128)(2,1)} %neigh_ref.1) | copy-start | bytes 393220
  59.9 16.7 %all-to-all-start.3 = ((bf16[64,8,256]{2,1,0:T(8,128)(2,1)}), bf16[64,8,256]{2,1,0:T(8,128)(2,1)S(1)}, u32[]{:S(2)}, u32[]{:S(2)}) async-start(bf16[64,8,256]{2,1,0:T(8,128)(2,1)} %repeat.1), calls=%async_computation.3 | async-start | bytes 524288 | tf_op jit(solution)/shard_map/all_to_all | solution.py:309

commit v6 on v5

--- a/solution.py
+++ b/solution.py
@@ -10,6 +10,7 @@
 from jax.sharding import PartitionSpec as P
 
 LANES = 128
+DEAD = -64
 INNER = math.sqrt(2.0 / math.pi)
 CUBIC = 0.044715
 VMEM_BYTES = 48 * 1024 * 1024
@@ -32,8 +33,10 @@
 
 
 def pick_kernel(
-    order, feats_hbm, ids_hbm, counts_hbm, self_hbm, neigh_hbm, out_ref, zeros_ref,
-    feats_ref, ids_ref, counts_ref, self_ref, neigh_ref, wide, table, sums, arrived,
+    order, feats_hbm, ids_hbm, counts_hbm, self_hbm, neigh_hbm, ids_two_hbm, counts_two_hbm,
+    cot_hbm, bias_one_hbm, bias_two_hbm, out_ref, send_ref, biases_ref,
+    feats_ref, ids_ref, counts_ref, self_ref, neigh_ref, ids_two_ref, counts_two_ref, cot_ref,
+    bias_one_ref, bias_two_ref, wide, table, sums, lists, arrived,
 ):
     copies = [
         pltpu.make_async_copy(source, target, arrived.at[i])
@@ -44,12 +47,16 @@
                 (counts_hbm, counts_ref),
                 (self_hbm, self_ref),
                 (neigh_hbm, neigh_ref),
+                (ids_two_hbm, ids_two_ref),
+                (counts_two_hbm, counts_two_ref),
+                (cot_hbm, cot_ref),
+                (bias_one_hbm, bias_one_ref),
+                (bias_two_hbm, bias_two_ref),
             )
         )
     ]
     for copy in copies:
         copy.start()
-    zeros_ref[...] = jnp.zeros_like(zeros_ref)
     rows, nodes = feats_ref.shape
     fan = ids_ref.shape[0]
     blocks = nodes // LANES
@@ -108,6 +115,20 @@
     lax.fori_loop(0, blocks // 4, four_blocks, 0, unroll=True)
     sums[:, 0:LANES] = sums[:, blocks * LANES : (blocks + 1) * LANES]
     sums[:, (blocks + 1) * LANES :] = sums[:, LANES : 2 * LANES]
+    node_rows = cot_ref.shape[0]
+    fan_two = ids_two_ref.shape[0]
+    lists[...] = jnp.zeros_like(lists)
+    lists[0:fan_two, :] = ids_two_ref[...]
+    row = lax.broadcasted_iota(jnp.int32, lists.shape, 0)
+    counts_two = jnp.broadcast_to(counts_two_ref[...], lists.shape)
+    place = jnp.bitwise_and(lists[...], LANES - 1)
+    block = jnp.where(row < counts_two, lax.shift_right_logical(lists[...], 7), DEAD)
+    place = jnp.where(row == fan_two, counts_two, place)
+    send_ref[0:node_rows, :] = cot_ref[...]
+    send_ref[node_rows:, 0:LANES] = place.astype(jnp.float32).astype(jnp.bfloat16)
+    send_ref[node_rows:, LANES:] = block.astype(jnp.float32).astype(jnp.bfloat16)
+    biases_ref[0:1, :] = bias_one_ref[...]
+    biases_ref[1:2, :] = bias_two_ref[...]
     weights = jnp.concatenate(
         [self_ref[...].astype(jnp.float32), neigh_ref[...].astype(jnp.float32)], axis=0
     ).astype(jnp.bfloat16)
@@ -128,45 +149,58 @@
 
 
 def layers_kernel(
-    core_ref, got_ref, own_meta_ref, other_meta_ref, counts_ref, bias_ref, self_ref, neigh_ref,
-    own_cot_ref, other_cot_ref, hidden_ref, parts_ref,
+    fan, place_ref, got_ref, own_ref, other_ref, bias_ref, self_ref, neigh_ref, hidden_ref, parts_ref,
 ):
-    node_rows, hid = own_cot_ref.shape
+    node_rows, hid = hidden_ref.shape
     span = 4 * node_rows
-    fan = own_meta_ref.shape[0]
     over_rows = (((0,), (0,)), ((), ()))
-    is_first = core_ref[0] == 0
+    is_first, first_block = place_ref[0] == 0, place_ref[1]
     got = got_ref[...]
     pre_one = lax.dot_general(
         got[:, :span], got[:, span:], over_rows, preferred_element_type=jnp.float32
     )
     hidden = gelu_parts(pre_one + bias_ref[0:1, :])[0].astype(jnp.bfloat16)
     own = hidden[node_rows : 3 * node_rows]
-    own_meta, other_meta = own_meta_ref[...], other_meta_ref[...]
+
+    def lists_of(ref):
+        kept = ref[node_rows:, :].astype(jnp.float32)
+        place = kept[:, :LANES]
+        numbers = (kept[:, LANES:].astype(jnp.int32) - first_block) * LANES + place.astype(jnp.int32)
+        return numbers, place
+
+    def in_order(own, other):
+        return jnp.where(is_first, own, other), jnp.where(is_first, other, own)
+
+    own_lists, other_lists = lists_of(own_ref), lists_of(other_ref)
     number = lax.broadcasted_iota(jnp.int32, (span, node_rows), 0).astype(jnp.int16)
     one, zero = jnp.ones((), jnp.bfloat16), jnp.zeros((), jnp.bfloat16)
     often = []
-    for meta in (
-        jnp.where(is_first, own_meta, other_meta),
-        jnp.where(is_first, other_meta, own_meta),
-    ):
+    for numbers in in_order(own_lists[0], other_lists[0]):
         total = jnp.zeros((span, node_rows), jnp.bfloat16)
         for k in range(fan):
-            ids = jnp.broadcast_to(meta[k : k + 1, :], (span, node_rows)).astype(jnp.int16)
+            ids = jnp.broadcast_to(numbers[k : k + 1, :], (span, node_rows)).astype(jnp.int16)
             total = total + jnp.where(ids == number, one, zero)
         often.append(total)
+    counts = jnp.concatenate(
+        [
+            jnp.broadcast_to(places[fan : fan + 1, :], (LANES, LANES)).T
+            for places in in_order(own_lists[1], other_lists[1])
+        ],
+        axis=0,
+    )
     summed = lax.dot_general(
         jnp.concatenate(often, axis=1), hidden, over_rows, preferred_element_type=jnp.float32
     )
-    agg = (summed / counts_ref[...].astype(jnp.float32)).astype(jnp.bfloat16)
+    agg = (summed / jnp.concatenate([counts] * (hid // LANES), axis=1)).astype(jnp.bfloat16)
     pre_two = jnp.dot(own, self_ref[...], preferred_element_type=jnp.float32)
     pre_two = pre_two + jnp.dot(agg, neigh_ref[...], preferred_element_type=jnp.float32)
     value, slope = gelu_parts(pre_two + bias_ref[1:2, :])
     hidden_ref[...] = jnp.where(is_first, value[:node_rows], value[node_rows:]).astype(jnp.bfloat16)
-    own_cot = own_cot_ref[...].astype(jnp.float32)
-    other_cot = other_cot_ref[...].astype(jnp.float32)
     cot = jnp.concatenate(
-        [jnp.where(is_first, own_cot, other_cot), jnp.where(is_first, other_cot, own_cot)], axis=0
+        in_order(
+            own_ref[0:node_rows, :].astype(jnp.float32), other_ref[0:node_rows, :].astype(jnp.float32)
+        ),
+        axis=0,
     )
     delta = (cot * slope).astype(jnp.bfloat16)
     rows = jnp.where(is_first, own, agg)
@@ -228,70 +262,46 @@
     part_order = from_member(first_part, group)
     every_order = from_member(first_part * cores, everyone)
     apart_order = from_member(others // 2, others)
-    chunks, zeros = pl.pallas_call(
+    lists = (16, node_rows)
+    loads = (
+        features, neighbours_one.T, counts_one[None, :], self_one, neigh_one, neighbours_two.T,
+        counts_two[None, :], cotangent, bias_one[None, :], bias_two[None, :],
+    )
+    chunks, send, biases = pl.pallas_call(
         functools.partial(pick_kernel, feat_order),
         out_shape=(
             jax.ShapeDtypeStruct((groups, 2 * rows, span + hid), jnp.bfloat16),
-            jax.ShapeDtypeStruct((1, hid), jnp.int32),
+            jax.ShapeDtypeStruct((node_rows + lists[0], hid), jnp.bfloat16),
+            jax.ShapeDtypeStruct((2, hid), jnp.float32),
         ),
-        in_specs=[pl.BlockSpec(memory_space=pltpu.HBM)] * 5,
-        scratch_shapes=[
-            pltpu.VMEM(features.shape, features.dtype),
-            pltpu.VMEM(neighbours_one.shape[::-1], jnp.int32),
-            pltpu.VMEM((1, batch_nodes), jnp.int32),
-            pltpu.VMEM(self_one.shape, self_one.dtype),
-            pltpu.VMEM(neigh_one.shape, neigh_one.dtype),
+        in_specs=[pl.BlockSpec(memory_space=pltpu.HBM)] * len(loads),
+        scratch_shapes=[pltpu.VMEM(load.shape, load.dtype) for load in loads]
+        + [
             pltpu.VMEM((2 * rows, batch_nodes), jnp.float32),
             pltpu.VMEM((4 * rows, batch_nodes), jnp.bfloat16),
             pltpu.VMEM((2 * rows, batch_nodes + 2 * node_rows), jnp.float32),
-            pltpu.SemaphoreType.DMA((5,)),
+            pltpu.VMEM(lists, jnp.int32),
+            pltpu.SemaphoreType.DMA((len(loads),)),
         ],
         compiler_params=pltpu.CompilerParams(vmem_limit_bytes=PICK_VMEM_BYTES),
         name="pick",
-    )(features, neighbours_one.T, counts_one[None, :], self_one, neigh_one)
+    )(*loads)
     got = lax.all_to_all(
         chunks, ("chip", "core"), 0, 0, tiled=True, axis_index_groups=[feat_order]
     )
-
-    swap = [(0, 1), (1, 0)]
-    core = lax.axis_index("core")
-    first_node = (lax.axis_index("chip") * cores - 1) * node_rows
-    meta = jnp.concatenate([neighbours_two.T, counts_two[None, :]], axis=0)
-    meta = meta + zeros[:, : meta.shape[1]]
-    other_meta = lax.ppermute(meta, "core", swap)
-    other_cot = lax.ppermute(jnp.where(zeros == 0, cotangent, 0), "core", swap)
-
-    def numbers(kept):
-        live = jnp.arange(kept.shape[0] - 1, dtype=jnp.int32)[:, None] < kept[-1:]
-        return jnp.where(live, kept[:-1] - first_node, -1)
-
-    counts = jnp.where(
-        core == 0,
-        jnp.concatenate([counts_two, other_meta[-1]]),
-        jnp.concatenate([other_meta[-1], counts_two]),
-    )
+    other = lax.ppermute(send, "core", [(0, 1), (1, 0)])
+    place = jnp.stack([lax.axis_index("core"), lax.axis_index("chip") * cores - 1])
     hidden_two, parts = pl.pallas_call(
-        layers_kernel,
+        functools.partial(layers_kernel, neighbours_two.shape[1]),
         out_shape=(
             jax.ShapeDtypeStruct((node_rows, hid), jnp.bfloat16),
             jax.ShapeDtypeStruct((group, 9, 2, LANES), jnp.float32),
         ),
         in_specs=[pl.BlockSpec(memory_space=pltpu.SMEM)]
-        + [pl.BlockSpec(memory_space=pltpu.VMEM)] * 9,
+        + [pl.BlockSpec(memory_space=pltpu.VMEM)] * 6,
         compiler_params=params,
         name="layers",
-    )(
-        core[None],
-        got.reshape(groups * 2 * rows, span + hid),
-        numbers(meta),
-        numbers(other_meta),
-        counts[:, None],
-        jnp.stack([bias_one, bias_two]),
-        self_two,
-        neigh_two,
-        cotangent,
-        other_cot,
-    )
+    )(place, got.reshape(groups * 2 * rows, span + hid), send, other, biases, self_two, neigh_two)
     inner = lax.all_to_all(
         parts, ("pair", "chip"), 0, 0, tiled=True, axis_index_groups=[part_order]
     ).sum(axis=0)

time: 77.9 us -> 77.1 us (0.990)
  waiting for transfers between devices: 3.51 us -> 6.69 us
  local copies, waits for them, and re-layouts: 3.79 us -> 0.62 us
  starting transfers between devices: 30.9 us -> 28.6 us
  blocking collectives: 28.4 us -> 29.5 us
    unnamed x16 -> x8, local copies, waits for them, and re-layouts: 2.91 us -> 0.02 us
    all_to_all x1, waiting for transfers between devices: 0.01 us -> 2.38 us  [local(): lax.all_to_all(chunks, ('chip', 'core'), 0, 0, tiled=True, axis_index_gro...]
    ppermute x2 -> x1, starting transfers between devices: 4.32 us -> 2.27 us  [local(): other = lax.ppermute(send, 'core', [(0, 1), (1, 0)])]
    all_to_all x1, blocking collectives: 11.2 us -> 12.3 us  [local(): lax.all_to_all(parts, ('pair', 'chip'), 0, 0, tiled=True, axis_index_grou...]
    ppermute x2 -> x1, waiting for transfers between devices: 0.01 us -> 0.81 us  [local(): other = lax.ppermute(send, 'core', [(0, 1), (1, 0)])]
  transfers between devices with their start and end apart: 4 -> 3, of which waited for: 1 -> 3; matrix products, arithmetic and copies ran while one was open for 1% -> 1% of each run, Pallas kernels for 0% -> 0%
where the time goes in v6:
time: 77.1 us; the launch traced here: 76.7 us
  blocking collectives  29.5 us (38%)
  starting transfers between devices  28.6 us (37%)
  Pallas kernels  10.3 us (13%)
  waiting for transfers between devices  6.69 us (9%)
    all_to_all x1, blocking collectives, local(): lax.all_to_all(spread, 'apart', 0, 0, tiled=True, axis_index_groups=[apar...  17.3 us
    all_to_all x1, starting transfers between devices, local(): lax.all_to_all(chunks, ('chip', 'core'), 0, 0, tiled=True, axis_index_gro...  14 us
    all_to_all x1, starting transfers between devices, local(): lax.all_to_all(spread, ('pair', 'chip', 'core'), 0, 0, tiled=True, axis_i...  12.3 us
    all_to_all x1, blocking collectives, local(): lax.all_to_all(parts, ('pair', 'chip'), 0, 0, tiled=True, axis_index_grou...  12.3 us
    pallas_call x1, Pallas kernels, local(): pl.pallas_call(functools.partial(pick_kernel, feat_order), out_shape=(jax...  6.47 us
    all_to_all x1, waiting for transfers between devices, local(): lax.all_to_all(spread, ('pair', 'chip', 'core'), 0, 0, tiled=True, axis_i...  3.5 us
    all_to_all x1, waiting for transfers between devices, local(): lax.all_to_all(chunks, ('chip', 'core'), 0, 0, tiled=True, axis_index_gro...  2.38 us
    pallas_call x1, Pallas kernels, local(): pl.pallas_call(functools.partial(layers_kernel, neighbours_two.shape[1]),...  2.3 us
  transfers between devices with their start and end apart: 3, of which 3 were waited for; matrix products, arithmetic and copies ran while one was open for 1% of the time, Pallas kernels for 0%

profile of v6, /device:TPU:1, one launch (start us, length us, event | category | flops | bytes accessed | tf_op | source)
XLA Modules:
  0.0 76.7 jit_solution(1877800029764831475)
XLA Ops:
  0.6 6.5 %pick.1 = (bf16[32,8,768]{2,1,0:T(8,128)(2,1)}, bf16[144,256]{1,0:T(8,128)(2,1)}, f32[2,256]{1,0:T(2,128)}) custom-call(bf16[4,4096]{1,0:T(4,128)(2,1)} %feats_hbm.1, s32[15,4096]{1,0:T(8,128)} %bitcast.14, s32[1,4096]{1,0:T(1,128)} %bitcast.15, bf16[4,256]{1,0:T(4,128)(2,1)} %self_hbm.1, bf16[4,256]{1,0:T(4,128)(2,1)} %neigh_hbm.1, s32[10,128]{1,0:T(8,128)} %bitcast.16, ...), custom_call_target="tpu_custom_call" | custom-call | tf_op jit(solution)/shard_map/pick/pallas_call | solution.py:270
  7.1 0.0 copy-start.2
  7.1 0.0 copy-start
  7.1 0.0 copy-start.1
  7.1 14.0 %all-to-all-start = ((bf16[32,8,768]{2,1,0:T(8,128)(2,1)}), bf16[32,8,768]{2,1,0:T(8,128)(2,1)S(1)}, u32[]{:S(2)}, u32[]{:S(2)}) async-start(bf16[32,8,768]{2,1,0:T(8,128)(2,1)} %get-tuple-element.11), calls=%async_computation | async-start | bytes 786432 | tf_op jit(solution)/shard_map/all_to_all | solution.py:289
  21.2 0.0 copy-done.2
  21.2 2.3 %collective-permute-start = (bf16[144,256]{1,0:T(8,128)(2,1)S(1)}, bf16[144,256]{1,0:T(8,128)(2,1)S(1)}, u32[]{:S(2)}, u32[]{:S(2)}) collective-permute-start(bf16[144,256]{1,0:T(8,128)(2,1)S(1)} %copy-done.2), channel_id=1, source_target_pairs={{0,1},{1,0},{2,3},{3,2},{4,5},{5,4},{6,7},{7,6},{8,9},{9,8},{10,11... | collective-permute-start | bytes 221192 | tf_op jit(solution)/shard_map/ppermute | solution.py:292
  23.5 0.1 pad_add_fusion.place_ref
  23.6 0.0 copy-start.3
  23.6 0.8 %collective-permute-done.other_ref = bf16[144,256]{1,0:T(8,128)(2,1)S(1)} collective-permute-done((bf16[144,256]{1,0:T(8,128)(2,1)S(1)}, bf16[144,256]{1,0:T(8,128)(2,1)S(1)}, u32[]{:S(2)}, u32[]{:S(2)}) %collective-permute-start) | collective-permute-done | bytes 73760 | tf_op jit(solution)/shard_map/ppermute | solution.py:292
  24.4 2.4 %all-to-all-done = bf16[32,8,768]{2,1,0:T(8,128)(2,1)S(1)} async-done(((bf16[32,8,768]{2,1,0:T(8,128)(2,1)}), bf16[32,8,768]{2,1,0:T(8,128)(2,1)S(1)}, u32[]{:S(2)}, u32[]{:S(2)}) %all-to-all-start) | async-done | bytes 393248 | tf_op jit(solution)/shard_map/all_to_all | solution.py:289
  26.7 0.0 copy-done
  26.7 0.0 copy-done.1
  26.7 0.0 copy-done.3
  26.8 2.3 %layers.1 = (bf16[128,256]{1,0:T(8,128)(2,1)}, f32[32,9,2,128]{3,2,1,0:T(2,128)S(1)}) custom-call(s32[2]{0:T(128)S(1)} %pad_add_fusion.place_ref, bf16[256,768]{1,0:T(8,128)(2,1)S(1)} %bitcast.12, bf16[144,256]{1,0:T(8,128)(2,1)S(1)} %copy-done.2, bf16[144,256]{1,0:T(8,128)(2,1)S(1)} %collective-permute-done.other_ref, f32[2,256]{1,0:T(2,128)S(1)} %copy-done.3, ...), custom_call_target="tpu_custom_call" | custom-call | tf_op jit(solution)/shard_map/layers/pallas_call | solution.py:294
  29.1 12.3 %all_to_all.20 = f32[32,9,2,128]{3,2,1,0:T(2,128)S(1)} all-to-all(f32[32,9,2,128]{3,2,1,0:T(2,128)S(1)} %get-tuple-element.15), channel_id=1, replica_groups={{52,54,56,58,60,62,0,2,4,6,8,10,12,14,16,18,20,22,24,26,28,30,32,34,36,..., dimensions={0} | all-to-all | bytes 589824 | tf_op jit(solution)/shard_map/all_to_all | solution.py:305
  41.3 0.1 reduce_sum.18
  41.5 17.3 %all_to_all.21 = f32[8,9,2,128]{3,2,1,0:T(2,128)S(1)} all-to-all(f32[8,9,2,128]{3,2,1,0:T(2,128)S(1)} %broadcast_in_dim.22), channel_id=1, replica_groups={{256,320,384,448,0,64,128,192},{257,321,385,449,1,65,129,193},{258,322,..., dimensions={0} | all-to-all | bytes 147456 | tf_op jit(solution)/shard_map/all_to_all | solution.py:309
  58.8 0.7 repeat.1
  59.5 12.3 %all-to-all-start.3 = ((bf16[64,8,256]{2,1,0:T(8,128)(2,1)}), bf16[64,8,256]{2,1,0:T(8,128)(2,1)S(1)}, u32[]{:S(2)}, u32[]{:S(2)}) async-start(bf16[64,8,256]{2,1,0:T(8,128)(2,1)} %repeat.1), calls=%async_computation.3 | async-start | bytes 524288 | tf_op jit(solution)/shard_map/all_to_all | solution.py:319
  71.9 0.6 slice_bitcast_fusion
  72.4 3.5 %all-to-all-done.3 = bf16[64,8,256]{2,1,0:T(8,128)(2,1)S(1)} async-done(((bf16[64,8,256]{2,1,0:T(8,128)(2,1)}), bf16[64,8,256]{2,1,0:T(8,128)(2,1)S(1)}, u32[]{:S(2)}, u32[]{:S(2)}) %all-to-all-start.3) | async-done | bytes 262176 | tf_op jit(solution)/shard_map/all_to_all | solution.py:319
  75.9 0.8 %widen.1 = (f32[256,256]{1,0:T(8,128)}, f32[256,256]{1,0:T(8,128)}) custom-call(bf16[32,2,8,256]{3,2,1,0:T(8,128)(2,1)S(1)} %bitcast.13), custom_call_target="tpu_custom_call" | custom-call | tf_op jit(solution)/shard_map/widen/pallas_call | solution.py:322
  (4 shorter events, 0.1 us)
Async XLA Ops:
  7.1 14.1 %copy-start.2 = (bf16[144,256]{1,0:T(8,128)(2,1)S(1)}, bf16[144,256]{1,0:T(8,128)(2,1)}, u32[]{:S(2)}) copy-start(bf16[144,256]{1,0:T(8,128)(2,1)} %get-tuple-element.12.own_ref) | copy-start | bytes 221188
  7.1 19.6 %copy-start = (bf16[256,256]{1,0:T(8,128)(2,1)S(1)}, bf16[256,256]{1,0:T(8,128)(2,1)}, u32[]{:S(2)}) copy-start(bf16[256,256]{1,0:T(8,128)(2,1)} %self_ref.1) | copy-start | bytes 393220
  7.1 19.6 %copy-start.1 = (bf16[256,256]{1,0:T(8,128)(2,1)S(1)}, bf16[256,256]{1,0:T(8,128)(2,1)}, u32[]{:S(2)}) copy-start(bf16[256,256]{1,0:T(8,128)(2,1)} %neigh_ref.1) | copy-start | bytes 393220
  7.1 19.6 %all-to-all-start = ((bf16[32,8,768]{2,1,0:T(8,128)(2,1)}), bf16[32,8,768]{2,1,0:T(8,128)(2,1)S(1)}, u32[]{:S(2)}, u32[]{:S(2)}) async-start(bf16[32,8,768]{2,1,0:T(8,128)(2,1)} %get-tuple-element.11), calls=%async_computation | async-start | bytes 786432 | tf_op jit(solution)/shard_map/all_to_all | solution.py:289
  21.2 3.2 %collective-permute-start = (bf16[144,256]{1,0:T(8,128)(2,1)S(1)}, bf16[144,256]{1,0:T(8,128)(2,1)S(1)}, u32[]{:S(2)}, u32[]{:S(2)}) collective-permute-start(bf16[144,256]{1,0:T(8,128)(2,1)S(1)} %copy-done.2), channel_id=1, source_target_pairs={{0,1},{1,0},{2,3},{3,2},{4,5},{5,4},{6,7},{7,6},{8,9},{9,8},{10,11... | collective-permute-start | bytes 221192 | tf_op jit(solution)/shard_map/ppermute | solution.py:292
  23.6 3.2 %copy-start.3 = (f32[2,256]{1,0:T(2,128)S(1)}, f32[2,256]{1,0:T(2,128)}, u32[]{:S(2)}) copy-start(f32[2,256]{1,0:T(2,128)} %get-tuple-element.13.bias_ref) | copy-start | bytes 6148
  59.5 16.4 %all-to-all-start.3 = ((bf16[64,8,256]{2,1,0:T(8,128)(2,1)}), bf16[64,8,256]{2,1,0:T(8,128)(2,1)S(1)}, u32[]{:S(2)}, u32[]{:S(2)}) async-start(bf16[64,8,256]{2,1,0:T(8,128)(2,1)} %repeat.1), calls=%async_computation.3 | async-start | bytes 524288 | tf_op jit(solution)/shard_map/all_to_all | solution.py:319

commit v7 on v6

--- a/solution.py
+++ b/solution.py
@@ -148,19 +148,12 @@
     return value * half, slope
 
 
-def layers_kernel(
-    fan, place_ref, got_ref, own_ref, other_ref, bias_ref, self_ref, neigh_ref, hidden_ref, parts_ref,
+def lists_kernel(
+    fan, place_ref, own_ref, other_ref, bias_ref, often_ref, counts_ref, cot_ref, biases_ref
 ):
-    node_rows, hid = hidden_ref.shape
-    span = 4 * node_rows
-    over_rows = (((0,), (0,)), ((), ()))
-    is_first, first_block = place_ref[0] == 0, place_ref[1]
-    got = got_ref[...]
-    pre_one = lax.dot_general(
-        got[:, :span], got[:, span:], over_rows, preferred_element_type=jnp.float32
-    )
-    hidden = gelu_parts(pre_one + bias_ref[0:1, :])[0].astype(jnp.bfloat16)
-    own = hidden[node_rows : 3 * node_rows]
+    span, node_rows = often_ref.shape[0], often_ref.shape[1] // 2
+    is_first = jnp.bitwise_and(place_ref[0], 1) == 0
+    first_block = lax.shift_right_logical(place_ref[0], 1) * 2 - 1
 
     def lists_of(ref):
         kept = ref[node_rows:, :].astype(jnp.float32)
@@ -168,41 +161,50 @@
         numbers = (kept[:, LANES:].astype(jnp.int32) - first_block) * LANES + place.astype(jnp.int32)
         return numbers, place
 
-    def in_order(own, other):
-        return jnp.where(is_first, own, other), jnp.where(is_first, other, own)
-
-    own_lists, other_lists = lists_of(own_ref), lists_of(other_ref)
+    biases_ref[...] = bias_ref[...]
+    own, other = lists_of(own_ref), lists_of(other_ref)
     number = lax.broadcasted_iota(jnp.int32, (span, node_rows), 0).astype(jnp.int16)
     one, zero = jnp.ones((), jnp.bfloat16), jnp.zeros((), jnp.bfloat16)
-    often = []
-    for numbers in in_order(own_lists[0], other_lists[0]):
+    own_cot, other_cot = own_ref[0:node_rows, :], other_ref[0:node_rows, :]
+    for block in range(2):
+        nodes = slice(block * node_rows, (block + 1) * node_rows)
+        is_own = is_first if block == 0 else jnp.logical_not(is_first)
+        numbers, places = (jnp.where(is_own, mine, its) for mine, its in zip(own, other))
         total = jnp.zeros((span, node_rows), jnp.bfloat16)
         for k in range(fan):
             ids = jnp.broadcast_to(numbers[k : k + 1, :], (span, node_rows)).astype(jnp.int16)
             total = total + jnp.where(ids == number, one, zero)
-        often.append(total)
-    counts = jnp.concatenate(
-        [
-            jnp.broadcast_to(places[fan : fan + 1, :], (LANES, LANES)).T
-            for places in in_order(own_lists[1], other_lists[1])
-        ],
-        axis=0,
-    )
+        often_ref[:, nodes] = total
+        counts_ref[nodes, :] = jnp.broadcast_to(places[fan : fan + 1, :], (LANES, LANES)).T
+        cot_ref[nodes, :] = jnp.where(is_own, own_cot, other_cot)
+
+
+def layers_kernel(
+    place_ref, got_ref, often_ref, counts_ref, cot_ref, bias_ref, self_ref, neigh_ref,
+    hidden_hbm, parts_ref, hidden_ref, left,
+):
+    node_rows, hid = hidden_ref.shape
+    span = 4 * node_rows
+    over_rows = (((0,), (0,)), ((), ()))
+    is_first = jnp.bitwise_and(place_ref[0], 1) == 0
+    got = got_ref[...]
+    pre_one = lax.dot_general(
+        got[:, :span], got[:, span:], over_rows, preferred_element_type=jnp.float32
+    )
+    hidden = gelu_parts(pre_one + bias_ref[0:1, :])[0].astype(jnp.bfloat16)
+    own = hidden[node_rows : 3 * node_rows]
     summed = lax.dot_general(
-        jnp.concatenate(often, axis=1), hidden, over_rows, preferred_element_type=jnp.float32
-    )
-    agg = (summed / jnp.concatenate([counts] * (hid // LANES), axis=1)).astype(jnp.bfloat16)
+        often_ref[...], hidden, over_rows, preferred_element_type=jnp.float32
+    )
+    counts = jnp.concatenate([counts_ref[...]] * (hid // LANES), axis=1)
+    agg = (summed / counts).astype(jnp.bfloat16)
     pre_two = jnp.dot(own, self_ref[...], preferred_element_type=jnp.float32)
     pre_two = pre_two + jnp.dot(agg, neigh_ref[...], preferred_element_type=jnp.float32)
     value, slope = gelu_parts(pre_two + bias_ref[1:2, :])
     hidden_ref[...] = jnp.where(is_first, value[:node_rows], value[node_rows:]).astype(jnp.bfloat16)
-    cot = jnp.concatenate(
-        in_order(
-            own_ref[0:node_rows, :].astype(jnp.float32), other_ref[0:node_rows, :].astype(jnp.float32)
-        ),
-        axis=0,
-    )
-    delta = (cot * slope).astype(jnp.bfloat16)
+    copy = pltpu.make_async_copy(hidden_ref, hidden_hbm, left)
+    copy.start()
+    delta = (cot_ref[...].astype(jnp.float32) * slope).astype(jnp.bfloat16)
     rows = jnp.where(is_first, own, agg)
     grads = lax.dot_general(rows, delta, over_rows, preferred_element_type=jnp.float32)
     bias = jnp.sum(delta.astype(jnp.float32), axis=0, keepdims=True)
@@ -213,6 +215,7 @@
                 part * 8 : part * 8 + 8, columns
             ].reshape(4, 2, LANES)
             parts_ref[part, 8, half : half + 1, :] = bias[:, columns]
+    copy.wait()
 
 
 def repeat_kernel(part_ref, out_ref):
@@ -290,18 +293,36 @@
         chunks, ("chip", "core"), 0, 0, tiled=True, axis_index_groups=[feat_order]
     )
     other = lax.ppermute(send, "core", [(0, 1), (1, 0)])
-    place = jnp.stack([lax.axis_index("core"), lax.axis_index("chip") * cores - 1])
+    place = lax.axis_index(("chip", "core"))[None]
+    scalar = pl.BlockSpec(memory_space=pltpu.SMEM)
+    array = pl.BlockSpec(memory_space=pltpu.VMEM)
+    often, counts, cot, biases = pl.pallas_call(
+        functools.partial(lists_kernel, neighbours_two.shape[1]),
+        out_shape=(
+            jax.ShapeDtypeStruct((span, 2 * node_rows), jnp.bfloat16),
+            jax.ShapeDtypeStruct((2 * node_rows, LANES), jnp.float32),
+            jax.ShapeDtypeStruct((2 * node_rows, hid), jnp.bfloat16),
+            jax.ShapeDtypeStruct(biases.shape, jnp.float32),
+        ),
+        in_specs=[scalar, array, array, array],
+        compiler_params=params,
+        name="lists",
+    )(place, send, other, biases)
     hidden_two, parts = pl.pallas_call(
-        functools.partial(layers_kernel, neighbours_two.shape[1]),
+        layers_kernel,
         out_shape=(
             jax.ShapeDtypeStruct((node_rows, hid), jnp.bfloat16),
             jax.ShapeDtypeStruct((group, 9, 2, LANES), jnp.float32),
         ),
-        in_specs=[pl.BlockSpec(memory_space=pltpu.SMEM)]
-        + [pl.BlockSpec(memory_space=pltpu.VMEM)] * 6,
+        in_specs=[scalar] + [array] * 7,
+        out_specs=(pl.BlockSpec(memory_space=pltpu.HBM), array),
+        scratch_shapes=[pltpu.VMEM((node_rows, hid), jnp.bfloat16), pltpu.SemaphoreType.DMA],
         compiler_params=params,
         name="layers",
-    )(place, got.reshape(groups * 2 * rows, span + hid), send, other, biases, self_two, neigh_two)
+    )(
+        place, got.reshape(groups * 2 * rows, span + hid), often, counts, cot, biases, self_two,
+        neigh_two,
+    )
     inner = lax.all_to_all(
         parts, ("pair", "chip"), 0, 0, tiled=True, axis_index_groups=[part_order]
     ).sum(axis=0)

time: 77.1 us -> 76.3 us (0.990)
    pallas_call x1 -> x2, Pallas kernels: 2.3 us -> 1.86 us  [the longest x1 1.51 us: local(): pl.pallas_call(layers_kernel, out_shape=(jax.ShapeDtypeStruct((node_rows,...]
where the time goes in v7:
time: 76.3 us; the launch traced here: 76 us
  blocking collectives  29.6 us (39%)
  starting transfers between devices  28.8 us (38%)
  Pallas kernels  9.86 us (13%)
  waiting for transfers between devices  6.27 us (8%)
    all_to_all x1, blocking collectives, local(): lax.all_to_all(spread, 'apart', 0, 0, tiled=True, axis_index_groups=[apar...  17.3 us
    all_to_all x1, starting transfers between devices, local(): lax.all_to_all(chunks, ('chip', 'core'), 0, 0, tiled=True, axis_index_gro...  14 us
    all_to_all x1, starting transfers between devices, local(): lax.all_to_all(spread, ('pair', 'chip', 'core'), 0, 0, tiled=True, axis_i...  12.3 us
    all_to_all x1, blocking collectives, local(): lax.all_to_all(parts, ('pair', 'chip'), 0, 0, tiled=True, axis_index_grou...  12.3 us
    pallas_call x1, Pallas kernels, local(): pl.pallas_call(functools.partial(pick_kernel, feat_order), out_shape=(jax...  6.46 us
    all_to_all x1, waiting for transfers between devices, local(): lax.all_to_all(spread, ('pair', 'chip', 'core'), 0, 0, tiled=True, axis_i...  3.5 us
    ppermute x1, starting transfers between devices, local(): other = lax.ppermute(send, 'core', [(0, 1), (1, 0)])  2.4 us
    all_to_all x1, waiting for transfers between devices, local(): lax.all_to_all(chunks, ('chip', 'core'), 0, 0, tiled=True, axis_index_gro...  1.88 us
  transfers between devices with their start and end apart: 3, of which 3 were waited for; matrix products, arithmetic and copies ran while one was open for 1% of the time, Pallas kernels for 0%

profile of v7, /device:TPU:1, one launch (start us, length us, event | category | flops | bytes accessed | tf_op | source)
XLA Modules:
  0.0 76.0 jit_solution(7555947098687809944)
XLA Ops:
  0.6 6.5 %pick.1 = (bf16[32,8,768]{2,1,0:T(8,128)(2,1)}, bf16[144,256]{1,0:T(8,128)(2,1)}, f32[2,256]{1,0:T(2,128)}) custom-call(bf16[4,4096]{1,0:T(4,128)(2,1)} %feats_hbm.1, s32[15,4096]{1,0:T(8,128)} %bitcast.13, s32[1,4096]{1,0:T(1,128)} %bitcast.14, bf16[4,256]{1,0:T(4,128)(2,1)} %self_hbm.1, bf16[4,256]{1,0:T(4,128)(2,1)} %neigh_hbm.1, s32[10,128]{1,0:T(8,128)} %bitcast.15, ...), custom_call_target="tpu_custom_call" | custom-call | tf_op jit(solution)/shard_map/pick/pallas_call | solution.py:273
  7.1 0.0 copy-start.2
  7.1 0.0 copy-start.3
  7.1 0.0 copy-start.1
  7.1 14.0 %all-to-all-start = ((bf16[32,8,768]{2,1,0:T(8,128)(2,1)}), bf16[32,8,768]{2,1,0:T(8,128)(2,1)S(1)}, u32[]{:S(2)}, u32[]{:S(2)}) async-start(bf16[32,8,768]{2,1,0:T(8,128)(2,1)} %get-tuple-element.15), calls=%async_computation | async-start | bytes 786432 | tf_op jit(solution)/shard_map/all_to_all | solution.py:292
  21.2 0.0 copy-start
  21.2 0.0 copy-done.2
  21.2 2.4 %collective-permute-start = (bf16[144,256]{1,0:T(8,128)(2,1)S(1)}, bf16[144,256]{1,0:T(8,128)(2,1)S(1)}, u32[]{:S(2)}, u32[]{:S(2)}) collective-permute-start(bf16[144,256]{1,0:T(8,128)(2,1)S(1)} %copy-done.2), channel_id=1, source_target_pairs={{0,1},{1,0},{2,3},{3,2},{4,5},{5,4},{6,7},{7,6},{8,9},{9,8},{10,11... | collective-permute-start | bytes 221192 | tf_op jit(solution)/shard_map/ppermute | solution.py:295
  23.6 0.9 %collective-permute-done.other_ref = bf16[144,256]{1,0:T(8,128)(2,1)S(1)} collective-permute-done((bf16[144,256]{1,0:T(8,128)(2,1)S(1)}, bf16[144,256]{1,0:T(8,128)(2,1)S(1)}, u32[]{:S(2)}, u32[]{:S(2)}) %collective-permute-start) | collective-permute-done | bytes 73760 | tf_op jit(solution)/shard_map/ppermute | solution.py:295
  24.5 0.0 copy-done.3
  24.5 0.3 lists.1
  24.8 1.9 %all-to-all-done = bf16[32,8,768]{2,1,0:T(8,128)(2,1)S(1)} async-done(((bf16[32,8,768]{2,1,0:T(8,128)(2,1)}), bf16[32,8,768]{2,1,0:T(8,128)(2,1)S(1)}, u32[]{:S(2)}, u32[]{:S(2)}) %all-to-all-start) | async-done | bytes 393248 | tf_op jit(solution)/shard_map/all_to_all | solution.py:292
  26.7 0.0 copy-done.1
  26.7 0.0 copy-done
  26.7 1.5 %layers.1 = (bf16[128,256]{1,0:T(8,128)(2,1)}, f32[32,9,2,128]{3,2,1,0:T(2,128)S(1)}) custom-call(s32[1]{0:T(128)} %bitcast.place_ref, bf16[256,768]{1,0:T(8,128)(2,1)S(1)} %bitcast.11, bf16[512,256]{1,0:T(8,128)(2,1)S(1)} %get-tuple-element.18.often_ref, f32[256,128]{1,0:T(8,128)S(1)} %get-tuple-element.19.counts_ref, ...), custom_call_target="tpu_custom_call" | custom-call | tf_op jit(solution)/shard_map/layers/pallas_call | solution.py:311
  28.3 12.3 %all_to_all.20 = f32[32,9,2,128]{3,2,1,0:T(2,128)S(1)} all-to-all(f32[32,9,2,128]{3,2,1,0:T(2,128)S(1)} %get-tuple-element.23), channel_id=1, replica_groups={{52,54,56,58,60,62,0,2,4,6,8,10,12,14,16,18,20,22,24,26,28,30,32,34,36,..., dimensions={0} | all-to-all | bytes 589824 | tf_op jit(solution)/shard_map/all_to_all | solution.py:326
  40.6 0.1 reduce_sum.18
  40.7 17.3 %all_to_all.21 = f32[8,9,2,128]{3,2,1,0:T(2,128)S(1)} all-to-all(f32[8,9,2,128]{3,2,1,0:T(2,128)S(1)} %broadcast_in_dim.26), channel_id=1, replica_groups={{256,320,384,448,0,64,128,192},{257,321,385,449,1,65,129,193},{258,322,..., dimensions={0} | all-to-all | bytes 147456 | tf_op jit(solution)/shard_map/all_to_all | solution.py:330
  58.0 0.7 repeat.1
  58.7 12.3 %all-to-all-start.3 = ((bf16[64,8,256]{2,1,0:T(8,128)(2,1)}), bf16[64,8,256]{2,1,0:T(8,128)(2,1)S(1)}, u32[]{:S(2)}, u32[]{:S(2)}) async-start(bf16[64,8,256]{2,1,0:T(8,128)(2,1)} %repeat.1), calls=%async_computation.3 | async-start | bytes 524288 | tf_op jit(solution)/shard_map/all_to_all | solution.py:340
  71.1 0.6 slice_bitcast_fusion
  71.6 3.5 %all-to-all-done.3 = bf16[64,8,256]{2,1,0:T(8,128)(2,1)S(1)} async-done(((bf16[64,8,256]{2,1,0:T(8,128)(2,1)}), bf16[64,8,256]{2,1,0:T(8,128)(2,1)S(1)}, u32[]{:S(2)}, u32[]{:S(2)}) %all-to-all-start.3) | async-done | bytes 262176 | tf_op jit(solution)/shard_map/all_to_all | solution.py:340
  75.1 0.8 %widen.1 = (f32[256,256]{1,0:T(8,128)}, f32[256,256]{1,0:T(8,128)}) custom-call(bf16[32,2,8,256]{3,2,1,0:T(8,128)(2,1)S(1)} %bitcast.12), custom_call_target="tpu_custom_call" | custom-call | tf_op jit(solution)/shard_map/widen/pallas_call | solution.py:343
  (4 shorter events, 0.1 us)
Async XLA Ops:
  7.1 14.1 %copy-start.2 = (bf16[144,256]{1,0:T(8,128)(2,1)S(1)}, bf16[144,256]{1,0:T(8,128)(2,1)}, u32[]{:S(2)}) copy-start(bf16[144,256]{1,0:T(8,128)(2,1)} %get-tuple-element.16.own_ref) | copy-start | bytes 221188
  7.1 17.4 %copy-start.3 = (f32[2,256]{1,0:T(2,128)S(1)}, f32[2,256]{1,0:T(2,128)}, u32[]{:S(2)}) copy-start(f32[2,256]{1,0:T(2,128)} %get-tuple-element.17.bias_ref) | copy-start | bytes 6148
  7.1 19.6 %copy-start.1 = (bf16[256,256]{1,0:T(8,128)(2,1)S(1)}, bf16[256,256]{1,0:T(8,128)(2,1)}, u32[]{:S(2)}) copy-start(bf16[256,256]{1,0:T(8,128)(2,1)} %neigh_ref.1) | copy-start | bytes 393220
  7.1 19.6 %all-to-all-start = ((bf16[32,8,768]{2,1,0:T(8,128)(2,1)}), bf16[32,8,768]{2,1,0:T(8,128)(2,1)S(1)}, u32[]{:S(2)}, u32[]{:S(2)}) async-start(bf16[32,8,768]{2,1,0:T(8,128)(2,1)} %get-tuple-element.15), calls=%async_computation | async-start | bytes 786432 | tf_op jit(solution)/shard_map/all_to_all | solution.py:292
  21.2 5.6 %copy-start = (bf16[256,256]{1,0:T(8,128)(2,1)S(1)}, bf16[256,256]{1,0:T(8,128)(2,1)}, u32[]{:S(2)}) copy-start(bf16[256,256]{1,0:T(8,128)(2,1)} %self_ref.1) | copy-start | bytes 393220
  21.2 3.3 %collective-permute-start = (bf16[144,256]{1,0:T(8,128)(2,1)S(1)}, bf16[144,256]{1,0:T(8,128)(2,1)S(1)}, u32[]{:S(2)}, u32[]{:S(2)}) collective-permute-start(bf16[144,256]{1,0:T(8,128)(2,1)S(1)} %copy-done.2), channel_id=1, source_target_pairs={{0,1},{1,0},{2,3},{3,2},{4,5},{5,4},{6,7},{7,6},{8,9},{9,8},{10,11... | collective-permute-start | bytes 221192 | tf_op jit(solution)/shard_map/ppermute | solution.py:295
  58.7 16.4 %all-to-all-start.3 = ((bf16[64,8,256]{2,1,0:T(8,128)(2,1)}), bf16[64,8,256]{2,1,0:T(8,128)(2,1)S(1)}, u32[]{:S(2)}, u32[]{:S(2)}) async-start(bf16[64,8,256]{2,1,0:T(8,128)(2,1)} %repeat.1), calls=%async_computation.3 | async-start | bytes 524288 | tf_op jit(solution)/shard_map/all_to_all | solution.py:340

commit v8 on v7

--- a/solution.py
+++ b/solution.py
@@ -151,7 +151,7 @@
 def lists_kernel(
     fan, place_ref, own_ref, other_ref, bias_ref, often_ref, counts_ref, cot_ref, biases_ref
 ):
-    span, node_rows = often_ref.shape[0], often_ref.shape[1] // 2
+    span, node_rows = often_ref.shape[1], often_ref.shape[0] // 2
     is_first = jnp.bitwise_and(place_ref[0], 1) == 0
     first_block = lax.shift_right_logical(place_ref[0], 1) * 2 - 1
 
@@ -174,7 +174,7 @@
         for k in range(fan):
             ids = jnp.broadcast_to(numbers[k : k + 1, :], (span, node_rows)).astype(jnp.int16)
             total = total + jnp.where(ids == number, one, zero)
-        often_ref[:, nodes] = total
+        often_ref[nodes, :] = total.T
         counts_ref[nodes, :] = jnp.broadcast_to(places[fan : fan + 1, :], (LANES, LANES)).T
         cot_ref[nodes, :] = jnp.where(is_own, own_cot, other_cot)
 
@@ -193,9 +193,7 @@
     )
     hidden = gelu_parts(pre_one + bias_ref[0:1, :])[0].astype(jnp.bfloat16)
     own = hidden[node_rows : 3 * node_rows]
-    summed = lax.dot_general(
-        often_ref[...], hidden, over_rows, preferred_element_type=jnp.float32
-    )
+    summed = jnp.dot(often_ref[...], hidden, preferred_element_type=jnp.float32)
     counts = jnp.concatenate([counts_ref[...]] * (hid // LANES), axis=1)
     agg = (summed / counts).astype(jnp.bfloat16)
     pre_two = jnp.dot(own, self_ref[...], preferred_element_type=jnp.float32)
@@ -224,15 +222,20 @@
         out_ref[to] = part
 
 
-def widen_kernel(got_ref, self_ref, neigh_ref):
+def widen_kernel(got_ref, total_ref, self_ref, neigh_ref, bias_ref):
     parts, _, rows, _ = got_ref.shape
     for part in range(parts):
-        self_ref[part * rows : (part + 1) * rows, :] = got_ref[part, 0].astype(jnp.float32)
-        neigh_ref[part * rows : (part + 1) * rows, :] = got_ref[part, 1].astype(jnp.float32)
+        self_ref[part * rows : (part + 1) * rows, :] = got_ref[part, 1].astype(jnp.float32)
+        neigh_ref[part * rows : (part + 1) * rows, :] = got_ref[part, 0].astype(jnp.float32)
+    bias_ref[...] = jnp.concatenate([total_ref[16:17, :], total_ref[17:18, :]], axis=1)
 
 
 def from_member(first, size):
     return [(first + i) % size for i in range(size)]
+
+
+def both_cores(order):
+    return [2 * chip + core for chip in order for core in (1, 0)]
 
 
 def local(
@@ -261,9 +264,9 @@
     everyone = group * cores
     first_chip = chips // 2 + chips // 8
     first_part = group - chips + first_chip
-    feat_order = from_member(first_chip * cores, groups)
+    feat_order = both_cores(from_member(first_chip, chips))
     part_order = from_member(first_part, group)
-    every_order = from_member(first_part * cores, everyone)
+    every_order = both_cores(part_order)
     apart_order = from_member(others // 2, others)
     lists = (16, node_rows)
     loads = (
@@ -299,7 +302,7 @@
     often, counts, cot, biases = pl.pallas_call(
         functools.partial(lists_kernel, neighbours_two.shape[1]),
         out_shape=(
-            jax.ShapeDtypeStruct((span, 2 * node_rows), jnp.bfloat16),
+            jax.ShapeDtypeStruct((2 * node_rows, span), jnp.bfloat16),
             jax.ShapeDtypeStruct((2 * node_rows, LANES), jnp.float32),
             jax.ShapeDtypeStruct((2 * node_rows, hid), jnp.bfloat16),
             jax.ShapeDtypeStruct(biases.shape, jnp.float32),
@@ -340,13 +343,17 @@
     whole = lax.all_to_all(
         spread, ("pair", "chip", "core"), 0, 0, tiled=True, axis_index_groups=[every_order]
     )
-    grad_self, grad_neigh = pl.pallas_call(
+    grad_self, grad_neigh, grad_bias = pl.pallas_call(
         widen_kernel,
-        out_shape=(jax.ShapeDtypeStruct((hid, hid), jnp.float32),) * 2,
+        out_shape=(
+            jax.ShapeDtypeStruct((hid, hid), jnp.float32),
+            jax.ShapeDtypeStruct((hid, hid), jnp.float32),
+            jax.ShapeDtypeStruct((1, hid), jnp.float32),
+        ),
         compiler_params=params,
         name="widen",
-    )(whole.reshape(group, cores, hid // group, hid))
-    return hidden_two, grad_self, grad_neigh, total[16:].reshape(hid)
+    )(whole.reshape(group, cores, hid // group, hid), total)
+    return hidden_two, grad_self, grad_neigh, grad_bias.reshape(hid)
 
 
 def solution(mesh):

time: 76.3 us -> 73.6 us (0.965)
  blocking collectives: 29.6 us -> 44.3 us
  starting transfers between devices: 28.8 us -> 16.2 us
  waiting for transfers between devices: 6.27 us -> 2.68 us
    all_to_all x0 -> x1, blocking collectives: none -> 16.1 us  [local(): lax.all_to_all(spread, ('pair', 'chip', 'core'), 0, 0, tiled=True, axis_i...]
    all_to_all x1 -> x0, starting transfers between devices: 12.3 us -> none  [local(): lax.all_to_all(spread, ('pair', 'chip', 'core'), 0, 0, tiled=True, axis_i...]
    all_to_all x1 -> x0, waiting for transfers between devices: 3.5 us -> none  [local(): lax.all_to_all(spread, ('pair', 'chip', 'core'), 0, 0, tiled=True, axis_i...]
    all_to_all x1, blocking collectives: 12.3 us -> 11.3 us  [local(): lax.all_to_all(parts, ('pair', 'chip'), 0, 0, tiled=True, axis_index_grou...]
  transfers between devices with their start and end apart: 3 -> 2, of which waited for: 3 -> 2; matrix products, arithmetic and copies ran while one was open for 1% -> 0% of each run, Pallas kernels for 0% -> 0%
where the time goes in v8:
time: 73.6 us; the launch traced here: 73.3 us
  blocking collectives  44.3 us (60%)
  starting transfers between devices  16.2 us (22%)
  Pallas kernels  9.15 us (12%)
  waiting for transfers between devices  2.68 us (4%)
  between operations  0.74 us (1%)
    all_to_all x1, blocking collectives, local(): lax.all_to_all(spread, 'apart', 0, 0, tiled=True, axis_index_groups=[apar...  17 us
    all_to_all x1, blocking collectives, local(): lax.all_to_all(spread, ('pair', 'chip', 'core'), 0, 0, tiled=True, axis_i...  16.1 us
    all_to_all x1, starting transfers between devices, local(): lax.all_to_all(chunks, ('chip', 'core'), 0, 0, tiled=True, axis_index_gro...  13.7 us
    all_to_all x1, blocking collectives, local(): lax.all_to_all(parts, ('pair', 'chip'), 0, 0, tiled=True, axis_index_grou...  11.3 us
    pallas_call x1, Pallas kernels, local(): pl.pallas_call(functools.partial(pick_kernel, feat_order), out_shape=(jax...  6.45 us
    ppermute x1, starting transfers between devices, local(): other = lax.ppermute(send, 'core', [(0, 1), (1, 0)])  2.47 us
    all_to_all x1, waiting for transfers between devices, local(): lax.all_to_all(chunks, ('chip', 'core'), 0, 0, tiled=True, axis_index_gro...  1.79 us
    pallas_call x1, Pallas kernels, local(): pl.pallas_call(layers_kernel, out_shape=(jax.ShapeDtypeStruct((node_rows,...  1.51 us
  transfers between devices with their start and end apart: 2, of which 2 were waited for; matrix products, arithmetic and copies ran while one was open for 0% of the time, Pallas kernels for 0%

profile of v8, /device:TPU:1, one launch (start us, length us, event | category | flops | bytes accessed | tf_op | source)
XLA Modules:
  0.0 73.3 jit_solution(910153773265647564)
XLA Ops:
  0.6 6.5 %pick.1 = (bf16[32,8,768]{2,1,0:T(8,128)(2,1)}, bf16[144,256]{1,0:T(8,128)(2,1)}, f32[2,256]{1,0:T(2,128)}) custom-call(bf16[4,4096]{1,0:T(4,128)(2,1)} %feats_hbm.1, s32[15,4096]{1,0:T(8,128)} %bitcast.12, s32[1,4096]{1,0:T(1,128)} %bitcast.13, bf16[4,256]{1,0:T(4,128)(2,1)} %self_hbm.1, bf16[4,256]{1,0:T(4,128)(2,1)} %neigh_hbm.1, s32[10,128]{1,0:T(8,128)} %bitcast.14, ...), custom_call_target="tpu_custom_call" | custom-call | tf_op jit(solution)/shard_map/pick/pallas_call | solution.py:276
  7.1 0.0 copy-start.2
  7.1 0.0 copy-start.3
  7.1 0.0 copy-start.1
  7.1 13.7 %all-to-all-start = ((bf16[32,8,768]{2,1,0:T(8,128)(2,1)}), bf16[32,8,768]{2,1,0:T(8,128)(2,1)S(1)}, u32[]{:S(2)}, u32[]{:S(2)}) async-start(bf16[32,8,768]{2,1,0:T(8,128)(2,1)} %get-tuple-element.16), calls=%async_computation | async-start | bytes 786432 | tf_op jit(solution)/shard_map/all_to_all | solution.py:295
  20.9 0.0 copy-start
  20.9 0.0 copy-done.2
  20.9 2.5 %collective-permute-start = (bf16[144,256]{1,0:T(8,128)(2,1)S(1)}, bf16[144,256]{1,0:T(8,128)(2,1)S(1)}, u32[]{:S(2)}, u32[]{:S(2)}) collective-permute-start(bf16[144,256]{1,0:T(8,128)(2,1)S(1)} %copy-done.2), channel_id=1, source_target_pairs={{0,1},{1,0},{2,3},{3,2},{4,5},{5,4},{6,7},{7,6},{8,9},{9,8},{10,11... | collective-permute-start | bytes 221192 | tf_op jit(solution)/shard_map/ppermute | solution.py:298
  23.4 0.9 %collective-permute-done.other_ref = bf16[144,256]{1,0:T(8,128)(2,1)S(1)} collective-permute-done((bf16[144,256]{1,0:T(8,128)(2,1)S(1)}, bf16[144,256]{1,0:T(8,128)(2,1)S(1)}, u32[]{:S(2)}, u32[]{:S(2)}) %collective-permute-start) | collective-permute-done | bytes 73760 | tf_op jit(solution)/shard_map/ppermute | solution.py:298
  24.2 0.0 copy-done.3
  24.2 0.4 lists.1
  24.6 1.8 %all-to-all-done = bf16[32,8,768]{2,1,0:T(8,128)(2,1)S(1)} async-done(((bf16[32,8,768]{2,1,0:T(8,128)(2,1)}), bf16[32,8,768]{2,1,0:T(8,128)(2,1)S(1)}, u32[]{:S(2)}, u32[]{:S(2)}) %all-to-all-start) | async-done | bytes 393248 | tf_op jit(solution)/shard_map/all_to_all | solution.py:295
  26.4 0.0 copy-done.1
  26.4 0.0 copy-done
  26.4 1.5 %layers.1 = (bf16[128,256]{1,0:T(8,128)(2,1)}, f32[32,9,2,128]{3,2,1,0:T(2,128)S(1)}) custom-call(s32[1]{0:T(128)} %bitcast.place_ref, bf16[256,768]{1,0:T(8,128)(2,1)S(1)} %bitcast.10, bf16[256,512]{1,0:T(8,128)(2,1)S(1)} %get-tuple-element.19.often_ref, f32[256,128]{1,0:T(8,128)S(1)} %get-tuple-element.20.counts_ref, ...), custom_call_target="tpu_custom_call" | custom-call | tf_op jit(solution)/shard_map/layers/pallas_call | solution.py:314
  27.9 11.3 %all_to_all.20 = f32[32,9,2,128]{3,2,1,0:T(2,128)S(1)} all-to-all(f32[32,9,2,128]{3,2,1,0:T(2,128)S(1)} %get-tuple-element.24), channel_id=1, replica_groups={{52,54,56,58,60,62,0,2,4,6,8,10,12,14,16,18,20,22,24,26,28,30,32,34,36,..., dimensions={0} | all-to-all | bytes 589824 | tf_op jit(solution)/shard_map/all_to_all | solution.py:329
  39.2 0.1 reduce_sum.18
  39.3 17.0 %all_to_all.21 = f32[8,9,2,128]{3,2,1,0:T(2,128)S(1)} all-to-all(f32[8,9,2,128]{3,2,1,0:T(2,128)S(1)} %broadcast_in_dim.26), channel_id=1, replica_groups={{256,320,384,448,0,64,128,192},{257,321,385,449,1,65,129,193},{258,322,..., dimensions={0} | all-to-all | bytes 147456 | tf_op jit(solution)/shard_map/all_to_all | solution.py:333
  56.4 16.1 %all_to_all.22 = bf16[64,8,256]{2,1,0:T(8,128)(2,1)S(1)} all-to-all(bf16[64,8,256]{2,1,0:T(8,128)(2,1)S(1)} %repeat.1), channel_id=1, replica_groups={{53,52,55,54,57,56,59,58,61,60,63,62,1,0,3,2,5,4,7,6,9,8,11,10,13,12,15..., dimensions={0} | all-to-all | bytes 524288 | tf_op jit(solution)/shard_map/all_to_all | solution.py:343
  72.5 0.8 %widen.1 = (f32[256,256]{1,0:T(8,128)}, f32[256,256]{1,0:T(8,128)}, f32[1,256]{1,0:T(1,128)}) custom-call(bf16[32,2,8,256]{3,2,1,0:T(8,128)(2,1)S(1)} %bitcast.11, f32[18,128]{1,0:T(8,128)S(1)} %mul.14.part_ref.total_ref), custom_call_target="tpu_custom_call" | custom-call | tf_op jit(solution)/shard_map/widen/pallas_call | solution.py:346
  (5 shorter events, 0.1 us)
Async XLA Ops:
  7.1 13.8 %copy-start.2 = (bf16[144,256]{1,0:T(8,128)(2,1)S(1)}, bf16[144,256]{1,0:T(8,128)(2,1)}, u32[]{:S(2)}) copy-start(bf16[144,256]{1,0:T(8,128)(2,1)} %get-tuple-element.17.own_ref) | copy-start | bytes 221188
  7.1 17.1 %copy-start.3 = (f32[2,256]{1,0:T(2,128)S(1)}, f32[2,256]{1,0:T(2,128)}, u32[]{:S(2)}) copy-start(f32[2,256]{1,0:T(2,128)} %get-tuple-element.18.bias_ref) | copy-start | bytes 6148
  7.1 19.3 %copy-start.1 = (bf16[256,256]{1,0:T(8,128)(2,1)S(1)}, bf16[256,256]{1,0:T(8,128)(2,1)}, u32[]{:S(2)}) copy-start(bf16[256,256]{1,0:T(8,128)(2,1)} %neigh_ref.1) | copy-start | bytes 393220
  7.1 19.3 %all-to-all-start = ((bf16[32,8,768]{2,1,0:T(8,128)(2,1)}), bf16[32,8,768]{2,1,0:T(8,128)(2,1)S(1)}, u32[]{:S(2)}, u32[]{:S(2)}) async-start(bf16[32,8,768]{2,1,0:T(8,128)(2,1)} %get-tuple-element.16), calls=%async_computation | async-start | bytes 786432 | tf_op jit(solution)/shard_map/all_to_all | solution.py:295
  20.9 5.5 %copy-start = (bf16[256,256]{1,0:T(8,128)(2,1)S(1)}, bf16[256,256]{1,0:T(8,128)(2,1)}, u32[]{:S(2)}) copy-start(bf16[256,256]{1,0:T(8,128)(2,1)} %self_ref.1) | copy-start | bytes 393220
  20.9 3.4 %collective-permute-start = (bf16[144,256]{1,0:T(8,128)(2,1)S(1)}, bf16[144,256]{1,0:T(8,128)(2,1)S(1)}, u32[]{:S(2)}, u32[]{:S(2)}) collective-permute-start(bf16[144,256]{1,0:T(8,128)(2,1)S(1)} %copy-done.2), channel_id=1, source_target_pairs={{0,1},{1,0},{2,3},{3,2},{4,5},{5,4},{6,7},{7,6},{8,9},{9,8},{10,11... | collective-permute-start | bytes 221192 | tf_op jit(solution)/shard_map/ppermute | solution.py:298

commit v9 on v8

--- a/solution.py
+++ b/solution.py
@@ -10,6 +10,8 @@
 from jax.sharding import PartitionSpec as P
 
 LANES = 128
+BY_MATMUL = 8
+REACH = 256
 DEAD = -64
 INNER = math.sqrt(2.0 / math.pi)
 CUBIC = 0.044715
@@ -65,8 +67,15 @@
     wide[0:rows, :] = values
     wide[rows : 2 * rows, :] = values
     table[...] = jnp.concatenate([wide[...]] * 2, axis=0).astype(jnp.bfloat16)
-    for copy in copies[1:]:
+    reaches = nodes // REACH
+    flat = jnp.concatenate(
+        [values[:, i * REACH : (i + 1) * REACH] for i in range(reaches)], axis=0
+    ).astype(jnp.bfloat16)
+    for copy in copies[1:3]:
         copy.wait()
+    in_reach = lax.broadcasted_iota(jnp.int32, (REACH, LANES), 0).astype(jnp.int16)
+    reach_of_row = lax.broadcasted_iota(jnp.int32, (reaches * rows, LANES), 0) // rows
+    one, zero = jnp.ones((), jnp.bfloat16), jnp.zeros((), jnp.bfloat16)
     row = lax.broadcasted_iota(jnp.int32, (4 * rows, LANES), 0)
     upper = lax.broadcasted_iota(jnp.int32, (2 * rows, LANES), 0) < rows
 
@@ -84,23 +93,44 @@
                 jnp.where(row < 3 * rows, parts[2], parts[3]),
             )
 
-        counts = spread(counts_ref, 0)
-        total = jnp.zeros(row.shape, jnp.float32)
-        for k in range(fan):
-            ids = spread(ids_ref, k)
-            lane = jnp.bitwise_and(ids, LANES - 1).astype(jnp.int16)
-            block = lax.shift_right_logical(ids, 7).astype(jnp.int16)
+        def by_lanes(k):
+            ids = spread(ids_ref, k).astype(jnp.int16)
+            lane = jnp.bitwise_and(ids, jnp.int16(LANES - 1))
             level = [
                 lane_gather(table[:, j * LANES : (j + 1) * LANES], lane) for j in range(blocks)
             ]
-            bit = 1
+            bit = LANES
             while len(level) > 1:
-                odd = jnp.bitwise_and(block, jnp.int16(bit)) != 0
+                odd = jnp.bitwise_and(ids, jnp.int16(bit)) != 0
                 level = [
                     jnp.where(odd, level[i + 1], level[i]) for i in range(0, len(level), 2)
                 ]
                 bit *= 2
-            total = total + jnp.where(counts > k, level[0].astype(jnp.float32), 0.0)
+            return jnp.where(counts > k, level[0].astype(jnp.float32), 0.0)
+
+        def by_matmul(k, i):
+            lanes = pl.ds(start + i * LANES, LANES)
+            ids, live = ids_ref[k : k + 1, lanes], counts_ref[0:1, lanes] > k
+            place = jnp.broadcast_to(jnp.bitwise_and(ids, REACH - 1), in_reach.shape)
+            hot = jnp.where(place.astype(jnp.int16) == in_reach, one, zero)
+            found = jnp.dot(flat, hot, preferred_element_type=jnp.float32)
+            reach = jnp.where(live, lax.shift_right_logical(ids, REACH.bit_length() - 1), -1)
+            found = jnp.where(jnp.broadcast_to(reach, found.shape) == reach_of_row, found, 0.0)
+            return jnp.sum(found.reshape(-1, 2 * rows, LANES), axis=0)
+
+        counts = spread(counts_ref, 0)
+        total = jnp.zeros(row.shape, jnp.float32)
+        pairs = [jnp.zeros(upper.shape, jnp.float32)] * 4
+        by_lane = fan - BY_MATMUL
+        for k in range(max(by_lane, BY_MATMUL)):
+            if k < by_lane:
+                total = total + by_lanes(k)
+            if k < BY_MATMUL:
+                pairs = [pair + by_matmul(by_lane + k, i) for i, pair in enumerate(pairs)]
+        pairs = [pair + pltpu.roll(pair, rows, axis=0) for pair in pairs]
+        total = total + jnp.concatenate(
+            [jnp.where(upper, pairs[i], pairs[i + 1]) for i in (0, 2)], axis=0
+        )
         mean = total / counts.astype(jnp.float32)
         for i in range(4):
             half = mean[(i // 2) * 2 * rows : (i // 2 + 1) * 2 * rows]
@@ -115,6 +145,8 @@
     lax.fori_loop(0, blocks // 4, four_blocks, 0, unroll=True)
     sums[:, 0:LANES] = sums[:, blocks * LANES : (blocks + 1) * LANES]
     sums[:, (blocks + 1) * LANES :] = sums[:, LANES : 2 * LANES]
+    for copy in copies[3:]:
+        copy.wait()
     node_rows = cot_ref.shape[0]
     fan_two = ids_two_ref.shape[0]
     lists[...] = jnp.zeros_like(lists)
@@ -267,7 +299,7 @@
     feat_order = both_cores(from_member(first_chip, chips))
     part_order = from_member(first_part, group)
     every_order = both_cores(part_order)
-    apart_order = from_member(others // 2, others)
+    apart_order = sorted(range(others), key=lambda i: (i != others // 2, min(i, others - i)))
     lists = (16, node_rows)
     loads = (
         features, neighbours_one.T, counts_one[None, :], self_one, neigh_one, neighbours_two.T,

time: 73.6 us -> 71.9 us (0.977)
  Pallas kernels: 9.15 us -> 7.6 us
    pallas_call x1, Pallas kernels: 6.45 us -> 4.9 us  [local(): pl.pallas_call(functools.partial(pick_kernel, feat_order), out_shape=(jax...]
where the time goes in v9:
time: 71.9 us; the launch traced here: 71.6 us
  blocking collectives  44.2 us (61%)
  starting transfers between devices  16.2 us (23%)
  Pallas kernels  7.6 us (11%)
  waiting for transfers between devices  2.68 us (4%)
  between operations  0.74 us (1%)
    all_to_all x1, blocking collectives, local(): lax.all_to_all(spread, 'apart', 0, 0, tiled=True, axis_index_groups=[apar...  17.1 us
    all_to_all x1, blocking collectives, local(): lax.all_to_all(spread, ('pair', 'chip', 'core'), 0, 0, tiled=True, axis_i...  15.8 us
    all_to_all x1, starting transfers between devices, local(): lax.all_to_all(chunks, ('chip', 'core'), 0, 0, tiled=True, axis_index_gro...  13.7 us
    all_to_all x1, blocking collectives, local(): lax.all_to_all(parts, ('pair', 'chip'), 0, 0, tiled=True, axis_index_grou...  11.3 us
    pallas_call x1, Pallas kernels, local(): pl.pallas_call(functools.partial(pick_kernel, feat_order), out_shape=(jax...  4.9 us
    ppermute x1, starting transfers between devices, local(): other = lax.ppermute(send, 'core', [(0, 1), (1, 0)])  2.47 us
    all_to_all x1, waiting for transfers between devices, local(): lax.all_to_all(chunks, ('chip', 'core'), 0, 0, tiled=True, axis_index_gro...  1.79 us
    pallas_call x1, Pallas kernels, local(): pl.pallas_call(layers_kernel, out_shape=(jax.ShapeDtypeStruct((node_rows,...  1.51 us
  transfers between devices with their start and end apart: 2, of which 2 were waited for; matrix products, arithmetic and copies ran while one was open for 0% of the time, Pallas kernels for 0%

profile of v9, /device:TPU:1, one launch (start us, length us, event | category | flops | bytes accessed | tf_op | source)
XLA Modules:
  0.0 71.6 jit_solution(3247025732521304155)
XLA Ops:
  0.6 4.9 %pick.1 = (bf16[32,8,768]{2,1,0:T(8,128)(2,1)}, bf16[144,256]{1,0:T(8,128)(2,1)}, f32[2,256]{1,0:T(2,128)}) custom-call(bf16[4,4096]{1,0:T(4,128)(2,1)} %feats_hbm.1, s32[15,4096]{1,0:T(8,128)} %bitcast.12, s32[1,4096]{1,0:T(1,128)} %bitcast.13, bf16[4,256]{1,0:T(4,128)(2,1)} %self_hbm.1, bf16[4,256]{1,0:T(4,128)(2,1)} %neigh_hbm.1, s32[10,128]{1,0:T(8,128)} %bitcast.14, ...), custom_call_target="tpu_custom_call" | custom-call | tf_op jit(solution)/shard_map/pick/pallas_call | solution.py:308
  5.5 0.0 copy-start.2
  5.6 0.0 copy-start.3
  5.6 0.0 copy-start.1
  5.6 13.7 %all-to-all-start = ((bf16[32,8,768]{2,1,0:T(8,128)(2,1)}), bf16[32,8,768]{2,1,0:T(8,128)(2,1)S(1)}, u32[]{:S(2)}, u32[]{:S(2)}) async-start(bf16[32,8,768]{2,1,0:T(8,128)(2,1)} %get-tuple-element.16), calls=%async_computation | async-start | bytes 786432 | tf_op jit(solution)/shard_map/all_to_all | solution.py:327
  19.3 0.0 copy-start
  19.3 0.0 copy-done.2
  19.3 2.5 %collective-permute-start = (bf16[144,256]{1,0:T(8,128)(2,1)S(1)}, bf16[144,256]{1,0:T(8,128)(2,1)S(1)}, u32[]{:S(2)}, u32[]{:S(2)}) collective-permute-start(bf16[144,256]{1,0:T(8,128)(2,1)S(1)} %copy-done.2), channel_id=1, source_target_pairs={{0,1},{1,0},{2,3},{3,2},{4,5},{5,4},{6,7},{7,6},{8,9},{9,8},{10,11... | collective-permute-start | bytes 221192 | tf_op jit(solution)/shard_map/ppermute | solution.py:330
  21.8 0.9 %collective-permute-done.other_ref = bf16[144,256]{1,0:T(8,128)(2,1)S(1)} collective-permute-done((bf16[144,256]{1,0:T(8,128)(2,1)S(1)}, bf16[144,256]{1,0:T(8,128)(2,1)S(1)}, u32[]{:S(2)}, u32[]{:S(2)}) %collective-permute-start) | collective-permute-done | bytes 73760 | tf_op jit(solution)/shard_map/ppermute | solution.py:330
  22.7 0.0 copy-done.3
  22.7 0.4 lists.1
  23.1 1.8 %all-to-all-done = bf16[32,8,768]{2,1,0:T(8,128)(2,1)S(1)} async-done(((bf16[32,8,768]{2,1,0:T(8,128)(2,1)}), bf16[32,8,768]{2,1,0:T(8,128)(2,1)S(1)}, u32[]{:S(2)}, u32[]{:S(2)}) %all-to-all-start) | async-done | bytes 393248 | tf_op jit(solution)/shard_map/all_to_all | solution.py:327
  24.8 0.0 copy-done.1
  24.8 0.0 copy-done
  24.8 1.5 %layers.1 = (bf16[128,256]{1,0:T(8,128)(2,1)}, f32[32,9,2,128]{3,2,1,0:T(2,128)S(1)}) custom-call(s32[1]{0:T(128)} %bitcast.place_ref, bf16[256,768]{1,0:T(8,128)(2,1)S(1)} %bitcast.10, bf16[256,512]{1,0:T(8,128)(2,1)S(1)} %get-tuple-element.19.often_ref, f32[256,128]{1,0:T(8,128)S(1)} %get-tuple-element.20.counts_ref, ...), custom_call_target="tpu_custom_call" | custom-call | tf_op jit(solution)/shard_map/layers/pallas_call | solution.py:346
  26.4 11.3 %all_to_all.20 = f32[32,9,2,128]{3,2,1,0:T(2,128)S(1)} all-to-all(f32[32,9,2,128]{3,2,1,0:T(2,128)S(1)} %get-tuple-element.24), channel_id=1, replica_groups={{52,54,56,58,60,62,0,2,4,6,8,10,12,14,16,18,20,22,24,26,28,30,32,34,36,..., dimensions={0} | all-to-all | bytes 589824 | tf_op jit(solution)/shard_map/all_to_all | solution.py:361
  37.6 0.1 reduce_sum.18
  37.8 17.1 %all_to_all.21 = f32[8,9,2,128]{3,2,1,0:T(2,128)S(1)} all-to-all(f32[8,9,2,128]{3,2,1,0:T(2,128)S(1)} %broadcast_in_dim.26), channel_id=1, replica_groups={{256,0,64,448,128,384,192,320},{257,1,65,449,129,385,193,321},{258,2,66..., dimensions={0} | all-to-all | bytes 147456 | tf_op jit(solution)/shard_map/all_to_all | solution.py:365
  54.9 15.8 %all_to_all.22 = bf16[64,8,256]{2,1,0:T(8,128)(2,1)S(1)} all-to-all(bf16[64,8,256]{2,1,0:T(8,128)(2,1)S(1)} %repeat.1), channel_id=1, replica_groups={{53,52,55,54,57,56,59,58,61,60,63,62,1,0,3,2,5,4,7,6,9,8,11,10,13,12,15..., dimensions={0} | all-to-all | bytes 524288 | tf_op jit(solution)/shard_map/all_to_all | solution.py:375
  70.7 0.8 %widen.1 = (f32[256,256]{1,0:T(8,128)}, f32[256,256]{1,0:T(8,128)}, f32[1,256]{1,0:T(1,128)}) custom-call(bf16[32,2,8,256]{3,2,1,0:T(8,128)(2,1)S(1)} %bitcast.11, f32[18,128]{1,0:T(8,128)S(1)} %mul.14.part_ref.total_ref), custom_call_target="tpu_custom_call" | custom-call | tf_op jit(solution)/shard_map/widen/pallas_call | solution.py:378
  (5 shorter events, 0.1 us)
Async XLA Ops:
  5.5 13.8 %copy-start.2 = (bf16[144,256]{1,0:T(8,128)(2,1)S(1)}, bf16[144,256]{1,0:T(8,128)(2,1)}, u32[]{:S(2)}) copy-start(bf16[144,256]{1,0:T(8,128)(2,1)} %get-tuple-element.17.own_ref) | copy-start | bytes 221188
  5.6 17.1 %copy-start.3 = (f32[2,256]{1,0:T(2,128)S(1)}, f32[2,256]{1,0:T(2,128)}, u32[]{:S(2)}) copy-start(f32[2,256]{1,0:T(2,128)} %get-tuple-element.18.bias_ref) | copy-start | bytes 6148
  5.6 19.3 %copy-start.1 = (bf16[256,256]{1,0:T(8,128)(2,1)S(1)}, bf16[256,256]{1,0:T(8,128)(2,1)}, u32[]{:S(2)}) copy-start(bf16[256,256]{1,0:T(8,128)(2,1)} %neigh_ref.1) | copy-start | bytes 393220
  5.6 19.3 %all-to-all-start = ((bf16[32,8,768]{2,1,0:T(8,128)(2,1)}), bf16[32,8,768]{2,1,0:T(8,128)(2,1)S(1)}, u32[]{:S(2)}, u32[]{:S(2)}) async-start(bf16[32,8,768]{2,1,0:T(8,128)(2,1)} %get-tuple-element.16), calls=%async_computation | async-start | bytes 786432 | tf_op jit(solution)/shard_map/all_to_all | solution.py:327
  19.3 5.5 %copy-start = (bf16[256,256]{1,0:T(8,128)(2,1)S(1)}, bf16[256,256]{1,0:T(8,128)(2,1)}, u32[]{:S(2)}) copy-start(bf16[256,256]{1,0:T(8,128)(2,1)} %self_ref.1) | copy-start | bytes 393220
  19.3 3.4 %collective-permute-start = (bf16[144,256]{1,0:T(8,128)(2,1)S(1)}, bf16[144,256]{1,0:T(8,128)(2,1)S(1)}, u32[]{:S(2)}, u32[]{:S(2)}) collective-permute-start(bf16[144,256]{1,0:T(8,128)(2,1)S(1)} %copy-done.2), channel_id=1, source_target_pairs={{0,1},{1,0},{2,3},{3,2},{4,5},{5,4},{6,7},{7,6},{8,9},{9,8},{10,11... | collective-permute-start | bytes 221192 | tf_op jit(solution)/shard_map/ppermute | solution.py:330

commit v10 on v9

--- a/solution.py
+++ b/solution.py
@@ -174,10 +174,10 @@
 
 def gelu_parts(value):
     square = value * value
-    bent = jnp.tanh(INNER * (value + CUBIC * (value * square)))
-    half = 0.5 * (1.0 + bent)
-    slope = half + 0.5 * value * (1.0 - bent * bent) * (INNER * (1.0 + 3.0 * CUBIC * square))
-    return value * half, slope
+    half = 0.5 + 0.5 * jnp.tanh(value * (INNER + (INNER * CUBIC) * square))
+    gelu = value * half
+    slope = half + gelu * (1.0 - half) * (2.0 * INNER + (6.0 * INNER * CUBIC) * square)
+    return gelu, slope
 
 
 def lists_kernel(
@@ -297,7 +297,9 @@
     first_chip = chips // 2 + chips // 8
     first_part = group - chips + first_chip
     feat_order = both_cores(from_member(first_chip, chips))
-    part_order = from_member(first_part, group)
+    part_order = sorted(
+        range(group), key=lambda i: (i != first_part, i // chips, (i - first_chip) % chips)
+    )
     every_order = both_cores(part_order)
     apart_order = sorted(range(others), key=lambda i: (i != others // 2, min(i, others - i)))
     lists = (16, node_rows)

time: 71.9 us -> 72.2 us (level)
  no operation moved by 1% of the time
where the time goes in v10:
time: 72.2 us; the launch traced here: 71.8 us
  blocking collectives  44.5 us (62%)
  starting transfers between devices  16.2 us (22%)
  Pallas kernels  7.55 us (10%)
  waiting for transfers between devices  2.68 us (4%)
  between operations  0.74 us (1%)
    all_to_all x1, blocking collectives, local(): lax.all_to_all(spread, 'apart', 0, 0, tiled=True, axis_index_groups=[apar...  17 us
    all_to_all x1, blocking collectives, local(): lax.all_to_all(spread, ('pair', 'chip', 'core'), 0, 0, tiled=True, axis_i...  16.3 us
    all_to_all x1, starting transfers between devices, local(): lax.all_to_all(chunks, ('chip', 'core'), 0, 0, tiled=True, axis_index_gro...  13.7 us
    all_to_all x1, blocking collectives, local(): lax.all_to_all(parts, ('pair', 'chip'), 0, 0, tiled=True, axis_index_grou...  11.1 us
    pallas_call x1, Pallas kernels, local(): pl.pallas_call(functools.partial(pick_kernel, feat_order), out_shape=(jax...  4.9 us
    ppermute x1, starting transfers between devices, local(): other = lax.ppermute(send, 'core', [(0, 1), (1, 0)])  2.47 us
    all_to_all x1, waiting for transfers between devices, local(): lax.all_to_all(chunks, ('chip', 'core'), 0, 0, tiled=True, axis_index_gro...  1.79 us
    pallas_call x1, Pallas kernels, local(): pl.pallas_call(layers_kernel, out_shape=(jax.ShapeDtypeStruct((node_rows,...  1.47 us
  transfers between devices with their start and end apart: 2, of which 2 were waited for; matrix products, arithmetic and copies ran while one was open for 0% of the time, Pallas kernels for 0%

profile of v10, /device:TPU:1, one launch (start us, length us, event | category | flops | bytes accessed | tf_op | source)
XLA Modules:
  0.0 71.8 jit_solution(15459102441894131328)
XLA Ops:
  0.6 4.9 %pick.1 = (bf16[32,8,768]{2,1,0:T(8,128)(2,1)}, bf16[144,256]{1,0:T(8,128)(2,1)}, f32[2,256]{1,0:T(2,128)}) custom-call(bf16[4,4096]{1,0:T(4,128)(2,1)} %feats_hbm.1, s32[15,4096]{1,0:T(8,128)} %bitcast.12, s32[1,4096]{1,0:T(1,128)} %bitcast.13, bf16[4,256]{1,0:T(4,128)(2,1)} %self_hbm.1, bf16[4,256]{1,0:T(4,128)(2,1)} %neigh_hbm.1, s32[10,128]{1,0:T(8,128)} %bitcast.14, ...), custom_call_target="tpu_custom_call" | custom-call | tf_op jit(solution)/shard_map/pick/pallas_call | solution.py:310
  5.5 0.0 copy-start.2
  5.6 0.0 copy-start.3
  5.6 0.0 copy-start.1
  5.6 13.7 %all-to-all-start = ((bf16[32,8,768]{2,1,0:T(8,128)(2,1)}), bf16[32,8,768]{2,1,0:T(8,128)(2,1)S(1)}, u32[]{:S(2)}, u32[]{:S(2)}) async-start(bf16[32,8,768]{2,1,0:T(8,128)(2,1)} %get-tuple-element.16), calls=%async_computation | async-start | bytes 786432 | tf_op jit(solution)/shard_map/all_to_all | solution.py:329
  19.3 0.0 copy-start
  19.3 0.0 copy-done.2
  19.3 2.5 %collective-permute-start = (bf16[144,256]{1,0:T(8,128)(2,1)S(1)}, bf16[144,256]{1,0:T(8,128)(2,1)S(1)}, u32[]{:S(2)}, u32[]{:S(2)}) collective-permute-start(bf16[144,256]{1,0:T(8,128)(2,1)S(1)} %copy-done.2), channel_id=1, source_target_pairs={{0,1},{1,0},{2,3},{3,2},{4,5},{5,4},{6,7},{7,6},{8,9},{9,8},{10,11... | collective-permute-start | bytes 221192 | tf_op jit(solution)/shard_map/ppermute | solution.py:332
  21.8 0.9 %collective-permute-done.other_ref = bf16[144,256]{1,0:T(8,128)(2,1)S(1)} collective-permute-done((bf16[144,256]{1,0:T(8,128)(2,1)S(1)}, bf16[144,256]{1,0:T(8,128)(2,1)S(1)}, u32[]{:S(2)}, u32[]{:S(2)}) %collective-permute-start) | collective-permute-done | bytes 73760 | tf_op jit(solution)/shard_map/ppermute | solution.py:332
  22.7 0.0 copy-done.3
  22.7 0.4 lists.1
  23.1 1.8 %all-to-all-done = bf16[32,8,768]{2,1,0:T(8,128)(2,1)S(1)} async-done(((bf16[32,8,768]{2,1,0:T(8,128)(2,1)}), bf16[32,8,768]{2,1,0:T(8,128)(2,1)S(1)}, u32[]{:S(2)}, u32[]{:S(2)}) %all-to-all-start) | async-done | bytes 393248 | tf_op jit(solution)/shard_map/all_to_all | solution.py:329
  24.8 0.0 copy-done.1
  24.8 0.0 copy-done
  24.8 1.5 %layers.1 = (bf16[128,256]{1,0:T(8,128)(2,1)}, f32[32,9,2,128]{3,2,1,0:T(2,128)S(1)}) custom-call(s32[1]{0:T(128)} %bitcast.place_ref, bf16[256,768]{1,0:T(8,128)(2,1)S(1)} %bitcast.10, bf16[256,512]{1,0:T(8,128)(2,1)S(1)} %get-tuple-element.19.often_ref, f32[256,128]{1,0:T(8,128)S(1)} %get-tuple-element.20.counts_ref, ...), custom_call_target="tpu_custom_call" | custom-call | tf_op jit(solution)/shard_map/layers/pallas_call | solution.py:348
  26.3 11.1 %all_to_all.20 = f32[32,9,2,128]{3,2,1,0:T(2,128)S(1)} all-to-all(f32[32,9,2,128]{3,2,1,0:T(2,128)S(1)} %get-tuple-element.24), channel_id=1, replica_groups={{52,20,22,24,26,28,30,0,2,4,6,8,10,12,14,16,18,54,56,58,60,62,32,34,36,..., dimensions={0} | all-to-all | bytes 589824 | tf_op jit(solution)/shard_map/all_to_all | solution.py:363
  37.5 0.1 reduce_sum.18
  37.6 17.0 %all_to_all.21 = f32[8,9,2,128]{3,2,1,0:T(2,128)S(1)} all-to-all(f32[8,9,2,128]{3,2,1,0:T(2,128)S(1)} %broadcast_in_dim.26), channel_id=1, replica_groups={{256,0,64,448,128,384,192,320},{257,1,65,449,129,385,193,321},{258,2,66..., dimensions={0} | all-to-all | bytes 147456 | tf_op jit(solution)/shard_map/all_to_all | solution.py:367
  54.7 16.3 %all_to_all.22 = bf16[64,8,256]{2,1,0:T(8,128)(2,1)S(1)} all-to-all(bf16[64,8,256]{2,1,0:T(8,128)(2,1)S(1)} %repeat.1), channel_id=1, replica_groups={{53,52,21,20,23,22,25,24,27,26,29,28,31,30,1,0,3,2,5,4,7,6,9,8,11,10,13..., dimensions={0} | all-to-all | bytes 524288 | tf_op jit(solution)/shard_map/all_to_all | solution.py:377
  71.0 0.8 %widen.1 = (f32[256,256]{1,0:T(8,128)}, f32[256,256]{1,0:T(8,128)}, f32[1,256]{1,0:T(1,128)}) custom-call(bf16[32,2,8,256]{3,2,1,0:T(8,128)(2,1)S(1)} %bitcast.11, f32[18,128]{1,0:T(8,128)S(1)} %mul.14.part_ref.total_ref), custom_call_target="tpu_custom_call" | custom-call | tf_op jit(solution)/shard_map/widen/pallas_call | solution.py:380
  (5 shorter events, 0.1 us)
Async XLA Ops:
  5.5 13.8 %copy-start.2 = (bf16[144,256]{1,0:T(8,128)(2,1)S(1)}, bf16[144,256]{1,0:T(8,128)(2,1)}, u32[]{:S(2)}) copy-start(bf16[144,256]{1,0:T(8,128)(2,1)} %get-tuple-element.17.own_ref) | copy-start | bytes 221188
  5.6 17.1 %copy-start.3 = (f32[2,256]{1,0:T(2,128)S(1)}, f32[2,256]{1,0:T(2,128)}, u32[]{:S(2)}) copy-start(f32[2,256]{1,0:T(2,128)} %get-tuple-element.18.bias_ref) | copy-start | bytes 6148
  5.6 19.3 %copy-start.1 = (bf16[256,256]{1,0:T(8,128)(2,1)S(1)}, bf16[256,256]{1,0:T(8,128)(2,1)}, u32[]{:S(2)}) copy-start(bf16[256,256]{1,0:T(8,128)(2,1)} %neigh_ref.1) | copy-start | bytes 393220
  5.6 19.3 %all-to-all-start = ((bf16[32,8,768]{2,1,0:T(8,128)(2,1)}), bf16[32,8,768]{2,1,0:T(8,128)(2,1)S(1)}, u32[]{:S(2)}, u32[]{:S(2)}) async-start(bf16[32,8,768]{2,1,0:T(8,128)(2,1)} %get-tuple-element.16), calls=%async_computation | async-start | bytes 786432 | tf_op jit(solution)/shard_map/all_to_all | solution.py:329
  19.3 5.5 %copy-start = (bf16[256,256]{1,0:T(8,128)(2,1)S(1)}, bf16[256,256]{1,0:T(8,128)(2,1)}, u32[]{:S(2)}) copy-start(bf16[256,256]{1,0:T(8,128)(2,1)} %self_ref.1) | copy-start | bytes 393220
  19.3 3.4 %collective-permute-start = (bf16[144,256]{1,0:T(8,128)(2,1)S(1)}, bf16[144,256]{1,0:T(8,128)(2,1)S(1)}, u32[]{:S(2)}, u32[]{:S(2)}) collective-permute-start(bf16[144,256]{1,0:T(8,128)(2,1)S(1)} %copy-done.2), channel_id=1, source_target_pairs={{0,1},{1,0},{2,3},{3,2},{4,5},{5,4},{6,7},{7,6},{8,9},{9,8},{10,11... | collective-permute-start | bytes 221192 | tf_op jit(solution)/shard_map/ppermute | solution.py:332

commit v11 on v10

--- a/solution.py
+++ b/solution.py
@@ -12,6 +12,7 @@
 LANES = 128
 BY_MATMUL = 8
 REACH = 256
+PIECES = 4
 DEAD = -64
 INNER = math.sqrt(2.0 / math.pi)
 CUBIC = 0.044715
@@ -40,13 +41,16 @@
     feats_ref, ids_ref, counts_ref, self_ref, neigh_ref, ids_two_ref, counts_two_ref, cot_ref,
     bias_one_ref, bias_two_ref, wide, table, sums, lists, arrived,
 ):
+    half_nodes = ids_ref.shape[1] // 2
+    early, late = pl.ds(0, half_nodes), pl.ds(half_nodes, half_nodes)
     copies = [
         pltpu.make_async_copy(source, target, arrived.at[i])
         for i, (source, target) in enumerate(
             (
                 (feats_hbm, feats_ref),
-                (ids_hbm, ids_ref),
+                (ids_hbm.at[:, early], ids_ref.at[:, early]),
                 (counts_hbm, counts_ref),
+                (ids_hbm.at[:, late], ids_ref.at[:, late]),
                 (self_hbm, self_ref),
                 (neigh_hbm, neigh_ref),
                 (ids_two_hbm, ids_two_ref),
@@ -142,10 +146,12 @@
             )
         return carry
 
-    lax.fori_loop(0, blocks // 4, four_blocks, 0, unroll=True)
+    lax.fori_loop(0, blocks // 8, four_blocks, 0, unroll=True)
+    copies[3].wait()
+    lax.fori_loop(blocks // 8, blocks // 4, four_blocks, 0, unroll=True)
     sums[:, 0:LANES] = sums[:, blocks * LANES : (blocks + 1) * LANES]
     sums[:, (blocks + 1) * LANES :] = sums[:, LANES : 2 * LANES]
-    for copy in copies[3:]:
+    for copy in copies[4:]:
         copy.wait()
     node_rows = cot_ref.shape[0]
     fan_two = ids_two_ref.shape[0]
@@ -254,12 +260,22 @@
         out_ref[to] = part
 
 
-def widen_kernel(got_ref, total_ref, self_ref, neigh_ref, bias_ref):
+def widen_kernel(got_ref, total_ref, self_hbm, neigh_hbm, bias_ref, self_ref, neigh_ref, left):
     parts, _, rows, _ = got_ref.shape
-    for part in range(parts):
-        self_ref[part * rows : (part + 1) * rows, :] = got_ref[part, 1].astype(jnp.float32)
-        neigh_ref[part * rows : (part + 1) * rows, :] = got_ref[part, 0].astype(jnp.float32)
+    each = parts // PIECES
+    copies = []
+    for piece in range(PIECES):
+        span = pl.ds(piece * each * rows, each * rows)
+        for core, (kept, out) in enumerate(((self_ref, self_hbm), (neigh_ref, neigh_hbm))):
+            for part in range(piece * each, (piece + 1) * each):
+                kept[part * rows : (part + 1) * rows, :] = got_ref[part, 1 - core].astype(jnp.float32)
+            copies.append(
+                pltpu.make_async_copy(kept.at[span, :], out.at[span, :], left.at[2 * piece + core])
+            )
+            copies[-1].start()
     bias_ref[...] = jnp.concatenate([total_ref[16:17, :], total_ref[17:18, :]], axis=1)
+    for copy in copies:
+        copy.wait()
 
 
 def from_member(first, size):
@@ -297,9 +313,7 @@
     first_chip = chips // 2 + chips // 8
     first_part = group - chips + first_chip
     feat_order = both_cores(from_member(first_chip, chips))
-    part_order = sorted(
-        range(group), key=lambda i: (i != first_part, i // chips, (i - first_chip) % chips)
-    )
+    part_order = from_member(first_part, group)
     every_order = both_cores(part_order)
     apart_order = sorted(range(others), key=lambda i: (i != others // 2, min(i, others - i)))
     lists = (16, node_rows)
@@ -321,7 +335,7 @@
             pltpu.VMEM((4 * rows, batch_nodes), jnp.bfloat16),
             pltpu.VMEM((2 * rows, batch_nodes + 2 * node_rows), jnp.float32),
             pltpu.VMEM(lists, jnp.int32),
-            pltpu.SemaphoreType.DMA((len(loads),)),
+            pltpu.SemaphoreType.DMA((len(loads) + 1,)),
         ],
         compiler_params=pltpu.CompilerParams(vmem_limit_bytes=PICK_VMEM_BYTES),
         name="pick",
@@ -384,6 +398,12 @@
             jax.ShapeDtypeStruct((hid, hid), jnp.float32),
             jax.ShapeDtypeStruct((1, hid), jnp.float32),
         ),
+        out_specs=(pl.BlockSpec(memory_space=pltpu.HBM),) * 2 + (array,),
+        scratch_shapes=[
+            pltpu.VMEM((hid, hid), jnp.float32),
+            pltpu.VMEM((hid, hid), jnp.float32),
+            pltpu.SemaphoreType.DMA((2 * PIECES,)),
+        ],
         compiler_params=params,
         name="widen",
     )(whole.reshape(group, cores, hid // group, hid), total)

time: 72.2 us -> 72.5 us (level)
  no operation moved by 1% of the time
where the time goes in v11:
time: 72.5 us; the launch traced here: 72.1 us
  blocking collectives  44.2 us (61%)
  starting transfers between devices  16.2 us (22%)
  Pallas kernels  8.17 us (11%)
  waiting for transfers between devices  2.68 us (4%)
  between operations  0.74 us (1%)
    all_to_all x1, blocking collectives, local(): lax.all_to_all(spread, 'apart', 0, 0, tiled=True, axis_index_groups=[apar...  17.1 us
    all_to_all x1, blocking collectives, local(): lax.all_to_all(spread, ('pair', 'chip', 'core'), 0, 0, tiled=True, axis_i...  15.8 us
    all_to_all x1, starting transfers between devices, local(): lax.all_to_all(chunks, ('chip', 'core'), 0, 0, tiled=True, axis_index_gro...  13.7 us
    all_to_all x1, blocking collectives, local(): lax.all_to_all(parts, ('pair', 'chip'), 0, 0, tiled=True, axis_index_grou...  11.3 us
    pallas_call x1, Pallas kernels, local(): pl.pallas_call(functools.partial(pick_kernel, feat_order), out_shape=(jax...  4.92 us
    ppermute x1, starting transfers between devices, local(): other = lax.ppermute(send, 'core', [(0, 1), (1, 0)])  2.47 us
    all_to_all x1, waiting for transfers between devices, local(): lax.all_to_all(chunks, ('chip', 'core'), 0, 0, tiled=True, axis_index_gro...  1.79 us
    pallas_call x1, Pallas kernels, local(): pl.pallas_call(layers_kernel, out_shape=(jax.ShapeDtypeStruct((node_rows,...  1.47 us
  transfers between devices with their start and end apart: 2, of which 2 were waited for; matrix products, arithmetic and copies ran while one was open for 0% of the time, Pallas kernels for 0%

profile of v11, /device:TPU:1, one launch (start us, length us, event | category | flops | bytes accessed | tf_op | source)
XLA Modules:
  0.0 72.1 jit_solution(10326698935443427672)
XLA Ops:
  0.6 4.9 %pick.1 = (bf16[32,8,768]{2,1,0:T(8,128)(2,1)}, bf16[144,256]{1,0:T(8,128)(2,1)}, f32[2,256]{1,0:T(2,128)}) custom-call(bf16[4,4096]{1,0:T(4,128)(2,1)} %feats_hbm.1, s32[15,4096]{1,0:T(8,128)} %bitcast.12, s32[1,4096]{1,0:T(1,128)} %bitcast.13, bf16[4,256]{1,0:T(4,128)(2,1)} %self_hbm.1, bf16[4,256]{1,0:T(4,128)(2,1)} %neigh_hbm.1, s32[10,128]{1,0:T(8,128)} %bitcast.14, ...), custom_call_target="tpu_custom_call" | custom-call | tf_op jit(solution)/shard_map/pick/pallas_call | solution.py:324
  5.6 0.0 copy-start.2
  5.6 0.0 copy-start.3
  5.6 0.0 copy-start.1
  5.6 13.7 %all-to-all-start = ((bf16[32,8,768]{2,1,0:T(8,128)(2,1)}), bf16[32,8,768]{2,1,0:T(8,128)(2,1)S(1)}, u32[]{:S(2)}, u32[]{:S(2)}) async-start(bf16[32,8,768]{2,1,0:T(8,128)(2,1)} %get-tuple-element.16), calls=%async_computation | async-start | bytes 786432 | tf_op jit(solution)/shard_map/all_to_all | solution.py:343
  19.3 0.0 copy-start
  19.3 0.0 copy-done.2
  19.3 2.5 %collective-permute-start = (bf16[144,256]{1,0:T(8,128)(2,1)S(1)}, bf16[144,256]{1,0:T(8,128)(2,1)S(1)}, u32[]{:S(2)}, u32[]{:S(2)}) collective-permute-start(bf16[144,256]{1,0:T(8,128)(2,1)S(1)} %copy-done.2), channel_id=1, source_target_pairs={{0,1},{1,0},{2,3},{3,2},{4,5},{5,4},{6,7},{7,6},{8,9},{9,8},{10,11... | collective-permute-start | bytes 221192 | tf_op jit(solution)/shard_map/ppermute | solution.py:346
  21.8 0.9 %collective-permute-done.other_ref = bf16[144,256]{1,0:T(8,128)(2,1)S(1)} collective-permute-done((bf16[144,256]{1,0:T(8,128)(2,1)S(1)}, bf16[144,256]{1,0:T(8,128)(2,1)S(1)}, u32[]{:S(2)}, u32[]{:S(2)}) %collective-permute-start) | collective-permute-done | bytes 73760 | tf_op jit(solution)/shard_map/ppermute | solution.py:346
  22.7 0.0 copy-done.3
  22.7 0.4 lists.1
  23.1 1.8 %all-to-all-done = bf16[32,8,768]{2,1,0:T(8,128)(2,1)S(1)} async-done(((bf16[32,8,768]{2,1,0:T(8,128)(2,1)}), bf16[32,8,768]{2,1,0:T(8,128)(2,1)S(1)}, u32[]{:S(2)}, u32[]{:S(2)}) %all-to-all-start) | async-done | bytes 393248 | tf_op jit(solution)/shard_map/all_to_all | solution.py:343
  24.9 0.0 copy-done.1
  24.9 0.0 copy-done
  24.9 1.5 %layers.1 = (bf16[128,256]{1,0:T(8,128)(2,1)}, f32[32,9,2,128]{3,2,1,0:T(2,128)S(1)}) custom-call(s32[1]{0:T(128)} %bitcast.place_ref, bf16[256,768]{1,0:T(8,128)(2,1)S(1)} %bitcast.10, bf16[256,512]{1,0:T(8,128)(2,1)S(1)} %get-tuple-element.19.often_ref, f32[256,128]{1,0:T(8,128)S(1)} %get-tuple-element.20.counts_ref, ...), custom_call_target="tpu_custom_call" | custom-call | tf_op jit(solution)/shard_map/layers/pallas_call | solution.py:362
  26.3 11.3 %all_to_all.20 = f32[32,9,2,128]{3,2,1,0:T(2,128)S(1)} all-to-all(f32[32,9,2,128]{3,2,1,0:T(2,128)S(1)} %get-tuple-element.24), channel_id=1, replica_groups={{52,54,56,58,60,62,0,2,4,6,8,10,12,14,16,18,20,22,24,26,28,30,32,34,36,..., dimensions={0} | all-to-all | bytes 589824 | tf_op jit(solution)/shard_map/all_to_all | solution.py:377
  37.6 0.1 reduce_sum.18
  37.7 17.1 %all_to_all.21 = f32[8,9,2,128]{3,2,1,0:T(2,128)S(1)} all-to-all(f32[8,9,2,128]{3,2,1,0:T(2,128)S(1)} %broadcast_in_dim.26), channel_id=1, replica_groups={{256,0,64,448,128,384,192,320},{257,1,65,449,129,385,193,321},{258,2,66..., dimensions={0} | all-to-all | bytes 147456 | tf_op jit(solution)/shard_map/all_to_all | solution.py:381
  54.9 15.8 %all_to_all.22 = bf16[64,8,256]{2,1,0:T(8,128)(2,1)S(1)} all-to-all(bf16[64,8,256]{2,1,0:T(8,128)(2,1)S(1)} %repeat.1), channel_id=1, replica_groups={{53,52,55,54,57,56,59,58,61,60,63,62,1,0,3,2,5,4,7,6,9,8,11,10,13,12,15..., dimensions={0} | all-to-all | bytes 524288 | tf_op jit(solution)/shard_map/all_to_all | solution.py:391
  70.7 1.4 %widen.1 = (f32[256,256]{1,0:T(8,128)}, f32[256,256]{1,0:T(8,128)}, f32[1,256]{1,0:T(1,128)}) custom-call(bf16[32,2,8,256]{3,2,1,0:T(8,128)(2,1)S(1)} %bitcast.11, f32[18,128]{1,0:T(8,128)S(1)} %mul.14.part_ref.total_ref), custom_call_target="tpu_custom_call" | custom-call | tf_op jit(solution)/shard_map/widen/pallas_call | solution.py:394
  (5 shorter events, 0.1 us)
Async XLA Ops:
  5.6 13.8 %copy-start.2 = (bf16[144,256]{1,0:T(8,128)(2,1)S(1)}, bf16[144,256]{1,0:T(8,128)(2,1)}, u32[]{:S(2)}) copy-start(bf16[144,256]{1,0:T(8,128)(2,1)} %get-tuple-element.17.own_ref) | copy-start | bytes 221188
  5.6 17.1 %copy-start.3 = (f32[2,256]{1,0:T(2,128)S(1)}, f32[2,256]{1,0:T(2,128)}, u32[]{:S(2)}) copy-start(f32[2,256]{1,0:T(2,128)} %get-tuple-element.18.bias_ref) | copy-start | bytes 6148
  5.6 19.3 %copy-start.1 = (bf16[256,256]{1,0:T(8,128)(2,1)S(1)}, bf16[256,256]{1,0:T(8,128)(2,1)}, u32[]{:S(2)}) copy-start(bf16[256,256]{1,0:T(8,128)(2,1)} %neigh_ref.1) | copy-start | bytes 393220
  5.6 19.3 %all-to-all-start = ((bf16[32,8,768]{2,1,0:T(8,128)(2,1)}), bf16[32,8,768]{2,1,0:T(8,128)(2,1)S(1)}, u32[]{:S(2)}, u32[]{:S(2)}) async-start(bf16[32,8,768]{2,1,0:T(8,128)(2,1)} %get-tuple-element.16), calls=%async_computation | async-start | bytes 786432 | tf_op jit(solution)/shard_map/all_to_all | solution.py:343
  19.3 5.5 %copy-start = (bf16[256,256]{1,0:T(8,128)(2,1)S(1)}, bf16[256,256]{1,0:T(8,128)(2,1)}, u32[]{:S(2)}) copy-start(bf16[256,256]{1,0:T(8,128)(2,1)} %self_ref.1) | copy-start | bytes 393220
  19.3 3.4 %collective-permute-start = (bf16[144,256]{1,0:T(8,128)(2,1)S(1)}, bf16[144,256]{1,0:T(8,128)(2,1)S(1)}, u32[]{:S(2)}, u32[]{:S(2)}) collective-permute-start(bf16[144,256]{1,0:T(8,128)(2,1)S(1)} %copy-done.2), channel_id=1, source_target_pairs={{0,1},{1,0},{2,3},{3,2},{4,5},{5,4},{6,7},{7,6},{8,9},{9,8},{10,11... | collective-permute-start | bytes 221192 | tf_op jit(solution)/shard_map/ppermute | solution.py:346

commit v12 on v10

--- a/solution.py
+++ b/solution.py
@@ -297,9 +297,7 @@
     first_chip = chips // 2 + chips // 8
     first_part = group - chips + first_chip
     feat_order = both_cores(from_member(first_chip, chips))
-    part_order = sorted(
-        range(group), key=lambda i: (i != first_part, i // chips, (i - first_chip) % chips)
-    )
+    part_order = from_member(first_part, group)
     every_order = both_cores(part_order)
     apart_order = sorted(range(others), key=lambda i: (i != others // 2, min(i, others - i)))
     lists = (16, node_rows)

time: 72.2 us -> 71.9 us (level)
  no operation moved by 1% of the time
where the time goes in v12:
time: 71.9 us; the launch traced here: 71.5 us
  blocking collectives  44.2 us (61%)
  starting transfers between devices  16.2 us (23%)
  Pallas kernels  7.55 us (11%)
  waiting for transfers between devices  2.68 us (4%)
  between operations  0.74 us (1%)
    all_to_all x1, blocking collectives, local(): lax.all_to_all(spread, 'apart', 0, 0, tiled=True, axis_index_groups=[apar...  17.1 us
    all_to_all x1, blocking collectives, local(): lax.all_to_all(spread, ('pair', 'chip', 'core'), 0, 0, tiled=True, axis_i...  15.8 us
    all_to_all x1, starting transfers between devices, local(): lax.all_to_all(chunks, ('chip', 'core'), 0, 0, tiled=True, axis_index_gro...  13.7 us
    all_to_all x1, blocking collectives, local(): lax.all_to_all(parts, ('pair', 'chip'), 0, 0, tiled=True, axis_index_grou...  11.3 us
    pallas_call x1, Pallas kernels, local(): pl.pallas_call(functools.partial(pick_kernel, feat_order), out_shape=(jax...  4.9 us
    ppermute x1, starting transfers between devices, local(): other = lax.ppermute(send, 'core', [(0, 1), (1, 0)])  2.47 us
    all_to_all x1, waiting for transfers between devices, local(): lax.all_to_all(chunks, ('chip', 'core'), 0, 0, tiled=True, axis_index_gro...  1.79 us
    pallas_call x1, Pallas kernels, local(): pl.pallas_call(layers_kernel, out_shape=(jax.ShapeDtypeStruct((node_rows,...  1.47 us
  transfers between devices with their start and end apart: 2, of which 2 were waited for; matrix products, arithmetic and copies ran while one was open for 0% of the time, Pallas kernels for 0%

profile of v12, /device:TPU:1, one launch (start us, length us, event | category | flops | bytes accessed | tf_op | source)
XLA Modules:
  0.0 71.5 jit_solution(8780392475787271461)
XLA Ops:
  0.6 4.9 %pick.1 = (bf16[32,8,768]{2,1,0:T(8,128)(2,1)}, bf16[144,256]{1,0:T(8,128)(2,1)}, f32[2,256]{1,0:T(2,128)}) custom-call(bf16[4,4096]{1,0:T(4,128)(2,1)} %feats_hbm.1, s32[15,4096]{1,0:T(8,128)} %bitcast.12, s32[1,4096]{1,0:T(1,128)} %bitcast.13, bf16[4,256]{1,0:T(4,128)(2,1)} %self_hbm.1, bf16[4,256]{1,0:T(4,128)(2,1)} %neigh_hbm.1, s32[10,128]{1,0:T(8,128)} %bitcast.14, ...), custom_call_target="tpu_custom_call" | custom-call | tf_op jit(solution)/shard_map/pick/pallas_call | solution.py:308
  5.5 0.0 copy-start.2
  5.6 0.0 copy-start.3
  5.6 0.0 copy-start.1
  5.6 13.7 %all-to-all-start = ((bf16[32,8,768]{2,1,0:T(8,128)(2,1)}), bf16[32,8,768]{2,1,0:T(8,128)(2,1)S(1)}, u32[]{:S(2)}, u32[]{:S(2)}) async-start(bf16[32,8,768]{2,1,0:T(8,128)(2,1)} %get-tuple-element.16), calls=%async_computation | async-start | bytes 786432 | tf_op jit(solution)/shard_map/all_to_all | solution.py:327
  19.3 0.0 copy-start
  19.3 0.0 copy-done.2
  19.3 2.5 %collective-permute-start = (bf16[144,256]{1,0:T(8,128)(2,1)S(1)}, bf16[144,256]{1,0:T(8,128)(2,1)S(1)}, u32[]{:S(2)}, u32[]{:S(2)}) collective-permute-start(bf16[144,256]{1,0:T(8,128)(2,1)S(1)} %copy-done.2), channel_id=1, source_target_pairs={{0,1},{1,0},{2,3},{3,2},{4,5},{5,4},{6,7},{7,6},{8,9},{9,8},{10,11... | collective-permute-start | bytes 221192 | tf_op jit(solution)/shard_map/ppermute | solution.py:330
  21.8 0.9 %collective-permute-done.other_ref = bf16[144,256]{1,0:T(8,128)(2,1)S(1)} collective-permute-done((bf16[144,256]{1,0:T(8,128)(2,1)S(1)}, bf16[144,256]{1,0:T(8,128)(2,1)S(1)}, u32[]{:S(2)}, u32[]{:S(2)}) %collective-permute-start) | collective-permute-done | bytes 73760 | tf_op jit(solution)/shard_map/ppermute | solution.py:330
  22.7 0.0 copy-done.3
  22.7 0.4 lists.1
  23.1 1.8 %all-to-all-done = bf16[32,8,768]{2,1,0:T(8,128)(2,1)S(1)} async-done(((bf16[32,8,768]{2,1,0:T(8,128)(2,1)}), bf16[32,8,768]{2,1,0:T(8,128)(2,1)S(1)}, u32[]{:S(2)}, u32[]{:S(2)}) %all-to-all-start) | async-done | bytes 393248 | tf_op jit(solution)/shard_map/all_to_all | solution.py:327
  24.8 0.0 copy-done.1
  24.8 0.0 copy-done
  24.8 1.5 %layers.1 = (bf16[128,256]{1,0:T(8,128)(2,1)}, f32[32,9,2,128]{3,2,1,0:T(2,128)S(1)}) custom-call(s32[1]{0:T(128)} %bitcast.place_ref, bf16[256,768]{1,0:T(8,128)(2,1)S(1)} %bitcast.10, bf16[256,512]{1,0:T(8,128)(2,1)S(1)} %get-tuple-element.19.often_ref, f32[256,128]{1,0:T(8,128)S(1)} %get-tuple-element.20.counts_ref, ...), custom_call_target="tpu_custom_call" | custom-call | tf_op jit(solution)/shard_map/layers/pallas_call | solution.py:346
  26.3 11.3 %all_to_all.20 = f32[32,9,2,128]{3,2,1,0:T(2,128)S(1)} all-to-all(f32[32,9,2,128]{3,2,1,0:T(2,128)S(1)} %get-tuple-element.24), channel_id=1, replica_groups={{52,54,56,58,60,62,0,2,4,6,8,10,12,14,16,18,20,22,24,26,28,30,32,34,36,..., dimensions={0} | all-to-all | bytes 589824 | tf_op jit(solution)/shard_map/all_to_all | solution.py:361
  37.6 0.1 reduce_sum.18
  37.7 17.1 %all_to_all.21 = f32[8,9,2,128]{3,2,1,0:T(2,128)S(1)} all-to-all(f32[8,9,2,128]{3,2,1,0:T(2,128)S(1)} %broadcast_in_dim.26), channel_id=1, replica_groups={{256,0,64,448,128,384,192,320},{257,1,65,449,129,385,193,321},{258,2,66..., dimensions={0} | all-to-all | bytes 147456 | tf_op jit(solution)/shard_map/all_to_all | solution.py:365
  54.9 15.8 %all_to_all.22 = bf16[64,8,256]{2,1,0:T(8,128)(2,1)S(1)} all-to-all(bf16[64,8,256]{2,1,0:T(8,128)(2,1)S(1)} %repeat.1), channel_id=1, replica_groups={{53,52,55,54,57,56,59,58,61,60,63,62,1,0,3,2,5,4,7,6,9,8,11,10,13,12,15..., dimensions={0} | all-to-all | bytes 524288 | tf_op jit(solution)/shard_map/all_to_all | solution.py:375
  70.7 0.8 %widen.1 = (f32[256,256]{1,0:T(8,128)}, f32[256,256]{1,0:T(8,128)}, f32[1,256]{1,0:T(1,128)}) custom-call(bf16[32,2,8,256]{3,2,1,0:T(8,128)(2,1)S(1)} %bitcast.11, f32[18,128]{1,0:T(8,128)S(1)} %mul.14.part_ref.total_ref), custom_call_target="tpu_custom_call" | custom-call | tf_op jit(solution)/shard_map/widen/pallas_call | solution.py:378
  (5 shorter events, 0.1 us)
Async XLA Ops:
  5.5 13.8 %copy-start.2 = (bf16[144,256]{1,0:T(8,128)(2,1)S(1)}, bf16[144,256]{1,0:T(8,128)(2,1)}, u32[]{:S(2)}) copy-start(bf16[144,256]{1,0:T(8,128)(2,1)} %get-tuple-element.17.own_ref) | copy-start | bytes 221188
  5.6 17.1 %copy-start.3 = (f32[2,256]{1,0:T(2,128)S(1)}, f32[2,256]{1,0:T(2,128)}, u32[]{:S(2)}) copy-start(f32[2,256]{1,0:T(2,128)} %get-tuple-element.18.bias_ref) | copy-start | bytes 6148
  5.6 19.3 %copy-start.1 = (bf16[256,256]{1,0:T(8,128)(2,1)S(1)}, bf16[256,256]{1,0:T(8,128)(2,1)}, u32[]{:S(2)}) copy-start(bf16[256,256]{1,0:T(8,128)(2,1)} %neigh_ref.1) | copy-start | bytes 393220
  5.6 19.3 %all-to-all-start = ((bf16[32,8,768]{2,1,0:T(8,128)(2,1)}), bf16[32,8,768]{2,1,0:T(8,128)(2,1)S(1)}, u32[]{:S(2)}, u32[]{:S(2)}) async-start(bf16[32,8,768]{2,1,0:T(8,128)(2,1)} %get-tuple-element.16), calls=%async_computation | async-start | bytes 786432 | tf_op jit(solution)/shard_map/all_to_all | solution.py:327
  19.3 5.5 %copy-start = (bf16[256,256]{1,0:T(8,128)(2,1)S(1)}, bf16[256,256]{1,0:T(8,128)(2,1)}, u32[]{:S(2)}) copy-start(bf16[256,256]{1,0:T(8,128)(2,1)} %self_ref.1) | copy-start | bytes 393220
  19.3 3.4 %collective-permute-start = (bf16[144,256]{1,0:T(8,128)(2,1)S(1)}, bf16[144,256]{1,0:T(8,128)(2,1)S(1)}, u32[]{:S(2)}, u32[]{:S(2)}) collective-permute-start(bf16[144,256]{1,0:T(8,128)(2,1)S(1)} %copy-done.2), channel_id=1, source_target_pairs={{0,1},{1,0},{2,3},{3,2},{4,5},{5,4},{6,7},{7,6},{8,9},{9,8},{10,11... | collective-permute-start | bytes 221192 | tf_op jit(solution)/shard_map/ppermute | solution.py:330
